TPU v7x, 256 devices: a whole 4x4x8 slice. The times are simulated.
256 devices in a mesh: dp: 32 (over z, x), group: 8 (over y, core).
Axes of the slice: x: 4, y: 4, z: 8, core: 2. Of those that a mesh axis runs over, the one named last changes fastest.
Arguments:
- inputs: bfloat16 [65536, 8192], P(('dp', 'group')), may hold values from -24 to 24
- grad_values: bfloat16 [65536, 512], P(('dp', 'group')), may hold values from -6 to 6
- value_weight: bfloat16 [8192, 512], P('dp'), may hold values from -0.0625 to 0.0625
- counts: int32 [256], P(('dp', 'group')), may hold values from 32 to 256, as said below
- loss_mask: int32 [65536], P(('dp', 'group')), may hold values 0 or 1
Outputs:
- input_grad: bfloat16 [65536, 8192], P(('dp', 'group'))
- weight_grad: float32 [8192, 512], P('dp')
Inputs may be any that keep to these rules, and one draw needn't show every extreme that they name: `counts`: slots of a block at or past its count hold data that must not contribute; at least one block is full in every draw.
All inputs are finite; a program needn't handle non-finite values. No bound on the sum of `loss_mask` on one device may be relied on, other than what follows from the above.
Results may differ from a plain program's by a relative error of at most 0.0049.
Values may be sent and summed in bfloat16 or wider, within the bound.
No kernel may reach another device: no remote copies, remote signals or barrier semaphores. Data moves between devices by JAX's collectives and lax.ppermute only.
A program may use at most 128 MiB of HBM per device.

v0:
```python
import jax
import jax.numpy as jnp
from jax import lax
from jax.sharding import PartitionSpec as P


def contract_rows(left, right):
    return lax.dot_general(
        left, right, (((0,), (0,)), ((), ())), preferred_element_type=jnp.float32
    )


def local(inputs, grad_values, value_weight, counts, loss_mask):
    tok_rows = inputs.shape[0]
    devices_all = lax.axis_size("dp") * lax.axis_size("group")
    total = lax.psum(counts.astype(jnp.float32), ("dp", "group"))
    factor = devices_all * counts.astype(jnp.float32) / total
    positions = jnp.arange(tok_rows, dtype=jnp.int32)
    live_rows = ((positions < counts[0]) & (loss_mask > 0)).astype(jnp.float32)
    scaled = (grad_values.astype(jnp.float32) * (factor[0] * live_rows)[:, None]).astype(
        jnp.bfloat16
    )
    input_grad = lax.dot_general(
        scaled,
        lax.all_gather(value_weight, "dp", axis=0, tiled=True),
        (((1,), (1,)), ((), ())),
        preferred_element_type=jnp.float32,
    ).astype(jnp.bfloat16)
    share = lax.psum_scatter(contract_rows(inputs, scaled), "dp", scatter_dimension=0, tiled=True)
    summed = lax.psum(share, "group")
    return (input_grad, summed)


def solution(mesh):
    return jax.shard_map(
        local,
        mesh=mesh,
        in_specs=(
            P(("dp", "group"), None),
            P(("dp", "group"), None),
            P("dp", None),
            P(("dp", "group")),
            P(("dp", "group")),
        ),
        out_specs=(P(("dp", "group"), None), P("dp", None)),
        check_vma=False,
    )
```

profile of v0, /device:TPU:1, one launch (start us, length us, event | category | flops | bytes accessed | tf_op | source)
XLA Modules:
  0.0 512.4 jit_solution(8348257995674666139)
XLA Ops:
  7.2 0.0 reduce-scatter.2.cloned.1.call-start
  7.9 81.4 %psum.14 = f32[1]{0:T(128)} all-reduce(f32[1]{0:T(128)S(6)} %convert_element_type.15), channel_id=1, replica_groups=mesh['dp'=32,'group'=8] {'dp','group'}, use_global_device_ids=true, to_apply=%region_0.0 | all-reduce | flops 1 | bytes 8 | tf_op jit(solution)/shard_map/psum | solution.py:16
  89.9 0.7 and_select_fusion
  90.6 10.5 %convolution_bitcast_fusion = f32[8192,512]{0,1:T(8,128)} fusion(bf16[256,8192]{1,0:T(8,128)(2,1)} %param.5, bf16[256,512]{1,0:T(8,128)(2,1)} %param.6, f32[256]{0:T(256)S(1)} %and_select_fusion), kind=kOutput, calls=%fused_computation | convolution fusion | flops 2147876864 | bytes 21234688 | tf_op jit(solution)/shard_map/dot_general | solution.py:8
  101.1 0.0 copy-start
  101.1 0.0 reduce-scatter.2.cloned.1.call-update
  101.1 0.0 all-gather.2.cloned.1.call-start
  101.1 0.7 all-gather.2.cloned.1.call-update
  101.8 0.0 all-reduce.2.cloned.1.call-start
  101.9 235.2 %reduce-scatter.2.cloned.1.call-done = f32[256,512]{0,1:T(8,128)} async-done(((f32[8192,512]{0,1:T(8,128)}), f32[256,512]{0,1:T(8,128)}) %reduce-scatter.2.cloned.1.call-update) | async-done | bytes 524304 | tf_op jit(solution)/shard_map/reduce_scatter | solution.py:29
  337.1 0.0 all-reduce.2.cloned.1.call-update
  337.1 103.0 %all-gather.2.cloned.1.call-done = bf16[8192,512]{1,0:T(8,128)(2,1)} async-done(((bf16[256,512]{1,0:T(8,128)(2,1)}), bf16[8192,512]{1,0:T(8,128)(2,1)}) %all-gather.2.cloned.1.call-update) | async-done | bytes 8388624 | tf_op jit(solution)/shard_map/all_gather | solution.py:25
  440.1 0.0 copy-done
  440.1 7.8 %convolution_convert_fusion = bf16[256,8192]{1,0:T(8,128)(2,1)} fusion(bf16[8192,512]{1,0:T(8,128)(2,1)} %all-gather.2.cloned.1.call-done, bf16[256,512]{1,0:T(8,128)(2,1)S(1)} %copy-done, f32[256]{0:T(256)S(1)} %and_select_fusion), kind=kOutput, calls=%fused_computation.1 | convolution fusion | flops 2149974016 | bytes 12846080 | tf_op jit(solution)/shard_map/dot_general | solution.py:23
  447.9 55.9 %all-reduce.2.cloned.1.call-done = f32[256,512]{0,1:T(8,128)} async-done(((f32[256,512]{0,1:T(8,128)}), f32[256,512]{0,1:T(8,128)}) %all-reduce.2.cloned.1.call-update) | async-done | bytes 524304 | tf_op jit(solution)/shard_map/psum | solution.py:30
  503.8 2.0 copy.7
Async XLA Ops:
  7.2 329.9 %reduce-scatter.2.cloned.1.call-start = ((), (), s32[]{:S(2)}) async-start(), calls=%async_computation.2 | async-start | bytes 17301504 | tf_op jit(solution)/shard_map/reduce_scatter | solution.py:29
  101.1 339.1 %copy-start = (bf16[256,512]{1,0:T(8,128)(2,1)S(1)}, bf16[256,512]{1,0:T(8,128)(2,1)}, u32[]{:S(2)}) copy-start(bf16[256,512]{1,0:T(8,128)(2,1)} %param.6) | copy-start | bytes 786436
  101.1 339.1 %all-gather.2.cloned.1.call-start = ((), (), s32[]{:S(2)}) async-start(), calls=%async_computation.1 | async-start | bytes 8650752 | tf_op jit(solution)/shard_map/all_gather | solution.py:25
  101.8 402.0 %all-reduce.2.cloned.1.call-start = ((), (), s32[]{:S(2)}) async-start(), calls=%async_computation.3 | async-start | bytes 1048576 | tf_op jit(solution)/shard_map/psum | solution.py:30
Sparse Core Ops, SparseCore 0:
  101.2 235.8 reduce-scatter.1
  339.7 100.4 all-gather.1
  442.5 61.3 all-reduce.1
where the time goes:
time: 514 us; the launch traced here: 512 us
  waiting for transfers between devices  395 us (77%)
  blocking collectives  81.4 us (16%)
  matrix products  18.2 us (4%)
  between operations  15.1 us (3%)
    reduce_scatter x1, waiting for transfers between devices, local(): lax.psum_scatter(contract_rows(inputs, scaled), 'dp', scatter_dimension=0...  235 us
    all_gather x1, waiting for transfers between devices, local(): lax.all_gather(value_weight, 'dp', axis=0, tiled=True)  103 us
    psum x1, blocking collectives, local(): total = lax.psum(counts.astype(jnp.float32), ('dp', 'group'))  81.4 us
    psum x1, waiting for transfers between devices, local(): summed = lax.psum(share, 'group')  55.9 us
    dot_general x1, matrix products, contract_rows(): lax.dot_general(left, right, (((0,), (0,)), ((), ())), preferred_element_...  10.5 us
  transfers between devices with their start and end apart: 3, of which 3 were waited for; matrix products, arithmetic and copies ran while one was open for 2% of the time, Pallas kernels for 0%

commit v1 on v0

v1 whole, which is shorter than its diff:
```python
import functools

import jax
import jax.numpy as jnp
from jax import lax
from jax.experimental import pallas as pl
from jax.experimental.pallas import tpu as pltpu
from jax.sharding import PartitionSpec as P

NZ, NX, NY = 8, 4, 4
HALF_Z = NZ // 2
DEVICES = NZ * NX * NY * 2
F32, BF16 = jnp.float32, jnp.bfloat16
MIB = 1 << 20
ANYWHERE = pl.BlockSpec(memory_space=pl.ANY)
SMEM = pl.BlockSpec(memory_space=pltpu.SMEM)


def hop(array, move):
    pairs = []
    for z in range(NZ):
        for x in range(NX):
            for y in range(NY):
                for c in range(2):
                    tz, tx, ty, tc = move(z, x, y, c)
                    source = (z * NX + x) * NY * 2 + y * 2 + c
                    target = ((tz % NZ) * NX + tx % NX) * NY * 2 + (ty % NY) * 2 + tc
                    pairs.append((source, target))
    return lax.ppermute(array, ("dp", "group"), pairs)


def swap(array):
    return hop(array, lambda z, x, y, c: (z, x, y, 1 - c))


def nt_dot(left, right):
    return lax.dot_general(left, right, (((1,), (1,)), ((), ())), preferred_element_type=F32)


def nn_dot(left, right):
    return lax.dot_general(left, right, (((1,), (0,)), ((), ())), preferred_element_type=F32)


def params(mib):
    return pltpu.CompilerParams(vmem_limit_bytes=mib * MIB)


def whole(array):
    return pl.BlockSpec(array.shape, lambda *_: (0,) * array.ndim)


def like(array):
    return jax.ShapeDtypeStruct(array.shape, array.dtype)


def partial_kernel(place, own_n, other_n, own_t, other_t, own_x, other_x, total, s0, s1, s2a, s2b, s3, total_out, own_r, other_r):
    x, y, c = place[0], place[1], place[2]
    i = pl.program_id(0)

    @pl.when(i == 0)
    def _():
        for q in range(NY):
            quarter = lax.select(c == 0, lax.rem(y + q, NY), q)
            rows = pl.ds(pl.multiple_of(quarter * 128, 128), 128)
            own_r[q * 128 : (q + 1) * 128, :] = own_t[rows, :]
            other_r[q * 128 : (q + 1) * 128, :] = other_t[rows, :]

    def store(r, j, tile):
        if r == 2:
            @pl.when(j < 2)
            def _():
                s2a[j, i] = tile

            @pl.when(j >= 2)
            def _():
                s2b[j - 2, i] = tile
        else:
            (s0, s1, None, s3)[r][j, i] = tile

    def product(at):
        cols = pl.ds(pl.multiple_of(at * 256, 256), 256)
        return own_n[0:1, :] * nn_dot(own_r[...], own_x[:, cols]) + other_n[0:1, :] * nn_dot(
            other_r[...], other_x[:, cols]
        )

    @pl.when(c == 0)
    def _():
        for at in range(NX):
            tile = product(at).astype(BF16)
            for q in range(NY):
                store(q, at, tile[q * 128 : (q + 1) * 128])

    @pl.when(c == 1)
    def _():
        for r in range(NX):
            tile = product(lax.rem(x + r, NX)).astype(BF16)
            for q in range(NY):
                store(r, q, tile[q * 128 : (q + 1) * 128])


def partials(place, own_n, other_n, own_t, other_t, inputs, other_x, total):
    tokens = own_t.shape[1]
    jobs = (4, 4, 2, 2, 4)
    return pl.pallas_call(
        partial_kernel,
        grid_spec=pltpu.PrefetchScalarGridSpec(
            num_scalar_prefetch=1,
            grid=(HALF_Z,),
            in_specs=[
                whole(own_n),
                whole(other_n),
                whole(own_t),
                whole(other_t),
                pl.BlockSpec((tokens, NX * 256), lambda i, p: (0, p[2] * HALF_Z + i)),
                pl.BlockSpec((tokens, NX * 256), lambda i, p: (0, p[2] * HALF_Z + i)),
                ANYWHERE,
            ],
            out_specs=[pl.BlockSpec((j, HALF_Z, 128, 256), lambda i, p: (0, 0, 0, 0)) for j in jobs] + [ANYWHERE],
            scratch_shapes=[pltpu.VMEM((512, tokens), BF16)] * 2,
        ),
        out_shape=[jax.ShapeDtypeStruct((j, HALF_Z, 128, 256), BF16) for j in jobs] + [like(total)],
        input_output_aliases={7: 5},
        compiler_params=params(20),
        cost_estimate=pl.CostEstimate(flops=2 * 512 * 512 * 4096, bytes_accessed=9 << 20, transcendentals=0),
    )(place, own_n, other_n, own_t, other_t, inputs, other_x, total)


def relay_kernel(plus, minus, from_minus, from_plus, *rest):
    plus_out, minus_out = rest[len(rest) // 2 - 1 : len(rest) // 2 + 1]
    plus_out[...] = (plus[...].astype(F32) + from_minus[...].astype(F32)).astype(BF16)
    minus_out[...] = (minus[...].astype(F32) + from_plus[...].astype(F32)).astype(BF16)


def relay(plus, minus, from_minus, from_plus, *through):
    half = (2, 1, 128, 256)
    low = pl.BlockSpec(half, lambda i: (0, i, 0, 0))
    high = pl.BlockSpec(half, lambda i: (1, i, 0, 0))
    count = len(through)
    return pl.pallas_call(
        relay_kernel,
        grid=(HALF_Z,),
        in_specs=[low, high, low, low] + [ANYWHERE] * count,
        out_specs=[low, high] + [ANYWHERE] * count,
        out_shape=[like(a) for a in (plus, minus, *through)],
        input_output_aliases={0: 0, 1: 1} | {4 + k: 2 + k for k in range(count)},
        compiler_params=params(8),
        cost_estimate=pl.CostEstimate(flops=1 << 20, bytes_accessed=3 << 20, transcendentals=0),
    )(plus, minus, from_minus, from_plus, *through)


def first_sum_kernel(place, a, b, c, *rest):
    count = (len(rest) - 4) // 2
    own = lax.select(place[2] == 0, place[0], place[1])
    for r, u in enumerate(rest[count : count + 4]):
        j = lax.rem(own + r, 4)
        total = a[j, 0].astype(F32) + (b[j, 0].astype(F32) + c[j, 0].astype(F32))
        u[0] = total.astype(u.dtype)


def first_sum(place, parts, *through):
    part = pl.BlockSpec((4, 1, 128, 256), lambda i, p: (0, i, 0, 0))
    out = pl.BlockSpec((1, 128, 256), lambda i, p: (i, 0, 0))
    shape = (HALF_Z, 128, 256)
    count = len(through)
    return pl.pallas_call(
        first_sum_kernel,
        grid_spec=pltpu.PrefetchScalarGridSpec(
            num_scalar_prefetch=1,
            grid=(HALF_Z,),
            in_specs=[part] * 3 + [ANYWHERE] * count,
            out_specs=[out] * 4 + [ANYWHERE] * count,
        ),
        out_shape=[jax.ShapeDtypeStruct(shape, F32)]
        + [jax.ShapeDtypeStruct(shape, BF16)] * 3
        + [like(a) for a in through],
        input_output_aliases={4 + k: 4 + k for k in range(count)},
        compiler_params=params(8),
        cost_estimate=pl.CostEstimate(flops=1 << 20, bytes_accessed=4 << 20, transcendentals=0),
    )(place, *parts, *through)


def second_sum_kernel(place, a, b, c, d, *rest):
    count = (len(rest) - 4) // 2
    for k, v in enumerate(rest[count : count + 4]):
        j = lax.rem(place[3] + k, HALF_Z)
        total = (a[j] + b[j].astype(F32)) + (c[j].astype(F32) + d[j].astype(F32))
        v[...] = total.astype(v.dtype)


def second_sum(place, parts, *through):
    count = len(through)
    shape = jax.ShapeDtypeStruct((128, 256), BF16)
    return pl.pallas_call(
        second_sum_kernel,
        grid=(1,),
        in_specs=[SMEM] + [whole(a) for a in parts] + [ANYWHERE] * count,
        out_specs=[whole(shape)] * 4 + [ANYWHERE] * count,
        out_shape=[shape] * 4 + [like(a) for a in through],
        input_output_aliases={5 + k: 4 + k for k in range(count)},
        compiler_params=params(8),
        cost_estimate=pl.CostEstimate(flops=1 << 19, bytes_accessed=1 << 20, transcendentals=0),
    )(place, *parts, *through)


def third_sum_kernel(place, a, b, c, d, *rest):
    count = (len(rest) - 2) // 2
    for core, out in zip((place[2], 1 - place[2]), rest[count : count + 2]):
        cols = pl.ds(pl.multiple_of(core * 128, 128), 128)
        out[...] = (a[:, cols].astype(F32) + b[:, cols].astype(F32)) + (
            c[:, cols].astype(F32) + d[:, cols].astype(F32)
        )


def third_sum(place, parts, *through):
    count = len(through)
    shape = jax.ShapeDtypeStruct((128, 128), F32)
    return pl.pallas_call(
        third_sum_kernel,
        grid=(1,),
        in_specs=[SMEM] + [whole(a) for a in parts] + [ANYWHERE] * count,
        out_specs=[whole(shape)] * 2 + [ANYWHERE] * count,
        out_shape=[shape] * 2 + [like(a) for a in through],
        input_output_aliases={5 + k: 2 + k for k in range(count)},
        compiler_params=params(8),
        cost_estimate=pl.CostEstimate(flops=1 << 17, bytes_accessed=1 << 19, transcendentals=0),
    )(place, *parts, *through)


def finish_kernel(place, total, own, y1, y2, y3, other, through, out, through_out):
    y, c = place[1], place[2]
    inverse = DEVICES / total[0:1, 0:128]
    for r, mine in enumerate((own, y1, y2, y3)):
        feature = lax.rem(y + NY - r, NY)
        cols = pl.ds(pl.multiple_of(feature * 128, 128), 128)
        for core, tile in ((c, mine[...]), (1 - c, other[r])):
            rows = pl.ds(pl.multiple_of(core * 128, 128), 128)
            out[rows, cols] = (tile * inverse).T


def finish(place, total, own, gathered, other, through):
    parts = (own, *gathered, other)
    shape = jax.ShapeDtypeStruct((256, 512), F32)
    return pl.pallas_call(
        finish_kernel,
        grid=(1,),
        in_specs=[SMEM, whole(total)] + [whole(a) for a in parts] + [ANYWHERE],
        out_specs=[whole(shape), ANYWHERE],
        out_shape=[shape, like(through)],
        input_output_aliases={7: 1},
        compiler_params=params(8),
        cost_estimate=pl.CostEstimate(flops=1 << 18, bytes_accessed=1 << 20, transcendentals=0),
    )(place, total, *parts, through)


def assemble_kernel(place, own, near, near_other, far, *rest):
    x, c = place[0], place[2]
    step = 1 - 2 * c
    out = rest[2]
    out[x] = own[...]
    out[lax.rem(x - step + NX, NX)] = near[...]
    out[lax.rem(x + step + NX, NX)] = near_other[...]
    out[lax.rem(x + 2, NX)] = far[...]


def assemble(place, parts, total, dep):
    rows, width = parts[0].shape
    shape = jax.ShapeDtypeStruct((NX, rows, width), BF16)
    return pl.pallas_call(
        assemble_kernel,
        grid=(1,),
        in_specs=[SMEM] + [whole(a) for a in parts] + [ANYWHERE] * 2,
        out_specs=[whole(shape), ANYWHERE],
        out_shape=[shape, like(total)],
        input_output_aliases={5: 1},
        compiler_params=params(8),
        cost_estimate=pl.CostEstimate(flops=0, bytes_accessed=2 << 20, transcendentals=0),
    )(place, *parts, total, dep)


def project_kernel(pieces, cols, filled, total, grads, *refs):
    out = refs[-5]
    held, made, in_sems, out_sems = refs[-4:]
    span = held.shape[1]
    loads, stores = [], []
    for n, (k, start) in enumerate(pieces):
        loads.append(pltpu.make_async_copy(refs[k].at[pl.ds(start, span)], held.at[n], in_sems.at[n]))
        to = pl.ds(pl.multiple_of(cols[k] + start, 256), span)
        stores.append(pltpu.make_async_copy(made.at[n], out.at[:, to], out_sems.at[n]))
    for load in loads:
        load.start()
    scale = filled[0:1, :] * (DEVICES / total[0:1, :])
    for n, load in enumerate(loads):
        load.wait()
        for at in range(0, span, 256):
            made[n, :, at : at + 256] = (nt_dot(grads[...], held[n, at : at + 256, :]) * scale).astype(BF16)
        stores[n].start()
    for store in stores:
        store.wait()


def project(cols, filled, total, grads, chunks, out):
    tokens, width = grads.shape
    span = 512
    pieces = [(k, start) for k, chunk in enumerate(chunks) for start in range(0, chunk.shape[0], span)]
    count = len(pieces)
    operands = [cols, filled, total, grads, *chunks] + ([] if out is None else [out])
    return pl.pallas_call(
        functools.partial(project_kernel, pieces),
        grid=(1,),
        in_specs=[SMEM] + [whole(a) for a in operands[1:4]] + [ANYWHERE] * (len(operands) - 4),
        out_specs=ANYWHERE,
        out_shape=jax.ShapeDtypeStruct((tokens, NZ * NX * 256), BF16),
        scratch_shapes=[
            pltpu.VMEM((count, span, width), BF16),
            pltpu.VMEM((count, tokens, span), BF16),
            pltpu.SemaphoreType.DMA((count,)),
            pltpu.SemaphoreType.DMA((count,)),
        ],
        input_output_aliases={} if out is None else {len(operands) - 1: 0},
        compiler_params=params(24),
        cost_estimate=pl.CostEstimate(
            flops=2 * tokens * width * span * count, bytes_accessed=count * span * 1536, transcendentals=0
        ),
    )(*operands)


def local(inputs, grad_values, value_weight, counts, loss_mask):
    tok_rows = inputs.shape[0]
    dp, group = lax.axis_index("dp"), lax.axis_index("group")
    z, x, y, c = dp // NX, dp % NX, group // 2, group % 2
    place = jnp.stack([x, y, c, z]).astype(jnp.int32)
    dir_z = 1 - 2 * c

    other_x = swap(inputs)
    near = hop(value_weight, lambda z, x, y, c: (z, x + 1 - 2 * c, y, c))
    filled = jnp.full((8, 256), counts[0].astype(F32))
    other_filled = swap(filled)
    positions = jnp.arange(tok_rows, dtype=jnp.int32)
    live = (positions < counts[0]) & (loss_mask > 0)
    grads = jnp.where(live[:, None], grad_values, jnp.zeros_like(grad_values))
    own_t = grads.T
    other_t = swap(own_t)

    rows, width = value_weight.shape
    near_other = swap(near)
    far = hop(near, lambda z, x, y, c: (z, x + 1 - 2 * c, y, c))

    total = filled + hop(filled, lambda z, x, y, c: (z, x, y + 1, c))
    total = total + hop(total, lambda z, x, y, c: (z, x, y + 2, c))
    s0, s1, s2a, s2b, s3, total = partials(place, filled, other_filled, own_t, other_t, inputs, other_x, total)
    s_moves = lambda r: lambda z, x, y, c: (z, x, y + r, c) if c == 0 else (z, x + r, y, c)
    u_moves = lambda r: lambda z, x, y, c: (z, x + r, y, c) if c == 0 else (z, x, y + r, c)
    around = lambda z, x, y, c: (z + 1 - 2 * c, x, y, c)
    total = total + swap(total)
    chunk, total = assemble(place, (value_weight, near, near_other, far), total, s0)
    chunk = chunk.reshape(NX * rows, width)

    ring1 = hop(chunk, around)
    passed_plus, passed_minus = hop(s2a, s_moves(1)), hop(s2b, s_moves(-1))
    total = total + hop(total, lambda z, x, y, c: (z, x + 1, y, c))
    s1, s3, ring1, total = relay(s1, s3, passed_plus, passed_minus, ring1, total)

    ring2, ring1_other = hop(ring1, around), swap(ring1)
    first = (s0, hop(s1, s_moves(1)), hop(s3, s_moves(-1)))
    total = total + hop(total, lambda z, x, y, c: (z, x + 2, y, c))
    u0, u1, u2, u3, ring2, ring1_other, total = first_sum(place, first, ring2, ring1_other, total)

    ring3, ring2_other = hop(ring2, around), swap(ring2)
    second = [u0] + [hop(u, u_moves(r)) for r, u in ((1, u1), (2, u2), (3, u3))]
    total = total + hop(total, lambda z, x, y, c: (z + 1, x, y, c))
    *sends, ring3, ring2_other, total = second_sum(place, second, ring3, ring2_other, total)

    half = NX * rows // 2
    last = hop(lax.dynamic_slice(ring3, (c * half, 0), (half, width)), around)
    ring3_other = swap(ring3)
    third = [
        hop(sends[k], lambda z, x, y, c: (HALF_Z * c + (z + k) % HALF_Z, x, y, z // HALF_Z)) for k in range(4)
    ]
    total = total + hop(total, lambda z, x, y, c: (z + 2, x, y, c))
    kept, given, last, ring3_other, total = third_sum(place, third, last, ring3_other, total)

    def col_of(distance):
        return ((z + distance + NZ) % NZ) * (NX * rows)

    kept = kept + swap(given)
    total = total + hop(total, lambda z, x, y, c: (z + 4, x, y, c))
    last_other = swap(last)
    gathered = [hop(kept, lambda z, x, y, c: (z, x, y + r, c)) for r in range(1, 4)]
    cols = jnp.stack([col_of(0)] + [col_of(s * dir_z) for s in (-1, 1, -2, 2)]).astype(jnp.int32)
    input_grad = project(
        cols, filled, total, grads, (chunk, ring1, ring1_other, ring2, ring2_other), None
    )
    cols = jnp.stack(
        [col_of(-3 * dir_z), col_of(3 * dir_z), col_of(HALF_Z) + c * half, col_of(HALF_Z) + (1 - c) * half]
    ).astype(jnp.int32)
    input_grad = project(cols, filled, total, grads, (ring3, ring3_other, last, last_other), input_grad)
    other = swap(jnp.stack([kept, *gathered]))
    weight_grad, input_grad = finish(place, total, kept, gathered, other, input_grad)
    return (input_grad, weight_grad)


def solution(mesh):
    return jax.shard_map(
        local,
        mesh=mesh,
        in_specs=(
            P(("dp", "group"), None),
            P(("dp", "group"), None),
            P("dp", None),
            P(("dp", "group")),
            P(("dp", "group")),
        ),
        out_specs=(P(("dp", "group"), None), P("dp", None)),
        check_vma=False,
    )
```

time: 514 us -> 141 us (0.27)
  waiting for transfers between devices: 395 us -> 41.3 us
  blocking collectives: 81.4 us -> 0 us
  starting transfers between devices: 0.12 us -> 61.4 us
  Pallas kernels: 0 us -> 20.1 us
  matrix products: 18.2 us -> 0 us
  between operations: 15.1 us -> 1.68 us
  local copies, waits for them, and re-layouts: 2.04 us -> 10.7 us
    reduce_scatter x1 -> x0, waiting for transfers between devices: 235 us -> none  [local(): lax.psum_scatter(contract_rows(inputs, scaled), 'dp', scatter_dimension=0...]
    all_gather x1 -> x0, waiting for transfers between devices: 103 us -> none  [local(): lax.all_gather(value_weight, 'dp', axis=0, tiled=True)]
    psum x1 -> x0, blocking collectives: 81.4 us -> none  [local(): total = lax.psum(counts.astype(jnp.float32), ('dp', 'group'))]
    ppermute x0 -> x38, starting transfers between devices: none -> 61.4 us  [hop(): return lax.ppermute(array, ('dp', 'group'), pairs)]
    psum x1 -> x0, waiting for transfers between devices: 55.9 us -> none  [local(): summed = lax.psum(share, 'group')]
    ppermute x0 -> x38, waiting for transfers between devices: none -> 41.3 us  [hop(): return lax.ppermute(array, ('dp', 'group'), pairs)]
    pallas_call x0 -> x9, Pallas kernels: none -> 20.1 us  [the longest x2 8.68 us: project(): pl.pallas_call(functools.partial(project_kernel, pieces), grid=(1,), in_s...]
    dot_general x2 -> x0, matrix products: 18.2 us -> none  [the longest x1 10.5 us: contract_rows(): lax.dot_general(left, right, (((0,), (0,)), ((), ())), preferred_element_...]
  transfers between devices with their start and end apart: 3 -> 38, of which waited for: 3 -> 15; matrix products, arithmetic and copies ran while one was open for 2% -> 5% of each run, Pallas kernels for 0% -> 10%
where the time goes in v1:
time: 141 us
  starting transfers between devices  61.4 us (44%)
  waiting for transfers between devices  41.3 us (29%)
  Pallas kernels  20.1 us (14%)
  local copies, waits for them, and re-layouts  10.7 us (8%)
  other arithmetic  5.78 us (4%)
  between operations  1.68 us (1%)
    ppermute x38, starting transfers between devices, hop(): return lax.ppermute(array, ('dp', 'group'), pairs)  61.4 us
    ppermute x38, waiting for transfers between devices, hop(): return lax.ppermute(array, ('dp', 'group'), pairs)  41.3 us
    unnamed x30, local copies, waits for them, and re-layouts  9.76 us
    pallas_call x2, Pallas kernels, project(): pl.pallas_call(functools.partial(project_kernel, pieces), grid=(1,), in_s...  8.68 us
    pallas_call x1, Pallas kernels, partials(): pl.pallas_call(partial_kernel, grid_spec=pltpu.PrefetchScalarGridSpec(num...  5.12 us
  transfers between devices with their start and end apart: 38, of which 15 were waited for; matrix products, arithmetic and copies ran while one was open for 5% of the time, Pallas kernels for 10%

profile of v1, /device:TPU:1, one launch (start us, length us, event | category | flops | bytes accessed | tf_op | source)
XLA Modules:
  0.0 140.9 jit_solution(5906609328491336539)
XLA Ops:
  0.6 3.3 %collective-permute-start.2 = (bf16[256,8192]{1,0:T(8,128)(2,1)}, bf16[256,8192]{1,0:T(8,128)(2,1)}, u32[]{:S(2)}, u32[]{:S(2)}) collective-permute-start(bf16[256,8192]{1,0:T(8,128)(2,1)} %own_x.1), channel_id=1, source_target_pairs={{0,1},{1,0},{2,3},{3,2},{4,5},{5,4},{6,7},{7,6},{8,9},{9,8},{10,11... | collective-permute-start | bytes 12582920 | tf_op jit(solution)/shard_map/ppermute | solution.py:29
  4.8 0.7 compare_and_fusion
  5.5 1.1 fusion.1
  6.6 0.6 collective-permute-start.1
  7.1 1.9 %collective-permute-start.7 = (bf16[256,512]{1,0:T(8,128)(2,1)}, bf16[256,512]{1,0:T(8,128)(2,1)S(1)}, u32[]{:S(2)}, u32[]{:S(2)}) collective-permute-start(bf16[256,512]{1,0:T(8,128)(2,1)} %own.1), channel_id=1, source_target_pairs={{0,8},{1,25},{2,10},{3,27},{4,12},{5,29},{6,14},{7,31},{8,16},{9,1... | collective-permute-start | bytes 786440 | tf_op jit(solution)/shard_map/ppermute | solution.py:29
  9.1 2.7 %collective-permute-start.4 = (f32[8,256]{1,0:T(8,128)S(1)}, f32[8,256]{1,0:T(8,128)S(1)}, u32[]{:S(2)}, u32[]{:S(2)}) collective-permute-start(f32[8,256]{1,0:T(8,128)S(1)} %broadcast_add_fusion), channel_id=1, source_target_pairs={{0,4},{1,5},{2,6},{3,7},{4,0},{5,1},{6,2},{7,3},{8,12},{9,13},{10,... | collective-permute-start | bytes 24584 | tf_op jit(solution)/shard_map/ppermute | solution.py:29
  12.0 0.9 collective-permute-done.7.near
  12.9 2.9 %collective-permute-start.9 = (bf16[256,512]{1,0:T(8,128)(2,1)S(1)}, bf16[256,512]{1,0:T(8,128)(2,1)S(1)}, u32[]{:S(2)}, u32[]{:S(2)}) collective-permute-start(bf16[256,512]{1,0:T(8,128)(2,1)S(1)} %collective-permute-done.7.near), channel_id=1, source_target_pairs={{0,8},{1,25},{2,10},{3,27},{4,12},{5,29},{6,14},{7,31},{8,16},{9,1... | collective-permute-start | bytes 786440 | tf_op jit(solution)/shard_map/ppermute | solution.py:29
  15.9 2.2 %copy-done.6 = bf16[256,8192]{1,0:T(8,128)(2,1)S(1)} copy-done((bf16[256,8192]{1,0:T(8,128)(2,1)S(1)}, bf16[256,8192]{1,0:T(8,128)(2,1)}, u32[]{:S(2)}) %copy-start.6) | copy-done | bytes 4194328
  18.1 5.1 %shard_map.68 = (bf16[4,4,128,256]{3,2,1,0:T(8,128)(2,1)S(1)}, bf16[4,4,128,256]{3,2,1,0:T(8,128)(2,1)S(1)}, bf16[2,4,128,256]{3,2,1,0:T(8,128)(2,1)S(1)}, bf16[...) custom-call(s32[4]{0:T(128)S(1)} %pad_add_fusion.place, ...), custom_call_target="tpu_custom_call", output_to_operand_aliasing={{5}: (7, {})} | custom-call | flops 2147483648 | bytes 9437184 | tf_op jit(solution)/shard_map/pallas_call | solution.py:104
  23.2 0.5 collective-permute-start.10
  23.8 0.8 collective-permute-done.10
  24.6 0.6 shard_map.69
  25.2 5.7 %collective-permute-start.11 = (bf16[1024,512]{1,0:T(8,128)(2,1)S(1)}, bf16[1024,512]{1,0:T(8,128)(2,1)S(1)}, u32[]{:S(2)}, u32[]{:S(2)}) collective-permute-start(bf16[1024,512]{1,0:T(8,128)(2,1)S(1)} %bitcast.23), channel_id=1, source_target_pairs={{0,32},{1,225},{2,34},{3,227},{4,36},{5,229},{6,38},{7,231},{8,40}... | collective-permute-start | bytes 3145736 | tf_op jit(solution)/shard_map/ppermute | solution.py:29
  30.9 1.0 copy-done.7
  32.2 2.3 %collective-permute-start.6 = (bf16[2,4,128,256]{3,2,1,0:T(8,128)(2,1)S(1)}, bf16[2,4,128,256]{3,2,1,0:T(8,128)(2,1)S(1)}, u32[]{:S(2)}, u32[]{:S(2)}) collective-permute-start(bf16[2,4,128,256]{3,2,1,0:T(8,128)(2,1)S(1)} %get-tuple-element.39), channel_id=1, source_target_pairs={{0,6},{1,25},{2,0},{3,27},{4,2},{5,29},{6,4},{7,31},{8,14},{9,1},{... | collective-permute-start | bytes 1572872 | tf_op jit(solution)/shard_map/ppermute | solution.py:29
  34.5 7.0 %collective-permute-done.12 = f32[8,256]{1,0:T(8,128)S(1)} collective-permute-done((f32[8,256]{1,0:T(8,128)S(1)}, f32[8,256]{1,0:T(8,128)S(1)}, u32[]{:S(2)}, u32[]{:S(2)}) %collective-permute-start.12) | collective-permute-done | bytes 8224 | tf_op jit(solution)/shard_map/ppermute | solution.py:29
  41.6 1.0 collective-permute-done.11.rest_0_
  42.6 0.5 shard_map.70
  43.6 2.3 %collective-permute-start.14 = (bf16[4,4,128,256]{3,2,1,0:T(8,128)(2,1)S(1)}, bf16[4,4,128,256]{3,2,1,0:T(8,128)(2,1)S(1)}, u32[]{:S(2)}, u32[]{:S(2)}) collective-permute-start(bf16[4,4,128,256]{3,2,1,0:T(8,128)(2,1)S(1)} %get-tuple-element.44), channel_id=1, source_target_pairs={{0,6},{1,25},{2,0},{3,27},{4,2},{5,29},{6,4},{7,31},{8,14},{9,1},{... | collective-permute-start | bytes 3145736 | tf_op jit(solution)/shard_map/ppermute | solution.py:29
  45.9 2.2 %collective-permute-start.16 = (bf16[1024,512]{1,0:T(8,128)(2,1)S(1)}, bf16[1024,512]{1,0:T(8,128)(2,1)S(1)}, u32[]{:S(2)}, u32[]{:S(2)}) collective-permute-start(bf16[1024,512]{1,0:T(8,128)(2,1)S(1)} %get-tuple-element.45.refs_1_), channel_id=1, source_target_pairs={{0,1},{1,0},{2,3},{3,2},{4,5},{5,4},{6,7},{7,6},{8,9},{9,8},{10,11... | collective-permute-start | bytes 3145736 | tf_op jit(solution)/shard_map/ppermute | solution.py:29
  48.2 1.7 %collective-permute-start.15 = (bf16[1024,512]{1,0:T(8,128)(2,1)S(1)}, bf16[1024,512]{1,0:T(8,128)(2,1)S(1)}, u32[]{:S(2)}, u32[]{:S(2)}) collective-permute-start(bf16[1024,512]{1,0:T(8,128)(2,1)S(1)} %get-tuple-element.45.refs_1_), channel_id=1, source_target_pairs={{0,32},{1,225},{2,34},{3,227},{4,36},{5,229},{6,38},{7,231},{8,40}... | collective-permute-start | bytes 3145736 | tf_op jit(solution)/shard_map/ppermute | solution.py:29
  49.9 1.0 copy-done.2
  50.9 1.4 collective-permute-start.17
  52.3 6.3 %collective-permute-done.17 = f32[8,256]{1,0:T(8,128)S(1)} collective-permute-done((f32[8,256]{1,0:T(8,128)S(1)}, f32[8,256]{1,0:T(8,128)S(1)}, u32[]{:S(2)}, u32[]{:S(2)}) %collective-permute-start.17) | collective-permute-done | bytes 8224 | tf_op jit(solution)/shard_map/ppermute | solution.py:29
  58.6 3.5 %collective-permute-done.15.rest_0_ = bf16[1024,512]{1,0:T(8,128)(2,1)S(1)} collective-permute-done((bf16[1024,512]{1,0:T(8,128)(2,1)S(1)}, bf16[1024,512]{1,0:T(8,128)(2,1)S(1)}, u32[]{:S(2)}, u32[]{:S(2)}) %collective-permute-start.15) | collective-permute-done | bytes 1048608 | tf_op jit(solution)/shard_map/ppermute | solution.py:29
  62.1 1.2 shard_map.71
  63.4 2.2 %collective-permute-start.22 = (bf16[1024,512]{1,0:T(8,128)(2,1)S(1)}, bf16[1024,512]{1,0:T(8,128)(2,1)S(1)}, u32[]{:S(2)}, u32[]{:S(2)}) collective-permute-start(bf16[1024,512]{1,0:T(8,128)(2,1)S(1)} %get-tuple-element.51.refs_3_), channel_id=1, source_target_pairs={{0,1},{1,0},{2,3},{3,2},{4,5},{5,4},{6,7},{7,6},{8,9},{9,8},{10,11... | collective-permute-start | bytes 3145736 | tf_op jit(solution)/shard_map/ppermute | solution.py:29
  65.5 0.7 collective-permute-start.21
  66.2 0.8 collective-permute-start.23
  67.1 1.4 %collective-permute-start.19 = (bf16[4,128,256]{2,1,0:T(8,128)(2,1)S(1)}, bf16[4,128,256]{2,1,0:T(8,128)(2,1)S(1)}, u32[]{:S(2)}, u32[]{:S(2)}) collective-permute-start(bf16[4,128,256]{2,1,0:T(8,128)(2,1)S(1)} %get-tuple-element.49), channel_id=1, source_target_pairs={{0,16},{1,5},{2,18},{3,7},{4,20},{5,1},{6,22},{7,3},{8,24},{9,13},... | collective-permute-start | bytes 786440 | tf_op jit(solution)/shard_map/ppermute | solution.py:29
  68.5 1.8 %collective-permute-done.23 = f32[8,256]{1,0:T(8,128)S(1)} collective-permute-done((f32[8,256]{1,0:T(8,128)S(1)}, f32[8,256]{1,0:T(8,128)S(1)}, u32[]{:S(2)}, u32[]{:S(2)}) %collective-permute-start.23) | collective-permute-done | bytes 8224 | tf_op jit(solution)/shard_map/ppermute | solution.py:29
  70.3 1.0 collective-permute-start.20
  71.4 5.2 %collective-permute-done.18.b = bf16[4,128,256]{2,1,0:T(8,128)(2,1)S(1)} collective-permute-done((bf16[4,128,256]{2,1,0:T(8,128)(2,1)S(1)}, bf16[4,128,256]{2,1,0:T(8,128)(2,1)S(1)}, u32[]{:S(2)}, u32[]{:S(2)}) %collective-permute-start.18) | collective-permute-done | bytes 262176 | tf_op jit(solution)/shard_map/ppermute | solution.py:29
  76.6 0.6 collective-permute-done.20.d
  77.1 2.4 %collective-permute-done.21.rest_0_ = bf16[1024,512]{1,0:T(8,128)(2,1)S(1)} collective-permute-done((bf16[1024,512]{1,0:T(8,128)(2,1)S(1)}, bf16[1024,512]{1,0:T(8,128)(2,1)S(1)}, u32[]{:S(2)}, u32[]{:S(2)}) %collective-permute-start.21) | collective-permute-done | bytes 1048608 | tf_op jit(solution)/shard_map/ppermute | solution.py:29
  79.5 1.2 shard_map.72
  80.7 8.7 %collective-permute-start.29 = (bf16[1024,512]{1,0:T(8,128)(2,1)S(1)}, bf16[1024,512]{1,0:T(8,128)(2,1)S(1)}, u32[]{:S(2)}, u32[]{:S(2)}) collective-permute-start(bf16[1024,512]{1,0:T(8,128)(2,1)S(1)} %get-tuple-element.57.refs_0_), channel_id=1, source_target_pairs={{0,1},{1,0},{2,3},{3,2},{4,5},{5,4},{6,7},{7,6},{8,9},{9,8},{10,11... | collective-permute-start | bytes 3145736 | tf_op jit(solution)/shard_map/ppermute | solution.py:29
  89.6 6.0 %collective-permute-start.24 = (bf16[128,256]{1,0:T(8,128)(2,1)S(1)}, bf16[128,256]{1,0:T(8,128)(2,1)S(1)}, u32[]{:S(2)}, u32[]{:S(2)}) collective-permute-start(bf16[128,256]{1,0:T(8,128)(2,1)S(1)} %get-tuple-element.53), channel_id=1, source_target_pairs={{0,0},{1,128},{2,2},{3,130},{4,4},{5,132},{6,6},{7,134},{8,8},{9,1... | collective-permute-start | bytes 196616 | tf_op jit(solution)/shard_map/ppermute | solution.py:29
  95.7 2.0 %collective-permute-start.25 = (bf16[128,256]{1,0:T(8,128)(2,1)}, bf16[128,256]{1,0:T(8,128)(2,1)S(1)}, u32[]{:S(2)}, u32[]{:S(2)}) collective-permute-start(bf16[128,256]{1,0:T(8,128)(2,1)} %get-tuple-element.54), channel_id=1, source_target_pairs={{0,32},{1,160},{2,34},{3,162},{4,36},{5,164},{6,38},{7,166},{8,40}... | collective-permute-start | bytes 196616 | tf_op jit(solution)/shard_map/ppermute | solution.py:29
  97.7 2.7 %collective-permute-done.30 = f32[8,256]{1,0:T(8,128)S(1)} collective-permute-done((f32[8,256]{1,0:T(8,128)S(1)}, f32[8,256]{1,0:T(8,128)S(1)}, u32[]{:S(2)}, u32[]{:S(2)}) %collective-permute-start.30) | collective-permute-done | bytes 8224 | tf_op jit(solution)/shard_map/ppermute | solution.py:29
  100.4 3.5 %collective-permute-start.26 = (bf16[128,256]{1,0:T(8,128)(2,1)}, bf16[128,256]{1,0:T(8,128)(2,1)S(1)}, u32[]{:S(2)}, u32[]{:S(2)}) collective-permute-start(bf16[128,256]{1,0:T(8,128)(2,1)} %get-tuple-element.55), channel_id=1, source_target_pairs={{0,64},{1,192},{2,66},{3,194},{4,68},{5,196},{6,70},{7,198},{8,72}... | collective-permute-start | bytes 196616 | tf_op jit(solution)/shard_map/ppermute | solution.py:29
  103.9 2.7 %collective-permute-done.26.c = bf16[128,256]{1,0:T(8,128)(2,1)S(1)} collective-permute-done((bf16[128,256]{1,0:T(8,128)(2,1)}, bf16[128,256]{1,0:T(8,128)(2,1)S(1)}, u32[]{:S(2)}, u32[]{:S(2)}) %collective-permute-start.26) | collective-permute-done | bytes 65568 | tf_op jit(solution)/shard_map/ppermute | solution.py:29
  106.6 4.0 %collective-permute-done.27.d = bf16[128,256]{1,0:T(8,128)(2,1)S(1)} collective-permute-done((bf16[128,256]{1,0:T(8,128)(2,1)S(1)}, bf16[128,256]{1,0:T(8,128)(2,1)S(1)}, u32[]{:S(2)}, u32[]{:S(2)}) %collective-permute-start.27) | collective-permute-done | bytes 65568 | tf_op jit(solution)/shard_map/ppermute | solution.py:29
  110.6 0.6 shard_map.73
  111.8 0.7 collective-permute-done.32
  112.6 0.6 collective-permute-start.35
  113.2 1.6 %collective-permute-start.34 = (f32[128,128]{1,0:T(8,128)S(1)}, f32[128,128]{1,0:T(8,128)}, u32[]{:S(2)}, u32[]{:S(2)}) collective-permute-start(f32[128,128]{1,0:T(8,128)S(1)} %add.128.own), channel_id=1, source_target_pairs={{0,4},{1,5},{2,6},{3,7},{4,0},{5,1},{6,2},{7,3},{8,12},{9,13},{10,... | collective-permute-start | bytes 196616 | tf_op jit(solution)/shard_map/ppermute | solution.py:29
  115.1 1.1 broadcast_select_fusion.grads
  116.2 1.7 %collective-permute-start.31 = (f32[8,256]{1,0:T(8,128)S(1)}, f32[8,256]{1,0:T(8,128)}, u32[]{:S(2)}, u32[]{:S(2)}) collective-permute-start(f32[8,256]{1,0:T(8,128)S(1)} %get-tuple-element.59), channel_id=1, source_target_pairs={{0,128},{1,129},{2,130},{3,131},{4,132},{5,133},{6,134},{7,135},{8... | collective-permute-start | bytes 24584 | tf_op jit(solution)/shard_map/ppermute | solution.py:29
  117.9 1.6 %collective-permute-done.33.y1 = f32[128,128]{1,0:T(8,128)} collective-permute-done((f32[128,128]{1,0:T(8,128)S(1)}, f32[128,128]{1,0:T(8,128)}, u32[]{:S(2)}, u32[]{:S(2)}) %collective-permute-start.33) | collective-permute-done | bytes 65568 | tf_op jit(solution)/shard_map/ppermute | solution.py:29
  119.5 1.6 %pad_maximum_fusion = f32[4,128,128]{2,1,0:T(8,128)} fusion(f32[1,128,128]{2,1,0:T(8,128)S(1)} %bitcast.26, f32[1,128,128]{2,1,0:T(8,128)} %bitcast.9, f32[1,128,128]{2,1,0:T(8,128)} %bitcast.8, f32[1,128,128]{2,1,0:T(8,128)S(1)} %bitcast.25), kind=kLoop, calls=%fused_computation | loop fusion | flops 196608 | bytes 524288 | tf_op jit(solution)/shard_map/stack | solution.py:397
  121.1 1.5 %collective-permute-start.36 = (f32[4,128,128]{2,1,0:T(8,128)}, f32[4,128,128]{2,1,0:T(8,128)}, u32[]{:S(2)}, u32[]{:S(2)}) collective-permute-start(f32[4,128,128]{2,1,0:T(8,128)} %pad_maximum_fusion), channel_id=1, source_target_pairs={{0,1},{1,0},{2,3},{3,2},{4,5},{5,4},{6,7},{7,6},{8,9},{9,8},{10,11... | collective-permute-start | bytes 786440 | tf_op jit(solution)/shard_map/ppermute | solution.py:29
  122.6 0.6 pad_add_fusion.1.cols
  123.2 0.7 stack.83.cols
  123.9 0.7 add.127.total
  124.6 1.2 copy-done.1
  125.8 1.2 copy-done.3
  127.0 1.2 copy-done.5
  128.2 1.2 copy-done.8
  129.5 0.7 copy-done.13
  130.1 5.2 %shard_map.74.refs_4_ = bf16[256,8192]{1,0:T(8,128)(2,1)} custom-call(s32[5]{0:T(128)S(1)} %copy-done.13, f32[8,256]{1,0:T(8,128)S(1)} %broadcast_in_dim.15.own_n.filled, f32[8,256]{1,0:T(8,128)S(1)} %add.127.total, bf16[256,512]{1,0:T(8,128)(2,1)S(1)} %broadcast_select_fusion.grads, bf16[1024,512]{1,0:T(8,128)(2,1)S(1)} %bitcast.24, ...), custom_call_target="tpu_custom_call" | custom-call | flops 1342177280 | bytes 7864320 | tf_op jit(solution)/shard_map/pallas_call | solution.py:307
  135.3 3.5 %shard_map.75.through = bf16[256,8192]{1,0:T(8,128)(2,1)} custom-call(s32[4]{0:T(128)S(1)} %copy-done.12, f32[8,256]{1,0:T(8,128)S(1)} %broadcast_in_dim.15.own_n.filled, f32[8,256]{1,0:T(8,128)S(1)} %add.127.total, bf16[256,512]{1,0:T(8,128)(2,1)S(1)} %broadcast_select_fusion.grads, ...), custom_call_target="tpu_custom_call", output_to_operand_aliasing={{}: (8, {})} | custom-call | flops 805306368 | bytes 4718592 | tf_op jit(solution)/shard_map/pallas_call | solution.py:307
  138.9 2.1 %shard_map.76 = (f32[256,512]{1,0:T(8,128)}, bf16[256,8192]{1,0:T(8,128)(2,1)}) custom-call(s32[4]{0:T(128)S(1)} %copy-done.11, f32[8,256]{1,0:T(8,128)S(1)} %add.127.total, f32[128,128]{1,0:T(8,128)S(1)} %add.128.own, f32[128,128]{1,0:T(8,128)} %collective-permute-done.33.y1, ...), custom_call_target="tpu_custom_call", output_to_operand_aliasing={{1}: (7, {})} | custom-call | flops 262144 | bytes 1048576 | tf_op jit(solution)/shard_map/pallas_call | solution.py:243
  (71 shorter events, 2.7 us)
Async XLA Ops:
  0.6 15.3 %collective-permute-start.2 = (bf16[256,8192]{1,0:T(8,128)(2,1)}, bf16[256,8192]{1,0:T(8,128)(2,1)}, u32[]{:S(2)}, u32[]{:S(2)}) collective-permute-start(bf16[256,8192]{1,0:T(8,128)(2,1)} %own_x.1), channel_id=1, source_target_pairs={{0,1},{1,0},{2,3},{3,2},{4,5},{5,4},{6,7},{7,6},{8,9},{9,8},{10,11... | collective-permute-start | bytes 12582920 | tf_op jit(solution)/shard_map/ppermute | solution.py:29
  4.6 4.5 %collective-permute-start.3 = (f32[8,256]{1,0:T(8,128)S(1)}, f32[8,256]{1,0:T(8,128)S(1)}, u32[]{:S(2)}, u32[]{:S(2)}) collective-permute-start(f32[8,256]{1,0:T(8,128)S(1)} %broadcast_in_dim.15.own_n.filled), channel_id=1, source_target_pairs={{0,2},{1,3},{2,4},{3,5},{4,6},{5,7},{6,0},{7,1},{8,10},{9,11},{10,... | collective-permute-start | bytes 24584 | tf_op jit(solution)/shard_map/ppermute | solution.py:29
  4.7 11.2 %collective-permute-start = (f32[8,256]{1,0:T(8,128)S(1)}, f32[8,256]{1,0:T(8,128)S(1)}, u32[]{:S(2)}, u32[]{:S(2)}) collective-permute-start(f32[8,256]{1,0:T(8,128)S(1)} %broadcast_in_dim.15.own_n.filled), channel_id=1, source_target_pairs={{0,1},{1,0},{2,3},{3,2},{4,5},{5,4},{6,7},{7,6},{8,9},{9,8},{10,11... | collective-permute-start | bytes 24584 | tf_op jit(solution)/shard_map/ppermute | solution.py:29
  5.5 3.6 %copy-start.14 = (pred[256]{0:T(512)(128)(4,1)}, pred[256]{0:T(512)(128)(4,1)S(1)}, u32[]{:S(2)}) copy-start(pred[256]{0:T(512)(128)(4,1)S(1)} %compare_and_fusion) | copy-start | bytes 772
  6.6 9.2 %collective-permute-start.1 = (bf16[512,256]{0,1:T(8,128)(2,1)S(1)}, bf16[512,256]{0,1:T(8,128)(2,1)S(1)}, u32[]{:S(2)}, u32[]{:S(2)}) collective-permute-start(bf16[512,256]{0,1:T(8,128)(2,1)S(1)} %fusion.1), channel_id=1, source_target_pairs={{0,1},{1,0},{2,3},{3,2},{4,5},{5,4},{6,7},{7,6},{8,9},{9,8},{10,11... | collective-permute-start | bytes 786440 | tf_op jit(solution)/shard_map/ppermute | solution.py:29
  7.1 5.7 %collective-permute-start.7 = (bf16[256,512]{1,0:T(8,128)(2,1)}, bf16[256,512]{1,0:T(8,128)(2,1)S(1)}, u32[]{:S(2)}, u32[]{:S(2)}) collective-permute-start(bf16[256,512]{1,0:T(8,128)(2,1)} %own.1), channel_id=1, source_target_pairs={{0,8},{1,25},{2,10},{3,27},{4,12},{5,29},{6,14},{7,31},{8,16},{9,1... | collective-permute-start | bytes 786440 | tf_op jit(solution)/shard_map/ppermute | solution.py:29
  9.1 6.6 %collective-permute-start.4 = (f32[8,256]{1,0:T(8,128)S(1)}, f32[8,256]{1,0:T(8,128)S(1)}, u32[]{:S(2)}, u32[]{:S(2)}) collective-permute-start(f32[8,256]{1,0:T(8,128)S(1)} %broadcast_add_fusion), channel_id=1, source_target_pairs={{0,4},{1,5},{2,6},{3,7},{4,0},{5,1},{6,2},{7,3},{8,12},{9,13},{10,... | collective-permute-start | bytes 24584 | tf_op jit(solution)/shard_map/ppermute | solution.py:29
  11.9 98.7 %copy-start.10 = (s32[4]{0:T(128)}, s32[4]{0:T(128)S(1)}, u32[]{:S(2)}) copy-start(s32[4]{0:T(128)S(1)} %pad_add_fusion.place) | copy-start | bytes 52
  12.9 11.7 %collective-permute-start.9 = (bf16[256,512]{1,0:T(8,128)(2,1)S(1)}, bf16[256,512]{1,0:T(8,128)(2,1)S(1)}, u32[]{:S(2)}, u32[]{:S(2)}) collective-permute-start(bf16[256,512]{1,0:T(8,128)(2,1)S(1)} %collective-permute-done.7.near), channel_id=1, source_target_pairs={{0,8},{1,25},{2,10},{3,27},{4,12},{5,29},{6,14},{7,31},{8,16},{9,1... | collective-permute-start | bytes 786440 | tf_op jit(solution)/shard_map/ppermute | solution.py:29
  15.7 8.9 %collective-permute-start.8 = (bf16[256,512]{1,0:T(8,128)(2,1)S(1)}, bf16[256,512]{1,0:T(8,128)(2,1)S(1)}, u32[]{:S(2)}, u32[]{:S(2)}) collective-permute-start(bf16[256,512]{1,0:T(8,128)(2,1)S(1)} %collective-permute-done.7.near), channel_id=1, source_target_pairs={{0,1},{1,0},{2,3},{3,2},{4,5},{5,4},{6,7},{7,6},{8,9},{9,8},{10,11... | collective-permute-start | bytes 786440 | tf_op jit(solution)/shard_map/ppermute | solution.py:29
  15.7 8.9 %copy-start.9 = (bf16[256,512]{1,0:T(8,128)(2,1)S(1)}, bf16[256,512]{1,0:T(8,128)(2,1)}, u32[]{:S(2)}) copy-start(bf16[256,512]{1,0:T(8,128)(2,1)} %own.1) | copy-start | bytes 786436
  15.9 2.2 %copy-start.6 = (bf16[256,8192]{1,0:T(8,128)(2,1)S(1)}, bf16[256,8192]{1,0:T(8,128)(2,1)}, u32[]{:S(2)}) copy-start(bf16[256,8192]{1,0:T(8,128)(2,1)} %own_x.1) | copy-start | bytes 12582916
  23.2 1.4 collective-permute-start.10
  25.2 17.4 %collective-permute-start.11 = (bf16[1024,512]{1,0:T(8,128)(2,1)S(1)}, bf16[1024,512]{1,0:T(8,128)(2,1)S(1)}, u32[]{:S(2)}, u32[]{:S(2)}) collective-permute-start(bf16[1024,512]{1,0:T(8,128)(2,1)S(1)} %bitcast.23), channel_id=1, source_target_pairs={{0,32},{1,225},{2,34},{3,227},{4,36},{5,229},{6,38},{7,231},{8,40}... | collective-permute-start | bytes 3145736 | tf_op jit(solution)/shard_map/ppermute | solution.py:29
  30.9 1.0 copy-start.7
  31.9 9.7 %collective-permute-start.5 = (bf16[2,4,128,256]{3,2,1,0:T(8,128)(2,1)S(1)}, bf16[2,4,128,256]{3,2,1,0:T(8,128)(2,1)S(1)}, u32[]{:S(2)}, u32[]{:S(2)}) collective-permute-start(bf16[2,4,128,256]{3,2,1,0:T(8,128)(2,1)S(1)} %get-tuple-element.38), channel_id=1, source_target_pairs={{0,2},{1,9},{2,4},{3,11},{4,6},{5,13},{6,0},{7,15},{8,10},{9,17},{... | collective-permute-start | bytes 1572872 | tf_op jit(solution)/shard_map/ppermute | solution.py:29
  32.2 9.4 %collective-permute-start.6 = (bf16[2,4,128,256]{3,2,1,0:T(8,128)(2,1)S(1)}, bf16[2,4,128,256]{3,2,1,0:T(8,128)(2,1)S(1)}, u32[]{:S(2)}, u32[]{:S(2)}) collective-permute-start(bf16[2,4,128,256]{3,2,1,0:T(8,128)(2,1)S(1)} %get-tuple-element.39), channel_id=1, source_target_pairs={{0,6},{1,25},{2,0},{3,27},{4,2},{5,29},{6,4},{7,31},{8,14},{9,1},{... | collective-permute-start | bytes 1572872 | tf_op jit(solution)/shard_map/ppermute | solution.py:29
  34.5 7.0 %collective-permute-start.12 = (f32[8,256]{1,0:T(8,128)S(1)}, f32[8,256]{1,0:T(8,128)S(1)}, u32[]{:S(2)}, u32[]{:S(2)}) collective-permute-start(f32[8,256]{1,0:T(8,128)S(1)} %get-tuple-element.42), channel_id=1, source_target_pairs={{0,8},{1,9},{2,10},{3,11},{4,12},{5,13},{6,14},{7,15},{8,16},{9,17... | collective-permute-start | bytes 24584 | tf_op jit(solution)/shard_map/ppermute | solution.py:29
  43.2 15.4 %collective-permute-start.13 = (bf16[4,4,128,256]{3,2,1,0:T(8,128)(2,1)S(1)}, bf16[4,4,128,256]{3,2,1,0:T(8,128)(2,1)S(1)}, u32[]{:S(2)}, u32[]{:S(2)}) collective-permute-start(bf16[4,4,128,256]{3,2,1,0:T(8,128)(2,1)S(1)} %get-tuple-element.43), channel_id=1, source_target_pairs={{0,2},{1,9},{2,4},{3,11},{4,6},{5,13},{6,0},{7,15},{8,10},{9,17},{... | collective-permute-start | bytes 3145736 | tf_op jit(solution)/shard_map/ppermute | solution.py:29
  43.6 15.0 %collective-permute-start.14 = (bf16[4,4,128,256]{3,2,1,0:T(8,128)(2,1)S(1)}, bf16[4,4,128,256]{3,2,1,0:T(8,128)(2,1)S(1)}, u32[]{:S(2)}, u32[]{:S(2)}) collective-permute-start(bf16[4,4,128,256]{3,2,1,0:T(8,128)(2,1)S(1)} %get-tuple-element.44), channel_id=1, source_target_pairs={{0,6},{1,25},{2,0},{3,27},{4,2},{5,29},{6,4},{7,31},{8,14},{9,1},{... | collective-permute-start | bytes 3145736 | tf_op jit(solution)/shard_map/ppermute | solution.py:29
  45.9 12.7 %collective-permute-start.16 = (bf16[1024,512]{1,0:T(8,128)(2,1)S(1)}, bf16[1024,512]{1,0:T(8,128)(2,1)S(1)}, u32[]{:S(2)}, u32[]{:S(2)}) collective-permute-start(bf16[1024,512]{1,0:T(8,128)(2,1)S(1)} %get-tuple-element.45.refs_1_), channel_id=1, source_target_pairs={{0,1},{1,0},{2,3},{3,2},{4,5},{5,4},{6,7},{7,6},{8,9},{9,8},{10,11... | collective-permute-start | bytes 3145736 | tf_op jit(solution)/shard_map/ppermute | solution.py:29
  48.2 13.9 %collective-permute-start.15 = (bf16[1024,512]{1,0:T(8,128)(2,1)S(1)}, bf16[1024,512]{1,0:T(8,128)(2,1)S(1)}, u32[]{:S(2)}, u32[]{:S(2)}) collective-permute-start(bf16[1024,512]{1,0:T(8,128)(2,1)S(1)} %get-tuple-element.45.refs_1_), channel_id=1, source_target_pairs={{0,32},{1,225},{2,34},{3,227},{4,36},{5,229},{6,38},{7,231},{8,40}... | collective-permute-start | bytes 3145736 | tf_op jit(solution)/shard_map/ppermute | solution.py:29
  49.9 1.0 copy-start.2
  50.9 7.7 %collective-permute-start.17 = (f32[8,256]{1,0:T(8,128)S(1)}, f32[8,256]{1,0:T(8,128)S(1)}, u32[]{:S(2)}, u32[]{:S(2)}) collective-permute-start(f32[8,256]{1,0:T(8,128)S(1)} %get-tuple-element.46), channel_id=1, source_target_pairs={{0,16},{1,17},{2,18},{3,19},{4,20},{5,21},{6,22},{7,23},{8,24},{9,... | collective-permute-start | bytes 24584 | tf_op jit(solution)/shard_map/ppermute | solution.py:29
  63.4 17.4 %copy-start = (bf16[1024,512]{1,0:T(8,128)(2,1)}, bf16[1024,512]{1,0:T(8,128)(2,1)S(1)}, u32[]{:S(2)}) copy-start(bf16[1024,512]{1,0:T(8,128)(2,1)S(1)} %get-tuple-element.64.refs_2_) | copy-start | bytes 3145732
  63.4 17.4 %copy-start.4 = (bf16[1024,512]{1,0:T(8,128)(2,1)}, bf16[1024,512]{1,0:T(8,128)(2,1)S(1)}, u32[]{:S(2)}) copy-start(bf16[1024,512]{1,0:T(8,128)(2,1)S(1)} %get-tuple-element.51.refs_3_) | copy-start | bytes 3145732
  63.4 13.7 %collective-permute-start.22 = (bf16[1024,512]{1,0:T(8,128)(2,1)S(1)}, bf16[1024,512]{1,0:T(8,128)(2,1)S(1)}, u32[]{:S(2)}, u32[]{:S(2)}) collective-permute-start(bf16[1024,512]{1,0:T(8,128)(2,1)S(1)} %get-tuple-element.51.refs_3_), channel_id=1, source_target_pairs={{0,1},{1,0},{2,3},{3,2},{4,5},{5,4},{6,7},{7,6},{8,9},{9,8},{10,11... | collective-permute-start | bytes 3145736 | tf_op jit(solution)/shard_map/ppermute | solution.py:29
  65.5 13.9 %collective-permute-start.21 = (bf16[1024,512]{1,0:T(8,128)(2,1)S(1)}, bf16[1024,512]{1,0:T(8,128)(2,1)S(1)}, u32[]{:S(2)}, u32[]{:S(2)}) collective-permute-start(bf16[1024,512]{1,0:T(8,128)(2,1)S(1)} %get-tuple-element.51.refs_3_), channel_id=1, source_target_pairs={{0,32},{1,225},{2,34},{3,227},{4,36},{5,229},{6,38},{7,231},{8,40}... | collective-permute-start | bytes 3145736 | tf_op jit(solution)/shard_map/ppermute | solution.py:29
  66.2 4.1 %collective-permute-start.23 = (f32[8,256]{1,0:T(8,128)S(1)}, f32[8,256]{1,0:T(8,128)S(1)}, u32[]{:S(2)}, u32[]{:S(2)}) collective-permute-start(f32[8,256]{1,0:T(8,128)S(1)} %get-tuple-element.52), channel_id=1, source_target_pairs={{0,32},{1,33},{2,34},{3,35},{4,36},{5,37},{6,38},{7,39},{8,40},{9,... | collective-permute-start | bytes 24584 | tf_op jit(solution)/shard_map/ppermute | solution.py:29
  67.0 9.5 %collective-permute-start.18 = (bf16[4,128,256]{2,1,0:T(8,128)(2,1)S(1)}, bf16[4,128,256]{2,1,0:T(8,128)(2,1)S(1)}, u32[]{:S(2)}, u32[]{:S(2)}) collective-permute-start(bf16[4,128,256]{2,1,0:T(8,128)(2,1)S(1)} %get-tuple-element.48), channel_id=1, source_target_pairs={{0,8},{1,3},{2,10},{3,5},{4,12},{5,7},{6,14},{7,1},{8,16},{9,11},{... | collective-permute-start | bytes 786440 | tf_op jit(solution)/shard_map/ppermute | solution.py:29
  67.1 9.5 %collective-permute-start.19 = (bf16[4,128,256]{2,1,0:T(8,128)(2,1)S(1)}, bf16[4,128,256]{2,1,0:T(8,128)(2,1)S(1)}, u32[]{:S(2)}, u32[]{:S(2)}) collective-permute-start(bf16[4,128,256]{2,1,0:T(8,128)(2,1)S(1)} %get-tuple-element.49), channel_id=1, source_target_pairs={{0,16},{1,5},{2,18},{3,7},{4,20},{5,1},{6,22},{7,3},{8,24},{9,13},... | collective-permute-start | bytes 786440 | tf_op jit(solution)/shard_map/ppermute | solution.py:29
  70.3 6.8 %collective-permute-start.20 = (bf16[4,128,256]{2,1,0:T(8,128)(2,1)S(1)}, bf16[4,128,256]{2,1,0:T(8,128)(2,1)S(1)}, u32[]{:S(2)}, u32[]{:S(2)}) collective-permute-start(bf16[4,128,256]{2,1,0:T(8,128)(2,1)S(1)} %get-tuple-element.50), channel_id=1, source_target_pairs={{0,24},{1,7},{2,26},{3,1},{4,28},{5,3},{6,30},{7,5},{8,0},{9,15},{... | collective-permute-start | bytes 786440 | tf_op jit(solution)/shard_map/ppermute | solution.py:29
  80.7 29.9 %collective-permute-start.29 = (bf16[1024,512]{1,0:T(8,128)(2,1)S(1)}, bf16[1024,512]{1,0:T(8,128)(2,1)S(1)}, u32[]{:S(2)}, u32[]{:S(2)}) collective-permute-start(bf16[1024,512]{1,0:T(8,128)(2,1)S(1)} %get-tuple-element.57.refs_0_), channel_id=1, source_target_pairs={{0,1},{1,0},{2,3},{3,2},{4,5},{5,4},{6,7},{7,6},{8,9},{9,8},{10,11... | collective-permute-start | bytes 3145736 | tf_op jit(solution)/shard_map/ppermute | solution.py:29
  89.5 21.1 %collective-permute-start.28 = (bf16[512,512]{1,0:T(8,128)(2,1)S(1)}, bf16[512,512]{1,0:T(8,128)(2,1)}, u32[]{:S(2)}, u32[]{:S(2)}) collective-permute-start(bf16[512,512]{1,0:T(8,128)(2,1)S(1)} %constant_dynamic-slice_fusion), channel_id=1, source_target_pairs={{0,32},{1,225},{2,34},{3,227},{4,36},{5,229},{6,38},{7,231},{8,40}... | collective-permute-start | bytes 1572872 | tf_op jit(solution)/shard_map/ppermute | solution.py:29
  89.6 14.3 %collective-permute-start.24 = (bf16[128,256]{1,0:T(8,128)(2,1)S(1)}, bf16[128,256]{1,0:T(8,128)(2,1)S(1)}, u32[]{:S(2)}, u32[]{:S(2)}) collective-permute-start(bf16[128,256]{1,0:T(8,128)(2,1)S(1)} %get-tuple-element.53), channel_id=1, source_target_pairs={{0,0},{1,128},{2,2},{3,130},{4,4},{5,132},{6,6},{7,134},{8,8},{9,1... | collective-permute-start | bytes 196616 | tf_op jit(solution)/shard_map/ppermute | solution.py:29
  95.6 4.8 %collective-permute-start.30 = (f32[8,256]{1,0:T(8,128)S(1)}, f32[8,256]{1,0:T(8,128)S(1)}, u32[]{:S(2)}, u32[]{:S(2)}) collective-permute-start(f32[8,256]{1,0:T(8,128)S(1)} %get-tuple-element.58), channel_id=1, source_target_pairs={{0,64},{1,65},{2,66},{3,67},{4,68},{5,69},{6,70},{7,71},{8,72},{9,... | collective-permute-start | bytes 24584 | tf_op jit(solution)/shard_map/ppermute | solution.py:29
  95.7 8.2 %collective-permute-start.25 = (bf16[128,256]{1,0:T(8,128)(2,1)}, bf16[128,256]{1,0:T(8,128)(2,1)S(1)}, u32[]{:S(2)}, u32[]{:S(2)}) collective-permute-start(bf16[128,256]{1,0:T(8,128)(2,1)} %get-tuple-element.54), channel_id=1, source_target_pairs={{0,32},{1,160},{2,34},{3,162},{4,36},{5,164},{6,38},{7,166},{8,40}... | collective-permute-start | bytes 196616 | tf_op jit(solution)/shard_map/ppermute | solution.py:29
  100.4 6.2 %collective-permute-start.26 = (bf16[128,256]{1,0:T(8,128)(2,1)}, bf16[128,256]{1,0:T(8,128)(2,1)S(1)}, u32[]{:S(2)}, u32[]{:S(2)}) collective-permute-start(bf16[128,256]{1,0:T(8,128)(2,1)} %get-tuple-element.55), channel_id=1, source_target_pairs={{0,64},{1,192},{2,66},{3,194},{4,68},{5,196},{6,70},{7,198},{8,72}... | collective-permute-start | bytes 196616 | tf_op jit(solution)/shard_map/ppermute | solution.py:29
  103.9 6.7 %collective-permute-start.27 = (bf16[128,256]{1,0:T(8,128)(2,1)S(1)}, bf16[128,256]{1,0:T(8,128)(2,1)S(1)}, u32[]{:S(2)}, u32[]{:S(2)}) collective-permute-start(bf16[128,256]{1,0:T(8,128)(2,1)S(1)} %get-tuple-element.56), channel_id=1, source_target_pairs={{0,96},{1,224},{2,98},{3,226},{4,100},{5,228},{6,102},{7,230},{8,1... | collective-permute-start | bytes 196616 | tf_op jit(solution)/shard_map/ppermute | solution.py:29
  111.2 1.3 collective-permute-start.32
  111.3 24.0 %collective-permute-start.37 = (bf16[512,512]{1,0:T(8,128)(2,1)}, bf16[512,512]{1,0:T(8,128)(2,1)}, u32[]{:S(2)}, u32[]{:S(2)}) collective-permute-start(bf16[512,512]{1,0:T(8,128)(2,1)} %get-tuple-element.63.refs_2_), channel_id=1, source_target_pairs={{0,1},{1,0},{2,3},{3,2},{4,5},{5,4},{6,7},{7,6},{8,9},{9,8},{10,11... | collective-permute-start | bytes 1572872 | tf_op jit(solution)/shard_map/ppermute | solution.py:29
  112.6 5.3 %collective-permute-start.35 = (f32[128,128]{1,0:T(8,128)S(1)}, f32[128,128]{1,0:T(8,128)S(1)}, u32[]{:S(2)}, u32[]{:S(2)}) collective-permute-start(f32[128,128]{1,0:T(8,128)S(1)} %add.128.own), channel_id=1, source_target_pairs={{0,6},{1,7},{2,0},{3,1},{4,2},{5,3},{6,4},{7,5},{8,14},{9,15},{10,... | collective-permute-start | bytes 196616 | tf_op jit(solution)/shard_map/ppermute | solution.py:29
  113.2 4.7 %collective-permute-start.34 = (f32[128,128]{1,0:T(8,128)S(1)}, f32[128,128]{1,0:T(8,128)}, u32[]{:S(2)}, u32[]{:S(2)}) collective-permute-start(f32[128,128]{1,0:T(8,128)S(1)} %add.128.own), channel_id=1, source_target_pairs={{0,4},{1,5},{2,6},{3,7},{4,0},{5,1},{6,2},{7,3},{8,12},{9,13},{10,... | collective-permute-start | bytes 196616 | tf_op jit(solution)/shard_map/ppermute | solution.py:29
  114.7 4.8 %collective-permute-start.33 = (f32[128,128]{1,0:T(8,128)S(1)}, f32[128,128]{1,0:T(8,128)}, u32[]{:S(2)}, u32[]{:S(2)}) collective-permute-start(f32[128,128]{1,0:T(8,128)S(1)} %add.128.own), channel_id=1, source_target_pairs={{0,2},{1,3},{2,4},{3,5},{4,6},{5,7},{6,0},{7,1},{8,10},{9,11},{10,... | collective-permute-start | bytes 196616 | tf_op jit(solution)/shard_map/ppermute | solution.py:29
  116.2 7.6 %collective-permute-start.31 = (f32[8,256]{1,0:T(8,128)S(1)}, f32[8,256]{1,0:T(8,128)}, u32[]{:S(2)}, u32[]{:S(2)}) collective-permute-start(f32[8,256]{1,0:T(8,128)S(1)} %get-tuple-element.59), channel_id=1, source_target_pairs={{0,128},{1,129},{2,130},{3,131},{4,132},{5,133},{6,134},{7,135},{8... | collective-permute-start | bytes 24584 | tf_op jit(solution)/shard_map/ppermute | solution.py:29
  121.1 17.8 %collective-permute-start.36 = (f32[4,128,128]{2,1,0:T(8,128)}, f32[4,128,128]{2,1,0:T(8,128)}, u32[]{:S(2)}, u32[]{:S(2)}) collective-permute-start(f32[4,128,128]{2,1,0:T(8,128)} %pad_maximum_fusion), channel_id=1, source_target_pairs={{0,1},{1,0},{2,3},{3,2},{4,5},{5,4},{6,7},{7,6},{8,9},{9,8},{10,11... | collective-permute-start | bytes 786440 | tf_op jit(solution)/shard_map/ppermute | solution.py:29
  124.6 1.2 copy-start.1
  125.8 1.2 copy-start.3
  127.0 1.2 copy-start.5
  128.2 1.2 copy-start.8
  129.5 0.7 copy-start.13
  130.1 5.2 %copy-start.12 = (s32[4]{0:T(128)S(1)}, s32[4]{0:T(128)}, u32[]{:S(2)}) copy-start(s32[4]{0:T(128)} %pad_add_fusion.1.cols) | copy-start | bytes 52
  135.3 3.6 %copy-start.11 = (s32[4]{0:T(128)S(1)}, s32[4]{0:T(128)}, u32[]{:S(2)}) copy-start(s32[4]{0:T(128)} %copy-done.10) | copy-start | bytes 52

commit v2 on v0

v2 whole, which is shorter than its diff:
```python
import functools

import jax
import jax.numpy as jnp
from jax import lax
from jax.experimental import pallas as pl
from jax.experimental.pallas import tpu as pltpu
from jax.sharding import PartitionSpec as P

NZ, NX, NY = 8, 4, 4
HALF_Z = NZ // 2
DEVICES = NZ * NX * NY * 2
PAD = 16
F32, BF16 = jnp.float32, jnp.bfloat16
MIB = 1 << 20
ANYWHERE = pl.BlockSpec(memory_space=pl.ANY)
HBM = pl.BlockSpec(memory_space=pltpu.HBM)
SMEM = pl.BlockSpec(memory_space=pltpu.SMEM)


def hop(array, move):
    pairs = []
    for z in range(NZ):
        for x in range(NX):
            for y in range(NY):
                for c in range(2):
                    tz, tx, ty, tc = move(z, x, y, c)
                    source = (z * NX + x) * NY * 2 + y * 2 + c
                    target = ((tz % NZ) * NX + tx % NX) * NY * 2 + (ty % NY) * 2 + tc
                    pairs.append((source, target))
    return lax.ppermute(array, ("dp", "group"), pairs)


def swap(array):
    return hop(array, lambda z, x, y, c: (z, x, y, 1 - c))


def nt_dot(left, right):
    return lax.dot_general(left, right, (((1,), (1,)), ((), ())), preferred_element_type=F32)


def nn_dot(left, right):
    return lax.dot_general(left, right, (((1,), (0,)), ((), ())), preferred_element_type=F32)


def params(mib):
    return pltpu.CompilerParams(vmem_limit_bytes=mib * MIB)


def whole(array):
    return pl.BlockSpec(array.shape, lambda *_: (0,) * array.ndim)


def like(array):
    return jax.ShapeDtypeStruct(array.shape, array.dtype)


def turn(place, gradient, out):
    for q in range(NY):
        quarter = lax.select(place[2] == 0, lax.rem(place[1] + q, NY), q)
        out[q * 128 : (q + 1) * 128, :] = gradient[pl.ds(pl.multiple_of(quarter * 128, 128), 128), :]


def step_loads(place, source, held, sems):
    i = pl.program_id(0)
    span = NX * 256

    def load(k):
        cols = pl.ds(pl.multiple_of((place[2] * HALF_Z + k) * span, span), span)
        return pltpu.make_async_copy(source.at[:, cols], held.at[k], sems.at[k])

    @pl.when(i == 0)
    def _():
        load(0).start()
        load(1).start()

    @pl.when((i > 0) & (i < HALF_Z - 1))
    def _():
        load(i + 1).start()

    load(i).wait()


def own_kernel(place, number, gradient, source, grads, added, grads_out, turned, held, sems):
    i = pl.program_id(0)

    @pl.when(i == 0)
    def _():
        turn(place, gradient, turned)

    step_loads(place, source, held, sems)
    for at in range(NX):
        added[i, at] = number[0:1, :] * nn_dot(turned[...], held[i, :, at * 256 : (at + 1) * 256])


def other_kernel(place, number, gradient, source, added, s0, plus, minus, s1, s3, turned, held, sems):
    x, c = place[0], place[2]
    i = pl.program_id(0)

    @pl.when(i == 0)
    def _():
        turn(place, gradient, turned)

    step_loads(place, source, held, sems)

    def store(r, j, tile):
        if r == 0:
            s0[j, i] = tile
            return

        @pl.when(j < 2)
        def _():
            if r == 1:
                s1[j, i] = tile
            elif r == 2:
                plus[j, i] = tile
            else:
                minus[2 + j, i] = tile

        @pl.when(j >= 2)
        def _():
            if r == 1:
                plus[j, i] = tile
            elif r == 2:
                minus[j - 2, i] = tile
            else:
                s3[j - 2, i] = tile

    def product(at):
        cols = pl.ds(pl.multiple_of(at * 256, 256), 256)
        return (added[i, at] + number[0:1, :] * nn_dot(turned[...], held[i, :, cols])).astype(BF16)

    @pl.when(c == 0)
    def _():
        for at in range(NX):
            tile = product(at)
            for q in range(NY):
                store(q, at, tile[q * 128 : (q + 1) * 128])

    @pl.when(c == 1)
    def _():
        for r in range(NX):
            tile = product(lax.rem(x + r, NX))
            for q in range(NY):
                store(r, q, tile[q * 128 : (q + 1) * 128])


def partials_scratch(tokens):
    return [
        pltpu.VMEM((512, tokens), BF16),
        pltpu.VMEM((HALF_Z, tokens, NX * 256), BF16),
        pltpu.SemaphoreType.DMA((HALF_Z,)),
    ]


def own_partials(place, number, gradient, inputs, grads):
    tokens = gradient.shape[1]
    shape = jax.ShapeDtypeStruct((HALF_Z, NX, 512, 256), F32)
    vmem = pl.BlockSpec(memory_space=pltpu.VMEM)
    return pl.pallas_call(
        own_kernel,
        grid=(HALF_Z,),
        in_specs=[SMEM, vmem, vmem, HBM, ANYWHERE],
        out_specs=[vmem, ANYWHERE],
        out_shape=[shape, like(grads)],
        scratch_shapes=partials_scratch(tokens),
        input_output_aliases={4: 1},
        compiler_params=params(16),
        cost_estimate=pl.CostEstimate(flops=512 * 512 * 4096, bytes_accessed=4 << 20, transcendentals=0),
    )(place, number, gradient, inputs, grads)


def partials(place, number, gradient, inputs, added):
    tokens = gradient.shape[1]
    jobs = (4, 4, 4, 2, 2)
    vmem = pl.BlockSpec(memory_space=pltpu.VMEM)
    return pl.pallas_call(
        other_kernel,
        grid=(HALF_Z,),
        in_specs=[SMEM, vmem, vmem, HBM, vmem],
        out_specs=[vmem] * 5,
        out_shape=[jax.ShapeDtypeStruct((j, HALF_Z, 128, 256), BF16) for j in jobs],
        scratch_shapes=partials_scratch(tokens),
        compiler_params=params(16),
        cost_estimate=pl.CostEstimate(flops=512 * 512 * 4096, bytes_accessed=8 << 20, transcendentals=0),
    )(place, number, gradient, inputs, added)


def relay_kernel(s1, s3, from_minus, from_plus, *rest):
    s1_out, s3_out = rest[len(rest) // 2 - 1 : len(rest) // 2 + 1]
    s1_out[...] = (s1[...].astype(F32) + from_minus[...].astype(F32)).astype(BF16)
    s3_out[...] = (s3[...].astype(F32) + from_plus[...].astype(F32)).astype(BF16)


def relay(s1, s3, from_minus, from_plus, *through):
    low = pl.BlockSpec((2, 1, 128, 256), lambda i: (0, i, 0, 0))
    count = len(through)
    return pl.pallas_call(
        relay_kernel,
        grid=(HALF_Z,),
        in_specs=[low] * 4 + [ANYWHERE] * count,
        out_specs=[low] * 2 + [ANYWHERE] * count,
        out_shape=[like(a) for a in (s1, s3, *through)],
        input_output_aliases={0: 0, 1: 1} | {4 + k: 2 + k for k in range(count)},
        compiler_params=params(8),
        cost_estimate=pl.CostEstimate(flops=1 << 20, bytes_accessed=3 << 20, transcendentals=0),
    )(s1, s3, from_minus, from_plus, *through)


def first_sum_kernel(place, s0, from_minus, from_plus, late_minus, late_plus, *rest):
    count = (len(rest) - 5) // 2
    added = rest[-1]
    for k in range(2):
        added[k] = s0[k, 0].astype(F32) + (late_minus[k, 0].astype(F32) + from_plus[k, 0].astype(F32))
        added[2 + k] = s0[2 + k, 0].astype(F32) + (late_plus[k, 0].astype(F32) + from_minus[k, 0].astype(F32))
    own = lax.select(place[2] == 0, place[0], place[1])
    for r, u in enumerate(rest[count : count + 4]):
        u[0] = added[lax.rem(own + r, 4)].astype(u.dtype)


def first_sum(place, parts, *through):
    four = pl.BlockSpec((4, 1, 128, 256), lambda i, p: (0, i, 0, 0))
    low = pl.BlockSpec((2, 1, 128, 256), lambda i, p: (0, i, 0, 0))
    high = pl.BlockSpec((2, 1, 128, 256), lambda i, p: (1, i, 0, 0))
    out = pl.BlockSpec((1, 128, 256), lambda i, p: (i, 0, 0))
    shape = (HALF_Z, 128, 256)
    count = len(through)
    return pl.pallas_call(
        first_sum_kernel,
        grid_spec=pltpu.PrefetchScalarGridSpec(
            num_scalar_prefetch=1,
            grid=(HALF_Z,),
            in_specs=[four, high, high, low, low] + [ANYWHERE] * count,
            out_specs=[out] * 4 + [ANYWHERE] * count,
            scratch_shapes=[pltpu.VMEM((4, 128, 256), F32)],
        ),
        out_shape=[jax.ShapeDtypeStruct(shape, F32)]
        + [jax.ShapeDtypeStruct(shape, BF16)] * 3
        + [like(a) for a in through],
        input_output_aliases={6 + k: 4 + k for k in range(count)},
        compiler_params=params(8),
        cost_estimate=pl.CostEstimate(flops=1 << 20, bytes_accessed=4 << 20, transcendentals=0),
    )(place, *parts, *through)


def second_sum_kernel(place, total, a, b, c, d, dep, *rest):
    count = (len(rest) - 4) // 2
    high = jnp.floor(total[...] * (1 / 256))
    ends = jnp.concatenate([high, total[...] - 256 * high], axis=0).astype(BF16)
    for k, v in enumerate(rest[count : count + 4]):
        j = lax.rem(place[3] + k, HALF_Z)
        added = (a[j] + b[j].astype(F32)) + (c[j].astype(F32) + d[j].astype(F32))
        v[0:128, :] = added.astype(v.dtype)
        v[128:144, :] = ends


def second_sum(place, total, parts, dep, *through):
    count = len(through)
    shape = jax.ShapeDtypeStruct((144, 256), BF16)
    return pl.pallas_call(
        second_sum_kernel,
        grid=(1,),
        in_specs=[SMEM, whole(total)] + [whole(a) for a in parts] + [ANYWHERE] * (1 + count),
        out_specs=[whole(shape)] * 4 + [ANYWHERE] * count,
        out_shape=[shape] * 4 + [like(a) for a in through],
        input_output_aliases={7 + k: 4 + k for k in range(count)},
        compiler_params=params(8),
        cost_estimate=pl.CostEstimate(flops=1 << 19, bytes_accessed=1 << 20, transcendentals=0),
    )(place, total, *parts, dep, *through)


def third_sum_kernel(a, b, c, d, *rest):
    out = rest[len(rest) // 2]
    added = (a[...].astype(F32) + b[...].astype(F32)) + (c[...].astype(F32) + d[...].astype(F32))
    out[0:128, :] = added[0:128]
    out[128:136, :] = 256 * added[128:136] + added[136:144]


def third_sum(parts, *through):
    count = len(through)
    shape = jax.ShapeDtypeStruct((136, 256), F32)
    return pl.pallas_call(
        third_sum_kernel,
        grid=(1,),
        in_specs=[whole(a) for a in parts] + [ANYWHERE] * count,
        out_specs=[whole(shape)] + [ANYWHERE] * count,
        out_shape=[shape] + [like(a) for a in through],
        input_output_aliases={4 + k: 1 + k for k in range(count)},
        compiler_params=params(8),
        cost_estimate=pl.CostEstimate(flops=1 << 17, bytes_accessed=1 << 19, transcendentals=0),
    )(*parts, *through)


def merge_kernel(place, own, other, out, half):
    out[...] = own[...] + other[...]
    rows = pl.ds(pl.multiple_of(place[2] * 64, 64), 64)
    half[...] = own[rows, :] + other[rows, :]


def merge(place, own, other):
    half = jax.ShapeDtypeStruct((64, 256), F32)
    vmem = pl.BlockSpec(memory_space=pltpu.VMEM)
    return pl.pallas_call(
        merge_kernel,
        in_specs=[SMEM] + [vmem] * 2,
        out_specs=[vmem] * 2,
        out_shape=[like(own), half],
        compiler_params=params(8),
        cost_estimate=pl.CostEstimate(flops=1 << 16, bytes_accessed=1 << 19, transcendentals=0),
    )(place, own, other)


def after_kernel(*refs):
    pass


def after(*arrays):
    return pl.pallas_call(
        after_kernel,
        in_specs=[ANYWHERE] * len(arrays),
        out_specs=[ANYWHERE] * len(arrays),
        out_shape=[like(a) for a in arrays],
        input_output_aliases={k: k for k in range(len(arrays))},
        compiler_params=params(8),
        cost_estimate=pl.CostEstimate(flops=0, bytes_accessed=0, transcendentals=0),
    )(*arrays)


def assemble_kernel(place, own, near, near_other, far, *rest):
    x, c = place[0], place[2]
    step = 1 - 2 * c
    out = rest[-1]
    rows = own.shape[0]
    to = (x, lax.rem(x - step + NX, NX), lax.rem(x + step + NX, NX), lax.rem(x + 2, NX))
    for at, part in zip(to, (own, near, near_other, far)):
        out[pl.ds(pl.multiple_of(at * rows, rows), rows), :] = part[...]
    out[NX * rows :, :] = jnp.zeros((PAD, out.shape[1]), BF16)


def assemble(place, parts, dep):
    rows, width = parts[0].shape
    shape = jax.ShapeDtypeStruct((NX * rows + PAD, width), BF16)
    return pl.pallas_call(
        assemble_kernel,
        grid=(1,),
        in_specs=[SMEM] + [whole(a) for a in parts] + [ANYWHERE],
        out_specs=whole(shape),
        out_shape=shape,
        compiler_params=params(8),
        cost_estimate=pl.CostEstimate(flops=0, bytes_accessed=2 << 20, transcendentals=0),
    )(place, *parts, dep)


SPAN = 512


def where_to(place, distance, half):
    block = lax.rem(place[3] + distance * (1 - 2 * place[2]) + NZ, NZ)
    return pl.multiple_of((2 * block + half) * SPAN, SPAN)


def products_kernel(grads, *refs):
    chunks, out = refs[:-1], refs[-1]
    for k, chunk in enumerate(chunks):
        for n in range(2):
            out[2 * k + n] = nt_dot(grads[...], chunk[n * SPAN : (n + 1) * SPAN, :])


def products(grads, chunks):
    tokens, width = grads.shape
    pieces = 2 * len(chunks)
    vmem = pl.BlockSpec(memory_space=pltpu.VMEM)
    return pl.pallas_call(
        products_kernel,
        in_specs=[vmem] * (1 + len(chunks)),
        out_specs=vmem,
        out_shape=jax.ShapeDtypeStruct((pieces, tokens, SPAN), F32),
        compiler_params=params(16),
        cost_estimate=pl.CostEstimate(
            flops=2 * tokens * width * SPAN * pieces, bytes_accessed=pieces << 20, transcendentals=0
        ),
    )(grads, *chunks)


def scale_of(filled, total):
    scale = filled[0:1, :] * (DEVICES / total[128:129, :])
    return jnp.concatenate([scale] * (SPAN // 256), axis=1)


def scaled_kernel(distances, place, filled, total, grads, raw, *refs):
    made, out_sems = refs[-2:]
    chunks, out = refs[:-3], refs[-3]
    count = raw.shape[0]
    scale = scale_of(filled, total)
    stores = []
    for n in range(made.shape[0]):
        if n < count:
            piece = raw[n]
        else:
            k, at = divmod(n - count, 2)
            piece = nt_dot(grads[...], chunks[k][at * SPAN : (at + 1) * SPAN, :])
        made[n] = (piece * scale).astype(BF16)
        to = pl.ds(where_to(place, distances[n // 2], n % 2), SPAN)
        stores.append(pltpu.make_async_copy(made.at[n], out.at[:, to], out_sems.at[n]))
        stores[n].start()
    for store in stores:
        store.wait()


def scaled(place, filled, total, grads, raw, raw_distances, chunks, distances):
    tokens = grads.shape[0]
    count = raw.shape[0] + 2 * len(chunks)
    return pl.pallas_call(
        functools.partial(scaled_kernel, (*raw_distances, *distances)),
        in_specs=[SMEM] + [pl.BlockSpec(memory_space=pltpu.VMEM)] * (4 + len(chunks)),
        out_specs=HBM,
        out_shape=jax.ShapeDtypeStruct((tokens, NZ * NX * 256), BF16),
        scratch_shapes=[
            pltpu.VMEM((count, tokens, SPAN), BF16),
            pltpu.SemaphoreType.DMA((count,)),
        ],
        compiler_params=params(16),
        cost_estimate=pl.CostEstimate(flops=count << 17, bytes_accessed=count * 3 << 18, transcendentals=0),
    )(place, filled, total, grads, raw, *chunks)


def finish_kernel(place, filled, own, near, near_other, far, far_other, grads, last, last_other, *rest):
    weight_out, out, made, done, sems = rest[1:]
    y, c = place[1], place[2]
    step = 1 - 2 * c
    scale = scale_of(filled, own)
    stores = []
    for n, chunk in enumerate((last, last_other)):
        made[n] = (nt_dot(grads[...], chunk[...]) * scale).astype(BF16)
        to = pl.ds(where_to(place, HALF_Z, lax.rem(n + c, 2)), SPAN)
        stores.append(pltpu.make_async_copy(made.at[n], out.at[:, to], sems.at[n]))
        stores[n].start()

    inverse = DEVICES / own[128:129, :]

    def put(feature, part):
        done[:, pl.ds(pl.multiple_of(feature * 128, 128), 128)] = (part * inverse).T

    put(y, own[0:128, :])
    put(lax.rem(y - step + NY, NY), near[0:128, :])
    put(lax.rem(y + step + NY, NY), near_other[0:128, :])
    first = jnp.where(c == 0, far[...], far_other[...])
    second = jnp.where(c == 0, far_other[...], far[...])
    put(lax.rem(y + 2, NY), jnp.concatenate([first, second], axis=0))
    stores.append(pltpu.make_async_copy(done, weight_out, sems.at[2]))
    stores[2].start()
    for store in stores:
        store.wait()


def finish(place, filled, parts, grads, lasts, out):
    shape = jax.ShapeDtypeStruct((256, 512), F32)
    tokens = grads.shape[0]
    operands = [place, filled, *parts, grads, *lasts, out]
    return pl.pallas_call(
        finish_kernel,
        in_specs=[SMEM] + [pl.BlockSpec(memory_space=pltpu.VMEM)] * (len(operands) - 2) + [HBM],
        out_specs=[HBM] * 2,
        out_shape=[shape, like(out)],
        scratch_shapes=[
            pltpu.VMEM((2, tokens, SPAN), BF16),
            pltpu.VMEM(shape.shape, F32),
            pltpu.SemaphoreType.DMA((3,)),
        ],
        input_output_aliases={len(operands) - 1: 1},
        compiler_params=params(8),
        cost_estimate=pl.CostEstimate(flops=1 << 28, bytes_accessed=3 << 20, transcendentals=0),
    )(*operands)


def local(inputs, grad_values, value_weight, counts, loss_mask):
    tok_rows = inputs.shape[0]
    dp, group = lax.axis_index("dp"), lax.axis_index("group")
    z, x, y, c = dp // NX, dp % NX, group // 2, group % 2
    place = jnp.stack([x, y, c, z]).astype(jnp.int32)

    other_x = swap(inputs)
    near = hop(value_weight, lambda z, x, y, c: (z, x + 1 - 2 * c, y, c))
    filled = jnp.full((8, 256), counts[0].astype(F32))
    other_filled = swap(filled)
    positions = jnp.arange(tok_rows, dtype=jnp.int32)
    live = (positions < counts[0]) & (loss_mask > 0)
    grads = jnp.where(live[:, None], grad_values, jnp.zeros_like(grad_values))
    own_t = grads.T
    other_t = swap(own_t)

    rows, width = value_weight.shape
    near_other = swap(near)
    far = hop(near, lambda z, x, y, c: (z, x + 1 - 2 * c, y, c))

    added, grads = own_partials(place, filled, own_t, inputs, grads)
    s0, plus, minus, s1, s3 = partials(place, other_filled, other_t, other_x, added)
    s_moves = lambda r: lambda z, x, y, c: (z, x, y + r, c) if c == 0 else (z, x + r, y, c)
    u_moves = lambda r: lambda z, x, y, c: (z, x + r, y, c) if c == 0 else (z, x, y + r, c)
    around = lambda z, x, y, c: (z + 1 - 2 * c, x, y, c)
    chunk = assemble(place, (value_weight, near, near_other, far), s0)

    ring1 = hop(chunk, around)
    from_minus, from_plus = hop(plus, s_moves(1)), hop(minus, s_moves(-1))
    total = filled + other_filled
    total = total + hop(total, lambda z, x, y, c: (z, x, y + 1, c))
    s1, s3, ring1, total = relay(s1, s3, from_minus, from_plus, ring1, total)

    ring2, ring1_other = hop(ring1, around), swap(ring1)
    first = (s0, from_minus, from_plus, hop(s1, s_moves(1)), hop(s3, s_moves(-1)))
    total = total + hop(total, lambda z, x, y, c: (z, x + 1, y, c))
    total = total + hop(total, lambda z, x, y, c: (z, x, y + 2, c))
    u0, u1, u2, u3, ring2, ring1_other, total = first_sum(place, first, ring2, ring1_other, total)

    ring3, ring2_other = hop(ring2, around), swap(ring2)
    second = [u0] + [hop(u, u_moves(r)) for r, u in ((1, u1), (2, u2), (3, u3))]
    total = total + hop(total, lambda z, x, y, c: (z, x + 2, y, c))
    raw = products(grads, (chunk, ring1, ring1_other, ring2, ring2_other))
    *sends, ring3 = second_sum(place, total, second, raw, ring3)

    half = NX * rows // 2
    last = lax.dynamic_slice(ring3, (c * half, 0), (half, width))
    ring3_other = swap(ring3)
    third = [
        hop(sends[k], lambda z, x, y, c: (HALF_Z * c + (z + k) % HALF_Z, x, y, z // HALF_Z)) for k in range(4)
    ]
    block, last, ring3, ring3_other = third_sum(third, last, ring3, ring3_other)

    last = hop(last, around)
    block, part = merge(place, block, swap(block))
    near = hop(block, lambda z, x, y, c: (z, x, y + 1 - 2 * c, c))
    far = hop(part, lambda z, x, y, c: (z, x, y + 2, c))
    input_grad = scaled(place, filled, block, grads, raw, (0, -1, 1, -2, 2), (ring3, ring3_other), (-3, 3))
    near, far, last, input_grad = after(near, far, last, input_grad)
    parts = (block, near, swap(near), far, swap(far))
    weight_grad, input_grad = finish(place, filled, parts, grads, (last, swap(last)), input_grad)
    return (input_grad, weight_grad)


def solution(mesh):
    return jax.shard_map(
        local,
        mesh=mesh,
        in_specs=(
            P(("dp", "group"), None),
            P(("dp", "group"), None),
            P("dp", None),
            P(("dp", "group")),
            P(("dp", "group")),
        ),
        out_specs=(P(("dp", "group"), None), P("dp", None)),
        check_vma=False,
    )
```

time: 514 us -> 110 us (0.21)
  waiting for transfers between devices: 395 us -> 33.1 us
  blocking collectives: 81.4 us -> 0 us
  starting transfers between devices: 0.12 us -> 49.2 us
  matrix products: 18.2 us -> 0 us
  Pallas kernels: 0 us -> 16.9 us
  between operations: 15.1 us -> 1.83 us
    reduce_scatter x1 -> x0, waiting for transfers between devices: 235 us -> none  [local(): lax.psum_scatter(contract_rows(inputs, scaled), 'dp', scatter_dimension=0...]
    all_gather x1 -> x0, waiting for transfers between devices: 103 us -> none  [local(): lax.all_gather(value_weight, 'dp', axis=0, tiled=True)]
    psum x1 -> x0, blocking collectives: 81.4 us -> none  [local(): total = lax.psum(counts.astype(jnp.float32), ('dp', 'group'))]
    psum x1 -> x0, waiting for transfers between devices: 55.9 us -> none  [local(): summed = lax.psum(share, 'group')]
    ppermute x0 -> x34, starting transfers between devices: none -> 49.2 us  [hop(): return lax.ppermute(array, ('dp', 'group'), pairs)]
    ppermute x0 -> x34, waiting for transfers between devices: none -> 33.1 us  [hop(): return lax.ppermute(array, ('dp', 'group'), pairs)]
    dot_general x2 -> x0, matrix products: 18.2 us -> none  [the longest x1 10.5 us: contract_rows(): lax.dot_general(left, right, (((0,), (0,)), ((), ())), preferred_element_...]
    pallas_call x0 -> x12, Pallas kernels: none -> 16.9 us  [the longest x1 4.16 us: partials(): pl.pallas_call(other_kernel, grid=(HALF_Z,), in_specs=[SMEM, vmem, vmem,...]
  transfers between devices with their start and end apart: 3 -> 34, of which waited for: 3 -> 14; matrix products, arithmetic and copies ran while one was open for 2% -> 2% of each run, Pallas kernels for 0% -> 11%
where the time goes in v2:
time: 110 us; the launch traced here: 108 us
  starting transfers between devices  49.2 us (45%)
  waiting for transfers between devices  33.1 us (30%)
  Pallas kernels  16.9 us (15%)
  local copies, waits for them, and re-layouts  5.94 us (5%)
  between operations  1.83 us (2%)
    ppermute x34, starting transfers between devices, hop(): return lax.ppermute(array, ('dp', 'group'), pairs)  49.2 us
    ppermute x34, waiting for transfers between devices, hop(): return lax.ppermute(array, ('dp', 'group'), pairs)  33.1 us
    unnamed x9, local copies, waits for them, and re-layouts  5.77 us
    pallas_call x1, Pallas kernels, partials(): pl.pallas_call(other_kernel, grid=(HALF_Z,), in_specs=[SMEM, vmem, vmem,...  4.16 us
    pallas_call x1, Pallas kernels, scaled(): pl.pallas_call(functools.partial(scaled_kernel, (*raw_distances, *distanc...  2.72 us
    pallas_call x1, Pallas kernels, own_partials(): pl.pallas_call(own_kernel, grid=(HALF_Z,), in_specs=[SMEM, vmem, vmem, HB...  2.64 us
  transfers between devices with their start and end apart: 34, of which 14 were waited for; matrix products, arithmetic and copies ran while one was open for 2% of the time, Pallas kernels for 11%

profile of v2, /device:TPU:1, one launch (start us, length us, event | category | flops | bytes accessed | tf_op | source)
XLA Modules:
  0.0 107.7 jit_solution(3476422346890148477)
XLA Ops:
  0.6 3.3 %collective-permute-start.2 = (bf16[256,8192]{1,0:T(8,128)(2,1)}, bf16[256,8192]{1,0:T(8,128)(2,1)}, u32[]{:S(2)}, u32[]{:S(2)}) collective-permute-start(bf16[256,8192]{1,0:T(8,128)(2,1)} %source.1), channel_id=1, source_target_pairs={{0,1},{1,0},{2,3},{3,2},{4,5},{5,4},{6,7},{7,6},{8,9},{9,8},{10,11... | collective-permute-start | bytes 12582920 | tf_op jit(solution)/shard_map/ppermute | solution.py:31
  4.6 0.1 collective-permute-start
  4.7 0.8 collective-permute-start.5
  5.5 1.1 %copy.24 = bf16[256,512]{0,1:T(8,128)(2,1)S(1)} copy(bf16[256,512]{1,0:T(8,128)(2,1)} %param.6) | data formatting | bytes 524288 | tf_op args[1]
  6.6 0.7 compare_and_fusion
  7.3 0.1 collective-permute-start.1
  7.5 0.1 copy.25.grads
  7.7 2.8 %collective-permute-done.5.near = bf16[256,512]{1,0:T(8,128)(2,1)S(1)} collective-permute-done((bf16[256,512]{1,0:T(8,128)(2,1)}, bf16[256,512]{1,0:T(8,128)(2,1)S(1)}, u32[]{:S(2)}, u32[]{:S(2)}) %collective-permute-start.5) | collective-permute-done | bytes 262176 | tf_op jit(solution)/shard_map/ppermute | solution.py:31
  10.5 2.5 %collective-permute-start.6 = (bf16[256,512]{1,0:T(8,128)(2,1)S(1)}, bf16[256,512]{1,0:T(8,128)(2,1)S(1)}, u32[]{:S(2)}, u32[]{:S(2)}) collective-permute-start(bf16[256,512]{1,0:T(8,128)(2,1)S(1)} %collective-permute-done.5.near), channel_id=1, source_target_pairs={{0,1},{1,0},{2,3},{3,2},{4,5},{5,4},{6,7},{7,6},{8,9},{9,8},{10,11... | collective-permute-start | bytes 786440 | tf_op jit(solution)/shard_map/ppermute | solution.py:31
  13.0 0.1 pad_add_fusion.place
  13.1 2.2 %copy-done.2 = bf16[256,8192]{1,0:T(8,128)(2,1)S(1)} copy-done((bf16[256,8192]{1,0:T(8,128)(2,1)S(1)}, bf16[256,8192]{1,0:T(8,128)(2,1)}, u32[]{:S(2)}) %copy-start.2) | copy-done | bytes 4194328
  15.3 2.6 %shard_map.68 = (f32[4,4,512,256]{3,2,1,0:T(8,128)S(1)}, bf16[256,512]{1,0:T(8,128)(2,1)S(1)}) custom-call(s32[4]{0:T(128)S(1)} %pad_add_fusion.place, f32[8,256]{1,0:T(8,128)S(1)} %broadcast_in_dim.15.number.filled, bf16[512,256]{1,0:T(8,128)(2,1)S(1)} %fusion.1.gradient, bf16[256,8192]{1,0:T(8,128)(2,1)S(1)} %copy-done.2, ...), custom_call_target="tpu_custom_call", output_to_operand_aliasing={{1}: (4, {})} | custom-call | flops 1073741824 | bytes 4194304 | tf_op jit(solution)/shard_map/pallas_call | solution.py:160
  17.9 0.0 collective-permute-done.1.gradient
  18.0 0.0 collective-permute-done.2.source
  18.0 0.0 copy-start.3
  18.0 4.2 %shard_map.69 = (bf16[4,4,128,256]{3,2,1,0:T(8,128)(2,1)S(1)}, bf16[4,4,128,256]{3,2,1,0:T(8,128)(2,1)S(1)}, bf16[4,4,128,256]{3,2,1,0:T(8,128)(2,1)S(1)}, bf16[...) custom-call(s32[4]{0:T(128)S(1)} %pad_add_fusion.place, f32[8,256]{1,0:T(8,128)S(1)} %collective-permute-done.number, ...), custom_call_target="tpu_custom_call" | custom-call | flops 1073741824 | bytes 8388608 | tf_op jit(solution)/shard_map/pallas_call | solution.py:177
  22.2 0.6 shard_map.70.refs_0_
  22.8 5.2 %collective-permute-start.8 = (bf16[1040,512]{1,0:T(8,128)(2,1)S(1)}, bf16[1040,512]{1,0:T(8,128)(2,1)S(1)}, u32[]{:S(2)}, u32[]{:S(2)}) collective-permute-start(bf16[1040,512]{1,0:T(8,128)(2,1)S(1)} %shard_map.70.refs_0_), channel_id=1, source_target_pairs={{0,32},{1,225},{2,34},{3,227},{4,36},{5,229},{6,38},{7,231},{8,40}... | collective-permute-start | bytes 3194888 | tf_op jit(solution)/shard_map/ppermute | solution.py:31
  28.0 0.2 collective-permute-start.3
  28.2 2.5 %collective-permute-start.4 = (bf16[4,4,128,256]{3,2,1,0:T(8,128)(2,1)S(1)}, bf16[4,4,128,256]{3,2,1,0:T(8,128)(2,1)S(1)}, u32[]{:S(2)}, u32[]{:S(2)}) collective-permute-start(bf16[4,4,128,256]{3,2,1,0:T(8,128)(2,1)S(1)} %get-tuple-element.40), channel_id=1, source_target_pairs={{0,6},{1,25},{2,0},{3,27},{4,2},{5,29},{6,4},{7,31},{8,14},{9,1},{... | collective-permute-start | bytes 3145736 | tf_op jit(solution)/shard_map/ppermute | solution.py:31
  30.7 1.3 %collective-permute-start.9 = (f32[8,256]{1,0:T(8,128)S(1)}, f32[8,256]{1,0:T(8,128)S(1)}, u32[]{:S(2)}, u32[]{:S(2)}) collective-permute-start(f32[8,256]{1,0:T(8,128)S(1)} %broadcast_add_fusion), channel_id=1, source_target_pairs={{0,2},{1,3},{2,4},{3,5},{4,6},{5,7},{6,0},{7,1},{8,10},{9,11},{10,... | collective-permute-start | bytes 24584 | tf_op jit(solution)/shard_map/ppermute | solution.py:31
  32.0 2.9 %collective-permute-done.9 = f32[8,256]{1,0:T(8,128)S(1)} collective-permute-done((f32[8,256]{1,0:T(8,128)S(1)}, f32[8,256]{1,0:T(8,128)S(1)}, u32[]{:S(2)}, u32[]{:S(2)}) %collective-permute-start.9) | collective-permute-done | bytes 8224 | tf_op jit(solution)/shard_map/ppermute | solution.py:31
  34.9 8.0 %collective-permute-done.3.from_minus = bf16[4,4,128,256]{3,2,1,0:T(8,128)(2,1)S(1)} collective-permute-done((bf16[4,4,128,256]{3,2,1,0:T(8,128)(2,1)S(1)}, bf16[4,4,128,256]{3,2,1,0:T(8,128)(2,1)S(1)}, u32[]{:S(2)}, u32[]{:S(2)}) %collective-permute-start.3) | collective-permute-done | bytes 1048608 | tf_op jit(solution)/shard_map/ppermute | solution.py:31
  42.8 0.5 shard_map.71
  43.4 0.8 collective-permute-start.12
  44.2 2.7 %collective-permute-start.11 = (bf16[2,4,128,256]{3,2,1,0:T(8,128)(2,1)S(1)}, bf16[2,4,128,256]{3,2,1,0:T(8,128)(2,1)S(1)}, u32[]{:S(2)}, u32[]{:S(2)}) collective-permute-start(bf16[2,4,128,256]{3,2,1,0:T(8,128)(2,1)S(1)} %get-tuple-element.44), channel_id=1, source_target_pairs={{0,6},{1,25},{2,0},{3,27},{4,2},{5,29},{6,4},{7,31},{8,14},{9,1},{... | collective-permute-start | bytes 1572872 | tf_op jit(solution)/shard_map/ppermute | solution.py:31
  46.9 0.0 collective-permute-start.14
  46.9 7.0 %collective-permute-done.14 = f32[8,256]{1,0:T(8,128)S(1)} collective-permute-done((f32[8,256]{1,0:T(8,128)S(1)}, f32[8,256]{1,0:T(8,128)S(1)}, u32[]{:S(2)}, u32[]{:S(2)}) %collective-permute-start.14) | collective-permute-done | bytes 8224 | tf_op jit(solution)/shard_map/ppermute | solution.py:31
  53.9 2.9 %collective-permute-start.15 = (f32[8,256]{1,0:T(8,128)S(1)}, f32[8,256]{1,0:T(8,128)S(1)}, u32[]{:S(2)}, u32[]{:S(2)}) collective-permute-start(f32[8,256]{1,0:T(8,128)S(1)} %add.31), channel_id=1, source_target_pairs={{0,4},{1,5},{2,6},{3,7},{4,0},{5,1},{6,2},{7,3},{8,12},{9,13},{10,... | collective-permute-start | bytes 24584 | tf_op jit(solution)/shard_map/ppermute | solution.py:31
  56.8 1.1 %collective-permute-done.15 = f32[8,256]{1,0:T(8,128)S(1)} collective-permute-done((f32[8,256]{1,0:T(8,128)S(1)}, f32[8,256]{1,0:T(8,128)S(1)}, u32[]{:S(2)}, u32[]{:S(2)}) %collective-permute-start.15) | collective-permute-done | bytes 8224 | tf_op jit(solution)/shard_map/ppermute | solution.py:31
  58.0 1.4 %shard_map.72 = (f32[4,128,256]{2,1,0:T(8,128)S(1)}, bf16[4,128,256]{2,1,0:T(8,128)(2,1)S(1)}, bf16[4,128,256]{2,1,0:T(8,128)(2,1)S(1)}, bf16[4,128,256]{2,1,0:T...) custom-call(s32[4]{0:T(128)S(1)} %pad_add_fusion.place, ...), custom_call_target="tpu_custom_call", output_to_operand_aliasing={{4}: (6, {}), {5}: (7, {}), {6}: (8, {})} | custom-call | flops 1048576 | bytes 4194304 | tf_op jit(solution)/shard_map/pallas_call | solution.py:228
  59.4 0.3 collective-permute-start.20
  59.7 1.2 %collective-permute-start.21 = (bf16[1040,512]{1,0:T(8,128)(2,1)S(1)}, bf16[1040,512]{1,0:T(8,128)(2,1)S(1)}, u32[]{:S(2)}, u32[]{:S(2)}) collective-permute-start(bf16[1040,512]{1,0:T(8,128)(2,1)S(1)} %get-tuple-element.54.refs_3_), channel_id=1, source_target_pairs={{0,32},{1,225},{2,34},{3,227},{4,36},{5,229},{6,38},{7,231},{8,40}... | collective-permute-start | bytes 3194888 | tf_op jit(solution)/shard_map/ppermute | solution.py:31
  60.8 2.3 %collective-permute-start.16 = (f32[8,256]{1,0:T(8,128)S(1)}, f32[8,256]{1,0:T(8,128)S(1)}, u32[]{:S(2)}, u32[]{:S(2)}) collective-permute-start(f32[8,256]{1,0:T(8,128)S(1)} %get-tuple-element.47), channel_id=1, source_target_pairs={{0,16},{1,17},{2,18},{3,19},{4,20},{5,21},{6,22},{7,23},{8,24},{9,... | collective-permute-start | bytes 24584 | tf_op jit(solution)/shard_map/ppermute | solution.py:31
  63.1 1.3 %collective-permute-start.17 = (bf16[4,128,256]{2,1,0:T(8,128)(2,1)S(1)}, bf16[4,128,256]{2,1,0:T(8,128)(2,1)S(1)}, u32[]{:S(2)}, u32[]{:S(2)}) collective-permute-start(bf16[4,128,256]{2,1,0:T(8,128)(2,1)S(1)} %get-tuple-element.49), channel_id=1, source_target_pairs={{0,8},{1,3},{2,10},{3,5},{4,12},{5,7},{6,14},{7,1},{8,16},{9,11},{... | collective-permute-start | bytes 786440 | tf_op jit(solution)/shard_map/ppermute | solution.py:31
  64.4 2.5 %collective-permute-start.18 = (bf16[4,128,256]{2,1,0:T(8,128)(2,1)S(1)}, bf16[4,128,256]{2,1,0:T(8,128)(2,1)S(1)}, u32[]{:S(2)}, u32[]{:S(2)}) collective-permute-start(bf16[4,128,256]{2,1,0:T(8,128)(2,1)S(1)} %get-tuple-element.50), channel_id=1, source_target_pairs={{0,16},{1,5},{2,18},{3,7},{4,20},{5,1},{6,22},{7,3},{8,24},{9,13},... | collective-permute-start | bytes 786440 | tf_op jit(solution)/shard_map/ppermute | solution.py:31
  66.9 0.9 collective-permute-start.19
  67.8 1.6 %shard_map.73.dep.raw = f32[10,256,512]{2,1,0:T(8,128)S(1)} custom-call(bf16[256,512]{1,0:T(8,128)(2,1)S(1)} %get-tuple-element.52.grads, bf16[1040,512]{1,0:T(8,128)(2,1)S(1)} %shard_map.70.refs_0_, bf16[1040,512]{1,0:T(8,128)(2,1)S(1)} %get-tuple-element.45.refs_1_, bf16[1040,512]{1,0:T(8,128)(2,1)S(1)} %get-tuple-element.53.refs_2_, ...), custom_call_target="tpu_custom_call" | custom-call | flops 1342177280 | bytes 10485760 | tf_op jit(solution)/shard_map/pallas_call | solution.py:373
  69.4 0.5 collective-permute-done.17.b
  69.9 3.6 %collective-permute-done.18.c = bf16[4,128,256]{2,1,0:T(8,128)(2,1)S(1)} collective-permute-done((bf16[4,128,256]{2,1,0:T(8,128)(2,1)S(1)}, bf16[4,128,256]{2,1,0:T(8,128)(2,1)S(1)}, u32[]{:S(2)}, u32[]{:S(2)}) %collective-permute-start.18) | collective-permute-done | bytes 262176 | tf_op jit(solution)/shard_map/ppermute | solution.py:31
  73.5 0.3 collective-permute-done.21.rest_0_
  73.8 0.7 shard_map.74
  74.5 2.5 %collective-permute-start.26 = (bf16[1040,512]{1,0:T(8,128)(2,1)S(1)}, bf16[1040,512]{1,0:T(8,128)(2,1)S(1)}, u32[]{:S(2)}, u32[]{:S(2)}) collective-permute-start(bf16[1040,512]{1,0:T(8,128)(2,1)S(1)} %get-tuple-element.59.rest_1_), channel_id=1, source_target_pairs={{0,1},{1,0},{2,3},{3,2},{4,5},{5,4},{6,7},{7,6},{8,9},{9,8},{10,11... | collective-permute-start | bytes 3194888 | tf_op jit(solution)/shard_map/ppermute | solution.py:31
  76.9 5.9 %collective-permute-start.22 = (bf16[144,256]{1,0:T(8,128)(2,1)S(1)}, bf16[144,256]{1,0:T(8,128)(2,1)S(1)}, u32[]{:S(2)}, u32[]{:S(2)}) collective-permute-start(bf16[144,256]{1,0:T(8,128)(2,1)S(1)} %get-tuple-element.55), channel_id=1, source_target_pairs={{0,0},{1,128},{2,2},{3,130},{4,4},{5,132},{6,6},{7,134},{8,8},{9,1... | collective-permute-start | bytes 221192 | tf_op jit(solution)/shard_map/ppermute | solution.py:31
  82.9 0.1 collective-permute-start.23
  83.0 1.7 %collective-permute-start.24 = (bf16[144,256]{1,0:T(8,128)(2,1)S(1)}, bf16[144,256]{1,0:T(8,128)(2,1)S(1)}, u32[]{:S(2)}, u32[]{:S(2)}) collective-permute-start(bf16[144,256]{1,0:T(8,128)(2,1)S(1)} %get-tuple-element.57), channel_id=1, source_target_pairs={{0,64},{1,192},{2,66},{3,194},{4,68},{5,196},{6,70},{7,198},{8,72}... | collective-permute-start | bytes 221192 | tf_op jit(solution)/shard_map/ppermute | solution.py:31
  84.7 2.7 %collective-permute-start.25 = (bf16[144,256]{1,0:T(8,128)(2,1)S(1)}, bf16[144,256]{1,0:T(8,128)(2,1)S(1)}, u32[]{:S(2)}, u32[]{:S(2)}) collective-permute-start(bf16[144,256]{1,0:T(8,128)(2,1)S(1)} %get-tuple-element.58), channel_id=1, source_target_pairs={{0,96},{1,224},{2,98},{3,226},{4,100},{5,228},{6,102},{7,230},{8,1... | collective-permute-start | bytes 221192 | tf_op jit(solution)/shard_map/ppermute | solution.py:31
  87.4 0.5 collective-permute-done.22.a
  87.9 0.4 collective-permute-done.23.b
  88.3 0.8 collective-permute-done.24.c
  89.2 2.4 %collective-permute-done.25.d = bf16[144,256]{1,0:T(8,128)(2,1)S(1)} collective-permute-done((bf16[144,256]{1,0:T(8,128)(2,1)S(1)}, bf16[144,256]{1,0:T(8,128)(2,1)S(1)}, u32[]{:S(2)}, u32[]{:S(2)}) %collective-permute-start.25) | collective-permute-done | bytes 73760 | tf_op jit(solution)/shard_map/ppermute | solution.py:31
  91.6 0.1 collective-permute-start.30
  91.7 0.1 collective-permute-start.27
  91.8 1.3 %collective-permute-done.27.other = f32[136,256]{1,0:T(8,128)S(1)} collective-permute-done((f32[136,256]{1,0:T(8,128)S(1)}, f32[136,256]{1,0:T(8,128)S(1)}, u32[]{:S(2)}, u32[]{:S(2)}) %collective-permute-start.27) | collective-permute-done | bytes 139296 | tf_op jit(solution)/shard_map/ppermute | solution.py:31
  93.1 0.6 shard_map.76
  93.7 2.8 %collective-permute-start.28 = (f32[136,256]{1,0:T(8,128)S(1)}, f32[136,256]{1,0:T(8,128)S(1)}, u32[]{:S(2)}, u32[]{:S(2)}) collective-permute-start(f32[136,256]{1,0:T(8,128)S(1)} %get-tuple-element.61.total.own), channel_id=1, source_target_pairs={{0,2},{1,7},{2,4},{3,1},{4,6},{5,3},{6,0},{7,5},{8,10},{9,15},{10,... | collective-permute-start | bytes 417800 | tf_op jit(solution)/shard_map/ppermute | solution.py:31
  96.5 0.4 collective-permute-start.29
  97.0 2.5 %copy-done.1 = f32[10,256,512]{2,1,0:T(8,128)S(1)} copy-done((f32[10,256,512]{2,1,0:T(8,128)S(1)}, f32[10,256,512]{2,1,0:T(8,128)}, u32[]{:S(2)}) %copy-start.1) | copy-done | bytes 5242904
  99.5 2.7 %shard_map.77.refs_3_ = bf16[256,8192]{1,0:T(8,128)(2,1)} custom-call(s32[4]{0:T(128)S(1)} %pad_add_fusion.place, f32[8,256]{1,0:T(8,128)S(1)} %broadcast_in_dim.15.number.filled, f32[136,256]{1,0:T(8,128)S(1)} %get-tuple-element.61.total.own, bf16[256,512]{1,0:T(8,128)(2,1)S(1)} %get-tuple-element.52.grads, f32[10,256,512]{2,1,0:T(8,128)S(1)} %copy-done.1, ...), custom_call_target="tpu_custom_call" | custom-call | flops 1835008 | bytes 11010048 | tf_op jit(solution)/shard_map/pallas_call | solution.py:413
  102.2 1.5 %collective-permute-start.33 = (bf16[512,512]{1,0:T(8,128)(2,1)S(1)}, bf16[512,512]{1,0:T(8,128)(2,1)S(1)}, u32[]{:S(2)}, u32[]{:S(2)}) collective-permute-start(bf16[512,512]{1,0:T(8,128)(2,1)S(1)} %get-tuple-element.68.last), channel_id=1, source_target_pairs={{0,1},{1,0},{2,3},{3,2},{4,5},{5,4},{6,7},{7,6},{8,9},{9,8},{10,11... | collective-permute-start | bytes 1572872 | tf_op jit(solution)/shard_map/ppermute | solution.py:31
  103.8 0.1 collective-permute-start.31
  103.9 0.4 collective-permute-start.32
  104.3 1.3 %collective-permute-done.32.far_other = f32[64,256]{1,0:T(8,128)S(1)} collective-permute-done((f32[64,256]{1,0:T(8,128)S(1)}, f32[64,256]{1,0:T(8,128)S(1)}, u32[]{:S(2)}, u32[]{:S(2)}) %collective-permute-start.32) | collective-permute-done | bytes 65568 | tf_op jit(solution)/shard_map/ppermute | solution.py:31
  105.6 1.9 %shard_map.79 = (f32[256,512]{1,0:T(8,128)}, bf16[256,8192]{1,0:T(8,128)(2,1)}) custom-call(s32[4]{0:T(128)S(1)} %pad_add_fusion.place, f32[8,256]{1,0:T(8,128)S(1)} %broadcast_in_dim.15.number.filled, f32[136,256]{1,0:T(8,128)S(1)} %get-tuple-element.61.total.own, f32[136,256]{1,0:T(8,128)S(1)} %get-tuple-element.66.near, ...), custom_call_target="tpu_custom_call", output_to_operand_aliasing={{1}: (10, {})} | custom-call | flops 268435456 | bytes 3145728 | tf_op jit(solution)/shard_map/pallas_call | solution.py:460
  (37 shorter events, 0.2 us)
Async XLA Ops:
  0.6 17.3 %collective-permute-start.2 = (bf16[256,8192]{1,0:T(8,128)(2,1)}, bf16[256,8192]{1,0:T(8,128)(2,1)}, u32[]{:S(2)}, u32[]{:S(2)}) collective-permute-start(bf16[256,8192]{1,0:T(8,128)(2,1)} %source.1), channel_id=1, source_target_pairs={{0,1},{1,0},{2,3},{3,2},{4,5},{5,4},{6,7},{7,6},{8,9},{9,8},{10,11... | collective-permute-start | bytes 12582920 | tf_op jit(solution)/shard_map/ppermute | solution.py:31
  4.6 13.3 %collective-permute-start = (f32[8,256]{1,0:T(8,128)S(1)}, f32[8,256]{1,0:T(8,128)S(1)}, u32[]{:S(2)}, u32[]{:S(2)}) collective-permute-start(f32[8,256]{1,0:T(8,128)S(1)} %broadcast_in_dim.15.number.filled), channel_id=1, source_target_pairs={{0,1},{1,0},{2,3},{3,2},{4,5},{5,4},{6,7},{7,6},{8,9},{9,8},{10,11... | collective-permute-start | bytes 24584 | tf_op jit(solution)/shard_map/ppermute | solution.py:31
  4.7 5.8 %collective-permute-start.5 = (bf16[256,512]{1,0:T(8,128)(2,1)}, bf16[256,512]{1,0:T(8,128)(2,1)S(1)}, u32[]{:S(2)}, u32[]{:S(2)}) collective-permute-start(bf16[256,512]{1,0:T(8,128)(2,1)} %own.1), channel_id=1, source_target_pairs={{0,8},{1,25},{2,10},{3,27},{4,12},{5,29},{6,14},{7,31},{8,16},{9,1... | collective-permute-start | bytes 786440 | tf_op jit(solution)/shard_map/ppermute | solution.py:31
  7.3 10.6 %collective-permute-start.1 = (bf16[512,256]{1,0:T(8,128)(2,1)S(1)}, bf16[512,256]{1,0:T(8,128)(2,1)S(1)}, u32[]{:S(2)}, u32[]{:S(2)}) collective-permute-start(bf16[512,256]{1,0:T(8,128)(2,1)S(1)} %fusion.1.gradient), channel_id=1, source_target_pairs={{0,1},{1,0},{2,3},{3,2},{4,5},{5,4},{6,7},{7,6},{8,9},{9,8},{10,11... | collective-permute-start | bytes 786440 | tf_op jit(solution)/shard_map/ppermute | solution.py:31
  10.5 11.6 %collective-permute-start.6 = (bf16[256,512]{1,0:T(8,128)(2,1)S(1)}, bf16[256,512]{1,0:T(8,128)(2,1)S(1)}, u32[]{:S(2)}, u32[]{:S(2)}) collective-permute-start(bf16[256,512]{1,0:T(8,128)(2,1)S(1)} %collective-permute-done.5.near), channel_id=1, source_target_pairs={{0,1},{1,0},{2,3},{3,2},{4,5},{5,4},{6,7},{7,6},{8,9},{9,8},{10,11... | collective-permute-start | bytes 786440 | tf_op jit(solution)/shard_map/ppermute | solution.py:31
  13.0 9.1 %collective-permute-start.7 = (bf16[256,512]{1,0:T(8,128)(2,1)S(1)}, bf16[256,512]{1,0:T(8,128)(2,1)S(1)}, u32[]{:S(2)}, u32[]{:S(2)}) collective-permute-start(bf16[256,512]{1,0:T(8,128)(2,1)S(1)} %collective-permute-done.5.near), channel_id=1, source_target_pairs={{0,8},{1,25},{2,10},{3,27},{4,12},{5,29},{6,14},{7,31},{8,16},{9,1... | collective-permute-start | bytes 786440 | tf_op jit(solution)/shard_map/ppermute | solution.py:31
  13.1 2.2 %copy-start.2 = (bf16[256,8192]{1,0:T(8,128)(2,1)S(1)}, bf16[256,8192]{1,0:T(8,128)(2,1)}, u32[]{:S(2)}) copy-start(bf16[256,8192]{1,0:T(8,128)(2,1)} %source.1) | copy-start | bytes 12582916
  18.0 4.2 %copy-start.3 = (bf16[256,512]{1,0:T(8,128)(2,1)S(1)}, bf16[256,512]{1,0:T(8,128)(2,1)}, u32[]{:S(2)}) copy-start(bf16[256,512]{1,0:T(8,128)(2,1)} %own.1) | copy-start | bytes 786436
  22.8 20.0 %collective-permute-start.8 = (bf16[1040,512]{1,0:T(8,128)(2,1)S(1)}, bf16[1040,512]{1,0:T(8,128)(2,1)S(1)}, u32[]{:S(2)}, u32[]{:S(2)}) collective-permute-start(bf16[1040,512]{1,0:T(8,128)(2,1)S(1)} %shard_map.70.refs_0_), channel_id=1, source_target_pairs={{0,32},{1,225},{2,34},{3,227},{4,36},{5,229},{6,38},{7,231},{8,40}... | collective-permute-start | bytes 3194888 | tf_op jit(solution)/shard_map/ppermute | solution.py:31
  28.0 14.9 %collective-permute-start.3 = (bf16[4,4,128,256]{3,2,1,0:T(8,128)(2,1)S(1)}, bf16[4,4,128,256]{3,2,1,0:T(8,128)(2,1)S(1)}, u32[]{:S(2)}, u32[]{:S(2)}) collective-permute-start(bf16[4,4,128,256]{3,2,1,0:T(8,128)(2,1)S(1)} %get-tuple-element.39), channel_id=1, source_target_pairs={{0,2},{1,9},{2,4},{3,11},{4,6},{5,13},{6,0},{7,15},{8,10},{9,17},{... | collective-permute-start | bytes 3145736 | tf_op jit(solution)/shard_map/ppermute | solution.py:31
  28.2 14.7 %collective-permute-start.4 = (bf16[4,4,128,256]{3,2,1,0:T(8,128)(2,1)S(1)}, bf16[4,4,128,256]{3,2,1,0:T(8,128)(2,1)S(1)}, u32[]{:S(2)}, u32[]{:S(2)}) collective-permute-start(bf16[4,4,128,256]{3,2,1,0:T(8,128)(2,1)S(1)} %get-tuple-element.40), channel_id=1, source_target_pairs={{0,6},{1,25},{2,0},{3,27},{4,2},{5,29},{6,4},{7,31},{8,14},{9,1},{... | collective-permute-start | bytes 3145736 | tf_op jit(solution)/shard_map/ppermute | solution.py:31
  30.7 4.2 %collective-permute-start.9 = (f32[8,256]{1,0:T(8,128)S(1)}, f32[8,256]{1,0:T(8,128)S(1)}, u32[]{:S(2)}, u32[]{:S(2)}) collective-permute-start(f32[8,256]{1,0:T(8,128)S(1)} %broadcast_add_fusion), channel_id=1, source_target_pairs={{0,2},{1,3},{2,4},{3,5},{4,6},{5,7},{6,0},{7,1},{8,10},{9,11},{10,... | collective-permute-start | bytes 24584 | tf_op jit(solution)/shard_map/ppermute | solution.py:31
  43.4 14.5 %collective-permute-start.12 = (bf16[1040,512]{1,0:T(8,128)(2,1)S(1)}, bf16[1040,512]{1,0:T(8,128)(2,1)S(1)}, u32[]{:S(2)}, u32[]{:S(2)}) collective-permute-start(bf16[1040,512]{1,0:T(8,128)(2,1)S(1)} %get-tuple-element.45.refs_1_), channel_id=1, source_target_pairs={{0,32},{1,225},{2,34},{3,227},{4,36},{5,229},{6,38},{7,231},{8,40}... | collective-permute-start | bytes 3194888 | tf_op jit(solution)/shard_map/ppermute | solution.py:31
  44.2 13.8 %collective-permute-start.13 = (bf16[1040,512]{1,0:T(8,128)(2,1)S(1)}, bf16[1040,512]{1,0:T(8,128)(2,1)S(1)}, u32[]{:S(2)}, u32[]{:S(2)}) collective-permute-start(bf16[1040,512]{1,0:T(8,128)(2,1)S(1)} %get-tuple-element.45.refs_1_), channel_id=1, source_target_pairs={{0,1},{1,0},{2,3},{3,2},{4,5},{5,4},{6,7},{7,6},{8,9},{9,8},{10,11... | collective-permute-start | bytes 3194888 | tf_op jit(solution)/shard_map/ppermute | solution.py:31
  44.2 13.7 %collective-permute-start.10 = (bf16[2,4,128,256]{3,2,1,0:T(8,128)(2,1)S(1)}, bf16[2,4,128,256]{3,2,1,0:T(8,128)(2,1)S(1)}, u32[]{:S(2)}, u32[]{:S(2)}) collective-permute-start(bf16[2,4,128,256]{3,2,1,0:T(8,128)(2,1)S(1)} %get-tuple-element.43), channel_id=1, source_target_pairs={{0,2},{1,9},{2,4},{3,11},{4,6},{5,13},{6,0},{7,15},{8,10},{9,17},{... | collective-permute-start | bytes 1572872 | tf_op jit(solution)/shard_map/ppermute | solution.py:31
  44.2 13.7 %collective-permute-start.11 = (bf16[2,4,128,256]{3,2,1,0:T(8,128)(2,1)S(1)}, bf16[2,4,128,256]{3,2,1,0:T(8,128)(2,1)S(1)}, u32[]{:S(2)}, u32[]{:S(2)}) collective-permute-start(bf16[2,4,128,256]{3,2,1,0:T(8,128)(2,1)S(1)} %get-tuple-element.44), channel_id=1, source_target_pairs={{0,6},{1,25},{2,0},{3,27},{4,2},{5,29},{6,4},{7,31},{8,14},{9,1},{... | collective-permute-start | bytes 1572872 | tf_op jit(solution)/shard_map/ppermute | solution.py:31
  46.9 7.0 %collective-permute-start.14 = (f32[8,256]{1,0:T(8,128)S(1)}, f32[8,256]{1,0:T(8,128)S(1)}, u32[]{:S(2)}, u32[]{:S(2)}) collective-permute-start(f32[8,256]{1,0:T(8,128)S(1)} %get-tuple-element.46), channel_id=1, source_target_pairs={{0,8},{1,9},{2,10},{3,11},{4,12},{5,13},{6,14},{7,15},{8,16},{9,17... | collective-permute-start | bytes 24584 | tf_op jit(solution)/shard_map/ppermute | solution.py:31
  53.9 4.0 %collective-permute-start.15 = (f32[8,256]{1,0:T(8,128)S(1)}, f32[8,256]{1,0:T(8,128)S(1)}, u32[]{:S(2)}, u32[]{:S(2)}) collective-permute-start(f32[8,256]{1,0:T(8,128)S(1)} %add.31), channel_id=1, source_target_pairs={{0,4},{1,5},{2,6},{3,7},{4,0},{5,1},{6,2},{7,3},{8,12},{9,13},{10,... | collective-permute-start | bytes 24584 | tf_op jit(solution)/shard_map/ppermute | solution.py:31
  59.4 8.5 %collective-permute-start.20 = (bf16[1040,512]{1,0:T(8,128)(2,1)S(1)}, bf16[1040,512]{1,0:T(8,128)(2,1)S(1)}, u32[]{:S(2)}, u32[]{:S(2)}) collective-permute-start(bf16[1040,512]{1,0:T(8,128)(2,1)S(1)} %get-tuple-element.54.refs_3_), channel_id=1, source_target_pairs={{0,1},{1,0},{2,3},{3,2},{4,5},{5,4},{6,7},{7,6},{8,9},{9,8},{10,11... | collective-permute-start | bytes 3194888 | tf_op jit(solution)/shard_map/ppermute | solution.py:31
  59.7 14.1 %collective-permute-start.21 = (bf16[1040,512]{1,0:T(8,128)(2,1)S(1)}, bf16[1040,512]{1,0:T(8,128)(2,1)S(1)}, u32[]{:S(2)}, u32[]{:S(2)}) collective-permute-start(bf16[1040,512]{1,0:T(8,128)(2,1)S(1)} %get-tuple-element.54.refs_3_), channel_id=1, source_target_pairs={{0,32},{1,225},{2,34},{3,227},{4,36},{5,229},{6,38},{7,231},{8,40}... | collective-permute-start | bytes 3194888 | tf_op jit(solution)/shard_map/ppermute | solution.py:31
  60.8 6.1 %collective-permute-start.16 = (f32[8,256]{1,0:T(8,128)S(1)}, f32[8,256]{1,0:T(8,128)S(1)}, u32[]{:S(2)}, u32[]{:S(2)}) collective-permute-start(f32[8,256]{1,0:T(8,128)S(1)} %get-tuple-element.47), channel_id=1, source_target_pairs={{0,16},{1,17},{2,18},{3,19},{4,20},{5,21},{6,22},{7,23},{8,24},{9,... | collective-permute-start | bytes 24584 | tf_op jit(solution)/shard_map/ppermute | solution.py:31
  63.1 6.7 %collective-permute-start.17 = (bf16[4,128,256]{2,1,0:T(8,128)(2,1)S(1)}, bf16[4,128,256]{2,1,0:T(8,128)(2,1)S(1)}, u32[]{:S(2)}, u32[]{:S(2)}) collective-permute-start(bf16[4,128,256]{2,1,0:T(8,128)(2,1)S(1)} %get-tuple-element.49), channel_id=1, source_target_pairs={{0,8},{1,3},{2,10},{3,5},{4,12},{5,7},{6,14},{7,1},{8,16},{9,11},{... | collective-permute-start | bytes 786440 | tf_op jit(solution)/shard_map/ppermute | solution.py:31
  64.4 9.0 %collective-permute-start.18 = (bf16[4,128,256]{2,1,0:T(8,128)(2,1)S(1)}, bf16[4,128,256]{2,1,0:T(8,128)(2,1)S(1)}, u32[]{:S(2)}, u32[]{:S(2)}) collective-permute-start(bf16[4,128,256]{2,1,0:T(8,128)(2,1)S(1)} %get-tuple-element.50), channel_id=1, source_target_pairs={{0,16},{1,5},{2,18},{3,7},{4,20},{5,1},{6,22},{7,3},{8,24},{9,13},... | collective-permute-start | bytes 786440 | tf_op jit(solution)/shard_map/ppermute | solution.py:31
  66.9 6.6 %collective-permute-start.19 = (bf16[4,128,256]{2,1,0:T(8,128)(2,1)S(1)}, bf16[4,128,256]{2,1,0:T(8,128)(2,1)S(1)}, u32[]{:S(2)}, u32[]{:S(2)}) collective-permute-start(bf16[4,128,256]{2,1,0:T(8,128)(2,1)S(1)} %get-tuple-element.51), channel_id=1, source_target_pairs={{0,24},{1,7},{2,26},{3,1},{4,28},{5,3},{6,30},{7,5},{8,0},{9,15},{... | collective-permute-start | bytes 786440 | tf_op jit(solution)/shard_map/ppermute | solution.py:31
  69.4 5.1 %copy-start = (f32[10,256,512]{2,1,0:T(8,128)}, f32[10,256,512]{2,1,0:T(8,128)S(1)}, u32[]{:S(2)}) copy-start(f32[10,256,512]{2,1,0:T(8,128)S(1)} %shard_map.73.dep.raw) | copy-start | bytes 15728644
  74.5 17.1 %collective-permute-start.26 = (bf16[1040,512]{1,0:T(8,128)(2,1)S(1)}, bf16[1040,512]{1,0:T(8,128)(2,1)S(1)}, u32[]{:S(2)}, u32[]{:S(2)}) collective-permute-start(bf16[1040,512]{1,0:T(8,128)(2,1)S(1)} %get-tuple-element.59.rest_1_), channel_id=1, source_target_pairs={{0,1},{1,0},{2,3},{3,2},{4,5},{5,4},{6,7},{7,6},{8,9},{9,8},{10,11... | collective-permute-start | bytes 3194888 | tf_op jit(solution)/shard_map/ppermute | solution.py:31
  76.9 11.0 %collective-permute-start.22 = (bf16[144,256]{1,0:T(8,128)(2,1)S(1)}, bf16[144,256]{1,0:T(8,128)(2,1)S(1)}, u32[]{:S(2)}, u32[]{:S(2)}) collective-permute-start(bf16[144,256]{1,0:T(8,128)(2,1)S(1)} %get-tuple-element.55), channel_id=1, source_target_pairs={{0,0},{1,128},{2,2},{3,130},{4,4},{5,132},{6,6},{7,134},{8,8},{9,1... | collective-permute-start | bytes 221192 | tf_op jit(solution)/shard_map/ppermute | solution.py:31
  82.9 5.5 %collective-permute-start.23 = (bf16[144,256]{1,0:T(8,128)(2,1)S(1)}, bf16[144,256]{1,0:T(8,128)(2,1)S(1)}, u32[]{:S(2)}, u32[]{:S(2)}) collective-permute-start(bf16[144,256]{1,0:T(8,128)(2,1)S(1)} %get-tuple-element.56), channel_id=1, source_target_pairs={{0,32},{1,160},{2,34},{3,162},{4,36},{5,164},{6,38},{7,166},{8,40}... | collective-permute-start | bytes 221192 | tf_op jit(solution)/shard_map/ppermute | solution.py:31
  83.0 6.2 %collective-permute-start.24 = (bf16[144,256]{1,0:T(8,128)(2,1)S(1)}, bf16[144,256]{1,0:T(8,128)(2,1)S(1)}, u32[]{:S(2)}, u32[]{:S(2)}) collective-permute-start(bf16[144,256]{1,0:T(8,128)(2,1)S(1)} %get-tuple-element.57), channel_id=1, source_target_pairs={{0,64},{1,192},{2,66},{3,194},{4,68},{5,196},{6,70},{7,198},{8,72}... | collective-permute-start | bytes 221192 | tf_op jit(solution)/shard_map/ppermute | solution.py:31
  84.7 6.9 %collective-permute-start.25 = (bf16[144,256]{1,0:T(8,128)(2,1)S(1)}, bf16[144,256]{1,0:T(8,128)(2,1)S(1)}, u32[]{:S(2)}, u32[]{:S(2)}) collective-permute-start(bf16[144,256]{1,0:T(8,128)(2,1)S(1)} %get-tuple-element.58), channel_id=1, source_target_pairs={{0,96},{1,224},{2,98},{3,226},{4,100},{5,228},{6,102},{7,230},{8,1... | collective-permute-start | bytes 221192 | tf_op jit(solution)/shard_map/ppermute | solution.py:31
  91.6 10.6 %collective-permute-start.30 = (bf16[512,512]{1,0:T(8,128)(2,1)S(1)}, bf16[512,512]{1,0:T(8,128)(2,1)S(1)}, u32[]{:S(2)}, u32[]{:S(2)}) collective-permute-start(bf16[512,512]{1,0:T(8,128)(2,1)S(1)} %get-tuple-element.63), channel_id=1, source_target_pairs={{0,32},{1,225},{2,34},{3,227},{4,36},{5,229},{6,38},{7,231},{8,40}... | collective-permute-start | bytes 1572872 | tf_op jit(solution)/shard_map/ppermute | solution.py:31
  91.7 1.4 %collective-permute-start.27 = (f32[136,256]{1,0:T(8,128)S(1)}, f32[136,256]{1,0:T(8,128)S(1)}, u32[]{:S(2)}, u32[]{:S(2)}) collective-permute-start(f32[136,256]{1,0:T(8,128)S(1)} %get-tuple-element.60.own), channel_id=1, source_target_pairs={{0,1},{1,0},{2,3},{3,2},{4,5},{5,4},{6,7},{7,6},{8,9},{9,8},{10,11... | collective-permute-start | bytes 417800 | tf_op jit(solution)/shard_map/ppermute | solution.py:31
  93.7 8.5 %collective-permute-start.28 = (f32[136,256]{1,0:T(8,128)S(1)}, f32[136,256]{1,0:T(8,128)S(1)}, u32[]{:S(2)}, u32[]{:S(2)}) collective-permute-start(f32[136,256]{1,0:T(8,128)S(1)} %get-tuple-element.61.total.own), channel_id=1, source_target_pairs={{0,2},{1,7},{2,4},{3,1},{4,6},{5,3},{6,0},{7,5},{8,10},{9,15},{10,... | collective-permute-start | bytes 417800 | tf_op jit(solution)/shard_map/ppermute | solution.py:31
  96.5 5.7 %collective-permute-start.29 = (f32[64,256]{1,0:T(8,128)S(1)}, f32[64,256]{1,0:T(8,128)S(1)}, u32[]{:S(2)}, u32[]{:S(2)}) collective-permute-start(f32[64,256]{1,0:T(8,128)S(1)} %get-tuple-element.62), channel_id=1, source_target_pairs={{0,4},{1,5},{2,6},{3,7},{4,0},{5,1},{6,2},{7,3},{8,12},{9,13},{10,... | collective-permute-start | bytes 196616 | tf_op jit(solution)/shard_map/ppermute | solution.py:31
  97.0 2.5 %copy-start.1 = (f32[10,256,512]{2,1,0:T(8,128)S(1)}, f32[10,256,512]{2,1,0:T(8,128)}, u32[]{:S(2)}) copy-start(f32[10,256,512]{2,1,0:T(8,128)} %copy-done) | copy-start | bytes 15728644
  102.2 3.4 %collective-permute-start.33 = (bf16[512,512]{1,0:T(8,128)(2,1)S(1)}, bf16[512,512]{1,0:T(8,128)(2,1)S(1)}, u32[]{:S(2)}, u32[]{:S(2)}) collective-permute-start(bf16[512,512]{1,0:T(8,128)(2,1)S(1)} %get-tuple-element.68.last), channel_id=1, source_target_pairs={{0,1},{1,0},{2,3},{3,2},{4,5},{5,4},{6,7},{7,6},{8,9},{9,8},{10,11... | collective-permute-start | bytes 1572872 | tf_op jit(solution)/shard_map/ppermute | solution.py:31
  103.8 1.8 %collective-permute-start.31 = (f32[136,256]{1,0:T(8,128)S(1)}, f32[136,256]{1,0:T(8,128)S(1)}, u32[]{:S(2)}, u32[]{:S(2)}) collective-permute-start(f32[136,256]{1,0:T(8,128)S(1)} %get-tuple-element.66.near), channel_id=1, source_target_pairs={{0,1},{1,0},{2,3},{3,2},{4,5},{5,4},{6,7},{7,6},{8,9},{9,8},{10,11... | collective-permute-start | bytes 417800 | tf_op jit(solution)/shard_map/ppermute | solution.py:31
  103.9 1.7 %collective-permute-start.32 = (f32[64,256]{1,0:T(8,128)S(1)}, f32[64,256]{1,0:T(8,128)S(1)}, u32[]{:S(2)}, u32[]{:S(2)}) collective-permute-start(f32[64,256]{1,0:T(8,128)S(1)} %get-tuple-element.67.far), channel_id=1, source_target_pairs={{0,1},{1,0},{2,3},{3,2},{4,5},{5,4},{6,7},{7,6},{8,9},{9,8},{10,11... | collective-permute-start | bytes 196616 | tf_op jit(solution)/shard_map/ppermute | solution.py:31

commit v3 on v2

--- a/solution.py
+++ b/solution.py
@@ -66,7 +66,8 @@
     span = NX * 256
 
     def load(k):
-        cols = pl.ds(pl.multiple_of((place[2] * HALF_Z + k) * span, span), span)
+        far = lax.select(place[2] == 0, jnp.int32(k), jnp.where(k == 0, HALF_Z, NZ - k).astype(jnp.int32))
+        cols = pl.ds(pl.multiple_of(lax.rem(place[3] + far, NZ) * span, span), span)
         return pltpu.make_async_copy(source.at[:, cols], held.at[k], sems.at[k])
 
     @pl.when(i == 0)
@@ -248,8 +249,7 @@
     high = jnp.floor(total[...] * (1 / 256))
     ends = jnp.concatenate([high, total[...] - 256 * high], axis=0).astype(BF16)
     for k, v in enumerate(rest[count : count + 4]):
-        j = lax.rem(place[3] + k, HALF_Z)
-        added = (a[j] + b[j].astype(F32)) + (c[j].astype(F32) + d[j].astype(F32))
+        added = (a[k] + b[k].astype(F32)) + (c[k].astype(F32) + d[k].astype(F32))
         v[0:128, :] = added.astype(v.dtype)
         v[128:144, :] = ends
 
@@ -521,9 +521,8 @@
     half = NX * rows // 2
     last = lax.dynamic_slice(ring3, (c * half, 0), (half, width))
     ring3_other = swap(ring3)
-    third = [
-        hop(sends[k], lambda z, x, y, c: (HALF_Z * c + (z + k) % HALF_Z, x, y, z // HALF_Z)) for k in range(4)
-    ]
+    third = [hop(sends[0], lambda z, x, y, c: (z + HALF_Z * c, x, y, c))]
+    third += [hop(sends[k], lambda z, x, y, c: (z + k * (1 - 2 * c), x, y, c)) for k in range(1, HALF_Z)]
     block, last, ring3, ring3_other = third_sum(third, last, ring3, ring3_other)
 
     last = hop(last, around)

time: 110 us -> 109 us (level); the launches traced: 108 us -> 109 us
  transfers between devices with their start and end apart: 34 -> 34, of which waited for: 14 -> 13; matrix products, arithmetic and copies ran while one was open for 2% -> 2% of each run, Pallas kernels for 11% -> 11%
where the time goes in v3:
time: 109 us
  starting transfers between devices  50.1 us (46%)
  waiting for transfers between devices  33.1 us (30%)
  Pallas kernels  16.9 us (16%)
  local copies, waits for them, and re-layouts  5.94 us (5%)
  between operations  1.81 us (2%)
    ppermute x34, starting transfers between devices, hop(): return lax.ppermute(array, ('dp', 'group'), pairs)  50.1 us
    ppermute x34, waiting for transfers between devices, hop(): return lax.ppermute(array, ('dp', 'group'), pairs)  33.1 us
    unnamed x9, local copies, waits for them, and re-layouts  5.77 us
    pallas_call x1, Pallas kernels, partials(): pl.pallas_call(other_kernel, grid=(HALF_Z,), in_specs=[SMEM, vmem, vmem,...  4.18 us
    pallas_call x1, Pallas kernels, scaled(): pl.pallas_call(functools.partial(scaled_kernel, (*raw_distances, *distanc...  2.72 us
    pallas_call x1, Pallas kernels, own_partials(): pl.pallas_call(own_kernel, grid=(HALF_Z,), in_specs=[SMEM, vmem, vmem, HB...  2.65 us
  transfers between devices with their start and end apart: 34, of which 13 were waited for; matrix products, arithmetic and copies ran while one was open for 2% of the time, Pallas kernels for 11%

profile of v3, /device:TPU:1, one launch (start us, length us, event | category | flops | bytes accessed | tf_op | source)
XLA Modules:
  0.0 108.8 jit_solution(12971441276152661776)
XLA Ops:
  0.6 3.3 %collective-permute-start.2 = (bf16[256,8192]{1,0:T(8,128)(2,1)}, bf16[256,8192]{1,0:T(8,128)(2,1)}, u32[]{:S(2)}, u32[]{:S(2)}) collective-permute-start(bf16[256,8192]{1,0:T(8,128)(2,1)} %source.1), channel_id=1, source_target_pairs={{0,1},{1,0},{2,3},{3,2},{4,5},{5,4},{6,7},{7,6},{8,9},{9,8},{10,11... | collective-permute-start | bytes 12582920 | tf_op jit(solution)/shard_map/ppermute | solution.py:31
  4.6 0.1 collective-permute-start
  4.7 0.8 collective-permute-start.5
  5.5 1.1 copy.24
  6.6 0.7 compare_and_fusion
  7.3 0.1 collective-permute-start.1
  7.5 0.1 copy.25.grads
  7.7 2.8 %collective-permute-done.5.near = bf16[256,512]{1,0:T(8,128)(2,1)S(1)} collective-permute-done((bf16[256,512]{1,0:T(8,128)(2,1)}, bf16[256,512]{1,0:T(8,128)(2,1)S(1)}, u32[]{:S(2)}, u32[]{:S(2)}) %collective-permute-start.5) | collective-permute-done | bytes 262176 | tf_op jit(solution)/shard_map/ppermute | solution.py:31
  10.5 2.5 %collective-permute-start.6 = (bf16[256,512]{1,0:T(8,128)(2,1)S(1)}, bf16[256,512]{1,0:T(8,128)(2,1)S(1)}, u32[]{:S(2)}, u32[]{:S(2)}) collective-permute-start(bf16[256,512]{1,0:T(8,128)(2,1)S(1)} %collective-permute-done.5.near), channel_id=1, source_target_pairs={{0,1},{1,0},{2,3},{3,2},{4,5},{5,4},{6,7},{7,6},{8,9},{9,8},{10,11... | collective-permute-start | bytes 786440 | tf_op jit(solution)/shard_map/ppermute | solution.py:31
  13.0 0.0 collective-permute-start.7
  13.0 0.1 pad_add_fusion.place
  13.1 2.2 %copy-done.2 = bf16[256,8192]{1,0:T(8,128)(2,1)S(1)} copy-done((bf16[256,8192]{1,0:T(8,128)(2,1)S(1)}, bf16[256,8192]{1,0:T(8,128)(2,1)}, u32[]{:S(2)}) %copy-start.2) | copy-done | bytes 4194328
  15.3 2.6 %shard_map.68 = (f32[4,4,512,256]{3,2,1,0:T(8,128)S(1)}, bf16[256,512]{1,0:T(8,128)(2,1)S(1)}) custom-call(s32[4]{0:T(128)S(1)} %pad_add_fusion.place, f32[8,256]{1,0:T(8,128)S(1)} %broadcast_in_dim.15.number.filled, bf16[512,256]{1,0:T(8,128)(2,1)S(1)} %fusion.1.gradient, bf16[256,8192]{1,0:T(8,128)(2,1)S(1)} %copy-done.2, ...), custom_call_target="tpu_custom_call", output_to_operand_aliasing={{1}: (4, {})} | custom-call | flops 1073741824 | bytes 4194304 | tf_op jit(solution)/shard_map/pallas_call | solution.py:161
  17.9 0.0 collective-permute-done.number
  18.0 0.0 collective-permute-done.2.source
  18.0 0.0 copy-start.3
  18.0 4.2 %shard_map.69 = (bf16[4,4,128,256]{3,2,1,0:T(8,128)(2,1)S(1)}, bf16[4,4,128,256]{3,2,1,0:T(8,128)(2,1)S(1)}, bf16[4,4,128,256]{3,2,1,0:T(8,128)(2,1)S(1)}, bf16[...) custom-call(s32[4]{0:T(128)S(1)} %pad_add_fusion.place, f32[8,256]{1,0:T(8,128)S(1)} %collective-permute-done.number, ...), custom_call_target="tpu_custom_call" | custom-call | flops 1073741824 | bytes 8388608 | tf_op jit(solution)/shard_map/pallas_call | solution.py:178
  22.2 0.0 collective-permute-done.7.far
  22.2 0.6 shard_map.70.refs_0_
  22.8 5.2 %collective-permute-start.8 = (bf16[1040,512]{1,0:T(8,128)(2,1)S(1)}, bf16[1040,512]{1,0:T(8,128)(2,1)S(1)}, u32[]{:S(2)}, u32[]{:S(2)}) collective-permute-start(bf16[1040,512]{1,0:T(8,128)(2,1)S(1)} %shard_map.70.refs_0_), channel_id=1, source_target_pairs={{0,32},{1,225},{2,34},{3,227},{4,36},{5,229},{6,38},{7,231},{8,40}... | collective-permute-start | bytes 3194888 | tf_op jit(solution)/shard_map/ppermute | solution.py:31
  28.0 0.2 collective-permute-start.3
  28.2 2.5 %collective-permute-start.4 = (bf16[4,4,128,256]{3,2,1,0:T(8,128)(2,1)S(1)}, bf16[4,4,128,256]{3,2,1,0:T(8,128)(2,1)S(1)}, u32[]{:S(2)}, u32[]{:S(2)}) collective-permute-start(bf16[4,4,128,256]{3,2,1,0:T(8,128)(2,1)S(1)} %get-tuple-element.40), channel_id=1, source_target_pairs={{0,6},{1,25},{2,0},{3,27},{4,2},{5,29},{6,4},{7,31},{8,14},{9,1},{... | collective-permute-start | bytes 3145736 | tf_op jit(solution)/shard_map/ppermute | solution.py:31
  30.7 1.3 %collective-permute-start.9 = (f32[8,256]{1,0:T(8,128)S(1)}, f32[8,256]{1,0:T(8,128)S(1)}, u32[]{:S(2)}, u32[]{:S(2)}) collective-permute-start(f32[8,256]{1,0:T(8,128)S(1)} %broadcast_add_fusion), channel_id=1, source_target_pairs={{0,2},{1,3},{2,4},{3,5},{4,6},{5,7},{6,0},{7,1},{8,10},{9,11},{10,... | collective-permute-start | bytes 24584 | tf_op jit(solution)/shard_map/ppermute | solution.py:31
  32.0 2.9 %collective-permute-done.9 = f32[8,256]{1,0:T(8,128)S(1)} collective-permute-done((f32[8,256]{1,0:T(8,128)S(1)}, f32[8,256]{1,0:T(8,128)S(1)}, u32[]{:S(2)}, u32[]{:S(2)}) %collective-permute-start.9) | collective-permute-done | bytes 8224 | tf_op jit(solution)/shard_map/ppermute | solution.py:31
  34.9 8.0 %collective-permute-done.3.from_minus = bf16[4,4,128,256]{3,2,1,0:T(8,128)(2,1)S(1)} collective-permute-done((bf16[4,4,128,256]{3,2,1,0:T(8,128)(2,1)S(1)}, bf16[4,4,128,256]{3,2,1,0:T(8,128)(2,1)S(1)}, u32[]{:S(2)}, u32[]{:S(2)}) %collective-permute-start.3) | collective-permute-done | bytes 1048608 | tf_op jit(solution)/shard_map/ppermute | solution.py:31
  42.9 0.0 collective-permute-done.4.from_plus
  42.9 0.5 shard_map.71
  43.4 0.8 collective-permute-start.12
  44.2 2.7 %collective-permute-start.11 = (bf16[2,4,128,256]{3,2,1,0:T(8,128)(2,1)S(1)}, bf16[2,4,128,256]{3,2,1,0:T(8,128)(2,1)S(1)}, u32[]{:S(2)}, u32[]{:S(2)}) collective-permute-start(bf16[2,4,128,256]{3,2,1,0:T(8,128)(2,1)S(1)} %get-tuple-element.44), channel_id=1, source_target_pairs={{0,6},{1,25},{2,0},{3,27},{4,2},{5,29},{6,4},{7,31},{8,14},{9,1},{... | collective-permute-start | bytes 1572872 | tf_op jit(solution)/shard_map/ppermute | solution.py:31
  46.9 0.0 collective-permute-start.14
  46.9 7.0 %collective-permute-done.14 = f32[8,256]{1,0:T(8,128)S(1)} collective-permute-done((f32[8,256]{1,0:T(8,128)S(1)}, f32[8,256]{1,0:T(8,128)S(1)}, u32[]{:S(2)}, u32[]{:S(2)}) %collective-permute-start.14) | collective-permute-done | bytes 8224 | tf_op jit(solution)/shard_map/ppermute | solution.py:31
  54.0 2.9 %collective-permute-start.15 = (f32[8,256]{1,0:T(8,128)S(1)}, f32[8,256]{1,0:T(8,128)S(1)}, u32[]{:S(2)}, u32[]{:S(2)}) collective-permute-start(f32[8,256]{1,0:T(8,128)S(1)} %add.31), channel_id=1, source_target_pairs={{0,4},{1,5},{2,6},{3,7},{4,0},{5,1},{6,2},{7,3},{8,12},{9,13},{10,... | collective-permute-start | bytes 24584 | tf_op jit(solution)/shard_map/ppermute | solution.py:31
  56.9 1.1 %collective-permute-done.15 = f32[8,256]{1,0:T(8,128)S(1)} collective-permute-done((f32[8,256]{1,0:T(8,128)S(1)}, f32[8,256]{1,0:T(8,128)S(1)}, u32[]{:S(2)}, u32[]{:S(2)}) %collective-permute-start.15) | collective-permute-done | bytes 8224 | tf_op jit(solution)/shard_map/ppermute | solution.py:31
  58.0 1.4 %shard_map.72 = (f32[4,128,256]{2,1,0:T(8,128)S(1)}, bf16[4,128,256]{2,1,0:T(8,128)(2,1)S(1)}, bf16[4,128,256]{2,1,0:T(8,128)(2,1)S(1)}, bf16[4,128,256]{2,1,0:T...) custom-call(s32[4]{0:T(128)S(1)} %pad_add_fusion.place, ...), custom_call_target="tpu_custom_call", output_to_operand_aliasing={{4}: (6, {}), {5}: (7, {}), {6}: (8, {})} | custom-call | flops 1048576 | bytes 4194304 | tf_op jit(solution)/shard_map/pallas_call | solution.py:229
  59.4 0.3 collective-permute-start.20
  59.7 1.2 %collective-permute-start.21 = (bf16[1040,512]{1,0:T(8,128)(2,1)S(1)}, bf16[1040,512]{1,0:T(8,128)(2,1)S(1)}, u32[]{:S(2)}, u32[]{:S(2)}) collective-permute-start(bf16[1040,512]{1,0:T(8,128)(2,1)S(1)} %get-tuple-element.54.refs_3_), channel_id=1, source_target_pairs={{0,32},{1,225},{2,34},{3,227},{4,36},{5,229},{6,38},{7,231},{8,40}... | collective-permute-start | bytes 3194888 | tf_op jit(solution)/shard_map/ppermute | solution.py:31
  60.9 2.3 %collective-permute-start.16 = (f32[8,256]{1,0:T(8,128)S(1)}, f32[8,256]{1,0:T(8,128)S(1)}, u32[]{:S(2)}, u32[]{:S(2)}) collective-permute-start(f32[8,256]{1,0:T(8,128)S(1)} %get-tuple-element.47), channel_id=1, source_target_pairs={{0,16},{1,17},{2,18},{3,19},{4,20},{5,21},{6,22},{7,23},{8,24},{9,... | collective-permute-start | bytes 24584 | tf_op jit(solution)/shard_map/ppermute | solution.py:31
  63.2 1.3 %collective-permute-start.17 = (bf16[4,128,256]{2,1,0:T(8,128)(2,1)S(1)}, bf16[4,128,256]{2,1,0:T(8,128)(2,1)S(1)}, u32[]{:S(2)}, u32[]{:S(2)}) collective-permute-start(bf16[4,128,256]{2,1,0:T(8,128)(2,1)S(1)} %get-tuple-element.49), channel_id=1, source_target_pairs={{0,8},{1,3},{2,10},{3,5},{4,12},{5,7},{6,14},{7,1},{8,16},{9,11},{... | collective-permute-start | bytes 786440 | tf_op jit(solution)/shard_map/ppermute | solution.py:31
  64.5 2.5 %collective-permute-start.18 = (bf16[4,128,256]{2,1,0:T(8,128)(2,1)S(1)}, bf16[4,128,256]{2,1,0:T(8,128)(2,1)S(1)}, u32[]{:S(2)}, u32[]{:S(2)}) collective-permute-start(bf16[4,128,256]{2,1,0:T(8,128)(2,1)S(1)} %get-tuple-element.50), channel_id=1, source_target_pairs={{0,16},{1,5},{2,18},{3,7},{4,20},{5,1},{6,22},{7,3},{8,24},{9,13},... | collective-permute-start | bytes 786440 | tf_op jit(solution)/shard_map/ppermute | solution.py:31
  66.9 0.9 collective-permute-start.19
  67.9 1.6 %shard_map.73.dep.raw = f32[10,256,512]{2,1,0:T(8,128)S(1)} custom-call(bf16[256,512]{1,0:T(8,128)(2,1)S(1)} %get-tuple-element.52.grads, bf16[1040,512]{1,0:T(8,128)(2,1)S(1)} %shard_map.70.refs_0_, bf16[1040,512]{1,0:T(8,128)(2,1)S(1)} %get-tuple-element.45.refs_1_, bf16[1040,512]{1,0:T(8,128)(2,1)S(1)} %get-tuple-element.53.refs_2_, ...), custom_call_target="tpu_custom_call" | custom-call | flops 1342177280 | bytes 10485760 | tf_op jit(solution)/shard_map/pallas_call | solution.py:373
  69.4 0.5 collective-permute-done.17.b
  69.9 3.6 %collective-permute-done.18.c = bf16[4,128,256]{2,1,0:T(8,128)(2,1)S(1)} collective-permute-done((bf16[4,128,256]{2,1,0:T(8,128)(2,1)S(1)}, bf16[4,128,256]{2,1,0:T(8,128)(2,1)S(1)}, u32[]{:S(2)}, u32[]{:S(2)}) %collective-permute-start.18) | collective-permute-done | bytes 262176 | tf_op jit(solution)/shard_map/ppermute | solution.py:31
  73.5 0.3 collective-permute-done.21.rest_0_
  73.8 0.7 shard_map.74
  74.5 2.5 %collective-permute-start.26 = (bf16[1040,512]{1,0:T(8,128)(2,1)S(1)}, bf16[1040,512]{1,0:T(8,128)(2,1)S(1)}, u32[]{:S(2)}, u32[]{:S(2)}) collective-permute-start(bf16[1040,512]{1,0:T(8,128)(2,1)S(1)} %get-tuple-element.59.rest_1_), channel_id=1, source_target_pairs={{0,1},{1,0},{2,3},{3,2},{4,5},{5,4},{6,7},{7,6},{8,9},{9,8},{10,11... | collective-permute-start | bytes 3194888 | tf_op jit(solution)/shard_map/ppermute | solution.py:31
  77.0 6.0 %collective-permute-start.22 = (bf16[144,256]{1,0:T(8,128)(2,1)S(1)}, bf16[144,256]{1,0:T(8,128)(2,1)S(1)}, u32[]{:S(2)}, u32[]{:S(2)}) collective-permute-start(bf16[144,256]{1,0:T(8,128)(2,1)S(1)} %get-tuple-element.55), channel_id=1, source_target_pairs={{0,0},{1,129},{2,2},{3,131},{4,4},{5,133},{6,6},{7,135},{8,8},{9,1... | collective-permute-start | bytes 221192 | tf_op jit(solution)/shard_map/ppermute | solution.py:31
  83.0 1.0 collective-permute-start.23
  84.0 1.4 %collective-permute-start.25 = (bf16[144,256]{1,0:T(8,128)(2,1)S(1)}, bf16[144,256]{1,0:T(8,128)(2,1)S(1)}, u32[]{:S(2)}, u32[]{:S(2)}) collective-permute-start(bf16[144,256]{1,0:T(8,128)(2,1)S(1)} %get-tuple-element.58), channel_id=1, source_target_pairs={{0,96},{1,161},{2,98},{3,163},{4,100},{5,165},{6,102},{7,167},{8,1... | collective-permute-start | bytes 221192 | tf_op jit(solution)/shard_map/ppermute | solution.py:31
  85.4 1.5 %collective-permute-done.22.a = bf16[144,256]{1,0:T(8,128)(2,1)S(1)} collective-permute-done((bf16[144,256]{1,0:T(8,128)(2,1)S(1)}, bf16[144,256]{1,0:T(8,128)(2,1)S(1)}, u32[]{:S(2)}, u32[]{:S(2)}) %collective-permute-start.22) | collective-permute-done | bytes 73760 | tf_op jit(solution)/shard_map/ppermute | solution.py:31
  86.9 2.6 %collective-permute-done.24.c = bf16[144,256]{1,0:T(8,128)(2,1)S(1)} collective-permute-done((bf16[144,256]{1,0:T(8,128)(2,1)S(1)}, bf16[144,256]{1,0:T(8,128)(2,1)S(1)}, u32[]{:S(2)}, u32[]{:S(2)}) %collective-permute-start.24) | collective-permute-done | bytes 73760 | tf_op jit(solution)/shard_map/ppermute | solution.py:31
  89.5 0.2 collective-permute-done.25.d
  89.7 3.3 %collective-permute-start.30 = (bf16[512,512]{1,0:T(8,128)(2,1)S(1)}, bf16[512,512]{1,0:T(8,128)(2,1)S(1)}, u32[]{:S(2)}, u32[]{:S(2)}) collective-permute-start(bf16[512,512]{1,0:T(8,128)(2,1)S(1)} %get-tuple-element.63), channel_id=1, source_target_pairs={{0,32},{1,225},{2,34},{3,227},{4,36},{5,229},{6,38},{7,231},{8,40}... | collective-permute-start | bytes 1572872 | tf_op jit(solution)/shard_map/ppermute | solution.py:31
  93.0 1.4 %collective-permute-done.27.other = f32[136,256]{1,0:T(8,128)S(1)} collective-permute-done((f32[136,256]{1,0:T(8,128)S(1)}, f32[136,256]{1,0:T(8,128)S(1)}, u32[]{:S(2)}, u32[]{:S(2)}) %collective-permute-start.27) | collective-permute-done | bytes 139296 | tf_op jit(solution)/shard_map/ppermute | solution.py:31
  94.3 0.6 shard_map.76
  94.9 2.7 %collective-permute-start.28 = (f32[136,256]{1,0:T(8,128)S(1)}, f32[136,256]{1,0:T(8,128)S(1)}, u32[]{:S(2)}, u32[]{:S(2)}) collective-permute-start(f32[136,256]{1,0:T(8,128)S(1)} %get-tuple-element.61.total.own), channel_id=1, source_target_pairs={{0,2},{1,7},{2,4},{3,1},{4,6},{5,3},{6,0},{7,5},{8,10},{9,15},{10,... | collective-permute-start | bytes 417800 | tf_op jit(solution)/shard_map/ppermute | solution.py:31
  97.6 0.5 collective-permute-start.29
  98.1 2.5 %copy-done.1 = f32[10,256,512]{2,1,0:T(8,128)S(1)} copy-done((f32[10,256,512]{2,1,0:T(8,128)S(1)}, f32[10,256,512]{2,1,0:T(8,128)}, u32[]{:S(2)}) %copy-start.1) | copy-done | bytes 5242904
  100.5 2.7 %shard_map.77.refs_3_ = bf16[256,8192]{1,0:T(8,128)(2,1)} custom-call(s32[4]{0:T(128)S(1)} %pad_add_fusion.place, f32[8,256]{1,0:T(8,128)S(1)} %broadcast_in_dim.15.number.filled, f32[136,256]{1,0:T(8,128)S(1)} %get-tuple-element.61.total.own, bf16[256,512]{1,0:T(8,128)(2,1)S(1)} %get-tuple-element.52.grads, f32[10,256,512]{2,1,0:T(8,128)S(1)} %copy-done.1, ...), custom_call_target="tpu_custom_call" | custom-call | flops 1835008 | bytes 11010048 | tf_op jit(solution)/shard_map/pallas_call | solution.py:413
  103.3 1.5 %collective-permute-start.33 = (bf16[512,512]{1,0:T(8,128)(2,1)S(1)}, bf16[512,512]{1,0:T(8,128)(2,1)S(1)}, u32[]{:S(2)}, u32[]{:S(2)}) collective-permute-start(bf16[512,512]{1,0:T(8,128)(2,1)S(1)} %get-tuple-element.68.last), channel_id=1, source_target_pairs={{0,1},{1,0},{2,3},{3,2},{4,5},{5,4},{6,7},{7,6},{8,9},{9,8},{10,11... | collective-permute-start | bytes 1572872 | tf_op jit(solution)/shard_map/ppermute | solution.py:31
  104.8 0.1 collective-permute-start.31
  104.9 0.4 collective-permute-start.32
  105.3 1.3 %collective-permute-done.32.far_other = f32[64,256]{1,0:T(8,128)S(1)} collective-permute-done((f32[64,256]{1,0:T(8,128)S(1)}, f32[64,256]{1,0:T(8,128)S(1)}, u32[]{:S(2)}, u32[]{:S(2)}) %collective-permute-start.32) | collective-permute-done | bytes 65568 | tf_op jit(solution)/shard_map/ppermute | solution.py:31
  106.6 1.9 %shard_map.79 = (f32[256,512]{1,0:T(8,128)}, bf16[256,8192]{1,0:T(8,128)(2,1)}) custom-call(s32[4]{0:T(128)S(1)} %pad_add_fusion.place, f32[8,256]{1,0:T(8,128)S(1)} %broadcast_in_dim.15.number.filled, f32[136,256]{1,0:T(8,128)S(1)} %get-tuple-element.61.total.own, f32[136,256]{1,0:T(8,128)S(1)} %get-tuple-element.66.near, ...), custom_call_target="tpu_custom_call", output_to_operand_aliasing={{1}: (10, {})} | custom-call | flops 268435456 | bytes 3145728 | tf_op jit(solution)/shard_map/pallas_call | solution.py:460
  (37 shorter events, 0.2 us)
Async XLA Ops:
  0.6 17.3 %collective-permute-start.2 = (bf16[256,8192]{1,0:T(8,128)(2,1)}, bf16[256,8192]{1,0:T(8,128)(2,1)}, u32[]{:S(2)}, u32[]{:S(2)}) collective-permute-start(bf16[256,8192]{1,0:T(8,128)(2,1)} %source.1), channel_id=1, source_target_pairs={{0,1},{1,0},{2,3},{3,2},{4,5},{5,4},{6,7},{7,6},{8,9},{9,8},{10,11... | collective-permute-start | bytes 12582920 | tf_op jit(solution)/shard_map/ppermute | solution.py:31
  4.6 13.3 %collective-permute-start = (f32[8,256]{1,0:T(8,128)S(1)}, f32[8,256]{1,0:T(8,128)S(1)}, u32[]{:S(2)}, u32[]{:S(2)}) collective-permute-start(f32[8,256]{1,0:T(8,128)S(1)} %broadcast_in_dim.15.number.filled), channel_id=1, source_target_pairs={{0,1},{1,0},{2,3},{3,2},{4,5},{5,4},{6,7},{7,6},{8,9},{9,8},{10,11... | collective-permute-start | bytes 24584 | tf_op jit(solution)/shard_map/ppermute | solution.py:31
  4.7 5.8 %collective-permute-start.5 = (bf16[256,512]{1,0:T(8,128)(2,1)}, bf16[256,512]{1,0:T(8,128)(2,1)S(1)}, u32[]{:S(2)}, u32[]{:S(2)}) collective-permute-start(bf16[256,512]{1,0:T(8,128)(2,1)} %own.1), channel_id=1, source_target_pairs={{0,8},{1,25},{2,10},{3,27},{4,12},{5,29},{6,14},{7,31},{8,16},{9,1... | collective-permute-start | bytes 786440 | tf_op jit(solution)/shard_map/ppermute | solution.py:31
  7.3 10.6 %collective-permute-start.1 = (bf16[512,256]{1,0:T(8,128)(2,1)S(1)}, bf16[512,256]{1,0:T(8,128)(2,1)S(1)}, u32[]{:S(2)}, u32[]{:S(2)}) collective-permute-start(bf16[512,256]{1,0:T(8,128)(2,1)S(1)} %fusion.1.gradient), channel_id=1, source_target_pairs={{0,1},{1,0},{2,3},{3,2},{4,5},{5,4},{6,7},{7,6},{8,9},{9,8},{10,11... | collective-permute-start | bytes 786440 | tf_op jit(solution)/shard_map/ppermute | solution.py:31
  10.5 11.6 %collective-permute-start.6 = (bf16[256,512]{1,0:T(8,128)(2,1)S(1)}, bf16[256,512]{1,0:T(8,128)(2,1)S(1)}, u32[]{:S(2)}, u32[]{:S(2)}) collective-permute-start(bf16[256,512]{1,0:T(8,128)(2,1)S(1)} %collective-permute-done.5.near), channel_id=1, source_target_pairs={{0,1},{1,0},{2,3},{3,2},{4,5},{5,4},{6,7},{7,6},{8,9},{9,8},{10,11... | collective-permute-start | bytes 786440 | tf_op jit(solution)/shard_map/ppermute | solution.py:31
  13.0 9.2 %collective-permute-start.7 = (bf16[256,512]{1,0:T(8,128)(2,1)S(1)}, bf16[256,512]{1,0:T(8,128)(2,1)S(1)}, u32[]{:S(2)}, u32[]{:S(2)}) collective-permute-start(bf16[256,512]{1,0:T(8,128)(2,1)S(1)} %collective-permute-done.5.near), channel_id=1, source_target_pairs={{0,8},{1,25},{2,10},{3,27},{4,12},{5,29},{6,14},{7,31},{8,16},{9,1... | collective-permute-start | bytes 786440 | tf_op jit(solution)/shard_map/ppermute | solution.py:31
  13.1 2.2 %copy-start.2 = (bf16[256,8192]{1,0:T(8,128)(2,1)S(1)}, bf16[256,8192]{1,0:T(8,128)(2,1)}, u32[]{:S(2)}) copy-start(bf16[256,8192]{1,0:T(8,128)(2,1)} %source.1) | copy-start | bytes 12582916
  18.0 4.2 %copy-start.3 = (bf16[256,512]{1,0:T(8,128)(2,1)S(1)}, bf16[256,512]{1,0:T(8,128)(2,1)}, u32[]{:S(2)}) copy-start(bf16[256,512]{1,0:T(8,128)(2,1)} %own.1) | copy-start | bytes 786436
  22.8 20.0 %collective-permute-start.8 = (bf16[1040,512]{1,0:T(8,128)(2,1)S(1)}, bf16[1040,512]{1,0:T(8,128)(2,1)S(1)}, u32[]{:S(2)}, u32[]{:S(2)}) collective-permute-start(bf16[1040,512]{1,0:T(8,128)(2,1)S(1)} %shard_map.70.refs_0_), channel_id=1, source_target_pairs={{0,32},{1,225},{2,34},{3,227},{4,36},{5,229},{6,38},{7,231},{8,40}... | collective-permute-start | bytes 3194888 | tf_op jit(solution)/shard_map/ppermute | solution.py:31
  28.0 14.9 %collective-permute-start.3 = (bf16[4,4,128,256]{3,2,1,0:T(8,128)(2,1)S(1)}, bf16[4,4,128,256]{3,2,1,0:T(8,128)(2,1)S(1)}, u32[]{:S(2)}, u32[]{:S(2)}) collective-permute-start(bf16[4,4,128,256]{3,2,1,0:T(8,128)(2,1)S(1)} %get-tuple-element.39), channel_id=1, source_target_pairs={{0,2},{1,9},{2,4},{3,11},{4,6},{5,13},{6,0},{7,15},{8,10},{9,17},{... | collective-permute-start | bytes 3145736 | tf_op jit(solution)/shard_map/ppermute | solution.py:31
  28.2 14.7 %collective-permute-start.4 = (bf16[4,4,128,256]{3,2,1,0:T(8,128)(2,1)S(1)}, bf16[4,4,128,256]{3,2,1,0:T(8,128)(2,1)S(1)}, u32[]{:S(2)}, u32[]{:S(2)}) collective-permute-start(bf16[4,4,128,256]{3,2,1,0:T(8,128)(2,1)S(1)} %get-tuple-element.40), channel_id=1, source_target_pairs={{0,6},{1,25},{2,0},{3,27},{4,2},{5,29},{6,4},{7,31},{8,14},{9,1},{... | collective-permute-start | bytes 3145736 | tf_op jit(solution)/shard_map/ppermute | solution.py:31
  30.7 4.2 %collective-permute-start.9 = (f32[8,256]{1,0:T(8,128)S(1)}, f32[8,256]{1,0:T(8,128)S(1)}, u32[]{:S(2)}, u32[]{:S(2)}) collective-permute-start(f32[8,256]{1,0:T(8,128)S(1)} %broadcast_add_fusion), channel_id=1, source_target_pairs={{0,2},{1,3},{2,4},{3,5},{4,6},{5,7},{6,0},{7,1},{8,10},{9,11},{10,... | collective-permute-start | bytes 24584 | tf_op jit(solution)/shard_map/ppermute | solution.py:31
  43.4 14.5 %collective-permute-start.12 = (bf16[1040,512]{1,0:T(8,128)(2,1)S(1)}, bf16[1040,512]{1,0:T(8,128)(2,1)S(1)}, u32[]{:S(2)}, u32[]{:S(2)}) collective-permute-start(bf16[1040,512]{1,0:T(8,128)(2,1)S(1)} %get-tuple-element.45.refs_1_), channel_id=1, source_target_pairs={{0,32},{1,225},{2,34},{3,227},{4,36},{5,229},{6,38},{7,231},{8,40}... | collective-permute-start | bytes 3194888 | tf_op jit(solution)/shard_map/ppermute | solution.py:31
  44.2 13.8 %collective-permute-start.13 = (bf16[1040,512]{1,0:T(8,128)(2,1)S(1)}, bf16[1040,512]{1,0:T(8,128)(2,1)S(1)}, u32[]{:S(2)}, u32[]{:S(2)}) collective-permute-start(bf16[1040,512]{1,0:T(8,128)(2,1)S(1)} %get-tuple-element.45.refs_1_), channel_id=1, source_target_pairs={{0,1},{1,0},{2,3},{3,2},{4,5},{5,4},{6,7},{7,6},{8,9},{9,8},{10,11... | collective-permute-start | bytes 3194888 | tf_op jit(solution)/shard_map/ppermute | solution.py:31
  44.2 13.7 %collective-permute-start.10 = (bf16[2,4,128,256]{3,2,1,0:T(8,128)(2,1)S(1)}, bf16[2,4,128,256]{3,2,1,0:T(8,128)(2,1)S(1)}, u32[]{:S(2)}, u32[]{:S(2)}) collective-permute-start(bf16[2,4,128,256]{3,2,1,0:T(8,128)(2,1)S(1)} %get-tuple-element.43), channel_id=1, source_target_pairs={{0,2},{1,9},{2,4},{3,11},{4,6},{5,13},{6,0},{7,15},{8,10},{9,17},{... | collective-permute-start | bytes 1572872 | tf_op jit(solution)/shard_map/ppermute | solution.py:31
  44.2 13.7 %collective-permute-start.11 = (bf16[2,4,128,256]{3,2,1,0:T(8,128)(2,1)S(1)}, bf16[2,4,128,256]{3,2,1,0:T(8,128)(2,1)S(1)}, u32[]{:S(2)}, u32[]{:S(2)}) collective-permute-start(bf16[2,4,128,256]{3,2,1,0:T(8,128)(2,1)S(1)} %get-tuple-element.44), channel_id=1, source_target_pairs={{0,6},{1,25},{2,0},{3,27},{4,2},{5,29},{6,4},{7,31},{8,14},{9,1},{... | collective-permute-start | bytes 1572872 | tf_op jit(solution)/shard_map/ppermute | solution.py:31
  46.9 7.0 %collective-permute-start.14 = (f32[8,256]{1,0:T(8,128)S(1)}, f32[8,256]{1,0:T(8,128)S(1)}, u32[]{:S(2)}, u32[]{:S(2)}) collective-permute-start(f32[8,256]{1,0:T(8,128)S(1)} %get-tuple-element.46), channel_id=1, source_target_pairs={{0,8},{1,9},{2,10},{3,11},{4,12},{5,13},{6,14},{7,15},{8,16},{9,17... | collective-permute-start | bytes 24584 | tf_op jit(solution)/shard_map/ppermute | solution.py:31
  54.0 4.0 %collective-permute-start.15 = (f32[8,256]{1,0:T(8,128)S(1)}, f32[8,256]{1,0:T(8,128)S(1)}, u32[]{:S(2)}, u32[]{:S(2)}) collective-permute-start(f32[8,256]{1,0:T(8,128)S(1)} %add.31), channel_id=1, source_target_pairs={{0,4},{1,5},{2,6},{3,7},{4,0},{5,1},{6,2},{7,3},{8,12},{9,13},{10,... | collective-permute-start | bytes 24584 | tf_op jit(solution)/shard_map/ppermute | solution.py:31
  59.4 8.5 %collective-permute-start.20 = (bf16[1040,512]{1,0:T(8,128)(2,1)S(1)}, bf16[1040,512]{1,0:T(8,128)(2,1)S(1)}, u32[]{:S(2)}, u32[]{:S(2)}) collective-permute-start(bf16[1040,512]{1,0:T(8,128)(2,1)S(1)} %get-tuple-element.54.refs_3_), channel_id=1, source_target_pairs={{0,1},{1,0},{2,3},{3,2},{4,5},{5,4},{6,7},{7,6},{8,9},{9,8},{10,11... | collective-permute-start | bytes 3194888 | tf_op jit(solution)/shard_map/ppermute | solution.py:31
  59.7 14.1 %collective-permute-start.21 = (bf16[1040,512]{1,0:T(8,128)(2,1)S(1)}, bf16[1040,512]{1,0:T(8,128)(2,1)S(1)}, u32[]{:S(2)}, u32[]{:S(2)}) collective-permute-start(bf16[1040,512]{1,0:T(8,128)(2,1)S(1)} %get-tuple-element.54.refs_3_), channel_id=1, source_target_pairs={{0,32},{1,225},{2,34},{3,227},{4,36},{5,229},{6,38},{7,231},{8,40}... | collective-permute-start | bytes 3194888 | tf_op jit(solution)/shard_map/ppermute | solution.py:31
  60.9 6.1 %collective-permute-start.16 = (f32[8,256]{1,0:T(8,128)S(1)}, f32[8,256]{1,0:T(8,128)S(1)}, u32[]{:S(2)}, u32[]{:S(2)}) collective-permute-start(f32[8,256]{1,0:T(8,128)S(1)} %get-tuple-element.47), channel_id=1, source_target_pairs={{0,16},{1,17},{2,18},{3,19},{4,20},{5,21},{6,22},{7,23},{8,24},{9,... | collective-permute-start | bytes 24584 | tf_op jit(solution)/shard_map/ppermute | solution.py:31
  63.2 6.7 %collective-permute-start.17 = (bf16[4,128,256]{2,1,0:T(8,128)(2,1)S(1)}, bf16[4,128,256]{2,1,0:T(8,128)(2,1)S(1)}, u32[]{:S(2)}, u32[]{:S(2)}) collective-permute-start(bf16[4,128,256]{2,1,0:T(8,128)(2,1)S(1)} %get-tuple-element.49), channel_id=1, source_target_pairs={{0,8},{1,3},{2,10},{3,5},{4,12},{5,7},{6,14},{7,1},{8,16},{9,11},{... | collective-permute-start | bytes 786440 | tf_op jit(solution)/shard_map/ppermute | solution.py:31
  64.5 9.0 %collective-permute-start.18 = (bf16[4,128,256]{2,1,0:T(8,128)(2,1)S(1)}, bf16[4,128,256]{2,1,0:T(8,128)(2,1)S(1)}, u32[]{:S(2)}, u32[]{:S(2)}) collective-permute-start(bf16[4,128,256]{2,1,0:T(8,128)(2,1)S(1)} %get-tuple-element.50), channel_id=1, source_target_pairs={{0,16},{1,5},{2,18},{3,7},{4,20},{5,1},{6,22},{7,3},{8,24},{9,13},... | collective-permute-start | bytes 786440 | tf_op jit(solution)/shard_map/ppermute | solution.py:31
  66.9 6.6 %collective-permute-start.19 = (bf16[4,128,256]{2,1,0:T(8,128)(2,1)S(1)}, bf16[4,128,256]{2,1,0:T(8,128)(2,1)S(1)}, u32[]{:S(2)}, u32[]{:S(2)}) collective-permute-start(bf16[4,128,256]{2,1,0:T(8,128)(2,1)S(1)} %get-tuple-element.51), channel_id=1, source_target_pairs={{0,24},{1,7},{2,26},{3,1},{4,28},{5,3},{6,30},{7,5},{8,0},{9,15},{... | collective-permute-start | bytes 786440 | tf_op jit(solution)/shard_map/ppermute | solution.py:31
  69.4 5.0 %copy-start = (f32[10,256,512]{2,1,0:T(8,128)}, f32[10,256,512]{2,1,0:T(8,128)S(1)}, u32[]{:S(2)}) copy-start(f32[10,256,512]{2,1,0:T(8,128)S(1)} %shard_map.73.dep.raw) | copy-start | bytes 15728644
  74.5 15.2 %collective-permute-start.26 = (bf16[1040,512]{1,0:T(8,128)(2,1)S(1)}, bf16[1040,512]{1,0:T(8,128)(2,1)S(1)}, u32[]{:S(2)}, u32[]{:S(2)}) collective-permute-start(bf16[1040,512]{1,0:T(8,128)(2,1)S(1)} %get-tuple-element.59.rest_1_), channel_id=1, source_target_pairs={{0,1},{1,0},{2,3},{3,2},{4,5},{5,4},{6,7},{7,6},{8,9},{9,8},{10,11... | collective-permute-start | bytes 3194888 | tf_op jit(solution)/shard_map/ppermute | solution.py:31
  77.0 10.0 %collective-permute-start.22 = (bf16[144,256]{1,0:T(8,128)(2,1)S(1)}, bf16[144,256]{1,0:T(8,128)(2,1)S(1)}, u32[]{:S(2)}, u32[]{:S(2)}) collective-permute-start(bf16[144,256]{1,0:T(8,128)(2,1)S(1)} %get-tuple-element.55), channel_id=1, source_target_pairs={{0,0},{1,129},{2,2},{3,131},{4,4},{5,133},{6,6},{7,135},{8,8},{9,1... | collective-permute-start | bytes 221192 | tf_op jit(solution)/shard_map/ppermute | solution.py:31
  83.0 3.9 %collective-permute-start.23 = (bf16[144,256]{1,0:T(8,128)(2,1)S(1)}, bf16[144,256]{1,0:T(8,128)(2,1)S(1)}, u32[]{:S(2)}, u32[]{:S(2)}) collective-permute-start(bf16[144,256]{1,0:T(8,128)(2,1)S(1)} %get-tuple-element.56), channel_id=1, source_target_pairs={{0,32},{1,225},{2,34},{3,227},{4,36},{5,229},{6,38},{7,231},{8,40}... | collective-permute-start | bytes 221192 | tf_op jit(solution)/shard_map/ppermute | solution.py:31
  84.0 5.5 %collective-permute-start.24 = (bf16[144,256]{1,0:T(8,128)(2,1)S(1)}, bf16[144,256]{1,0:T(8,128)(2,1)S(1)}, u32[]{:S(2)}, u32[]{:S(2)}) collective-permute-start(bf16[144,256]{1,0:T(8,128)(2,1)S(1)} %get-tuple-element.57), channel_id=1, source_target_pairs={{0,64},{1,193},{2,66},{3,195},{4,68},{5,197},{6,70},{7,199},{8,72}... | collective-permute-start | bytes 221192 | tf_op jit(solution)/shard_map/ppermute | solution.py:31
  84.0 5.7 %collective-permute-start.25 = (bf16[144,256]{1,0:T(8,128)(2,1)S(1)}, bf16[144,256]{1,0:T(8,128)(2,1)S(1)}, u32[]{:S(2)}, u32[]{:S(2)}) collective-permute-start(bf16[144,256]{1,0:T(8,128)(2,1)S(1)} %get-tuple-element.58), channel_id=1, source_target_pairs={{0,96},{1,161},{2,98},{3,163},{4,100},{5,165},{6,102},{7,167},{8,1... | collective-permute-start | bytes 221192 | tf_op jit(solution)/shard_map/ppermute | solution.py:31
  89.7 13.6 %collective-permute-start.30 = (bf16[512,512]{1,0:T(8,128)(2,1)S(1)}, bf16[512,512]{1,0:T(8,128)(2,1)S(1)}, u32[]{:S(2)}, u32[]{:S(2)}) collective-permute-start(bf16[512,512]{1,0:T(8,128)(2,1)S(1)} %get-tuple-element.63), channel_id=1, source_target_pairs={{0,32},{1,225},{2,34},{3,227},{4,36},{5,229},{6,38},{7,231},{8,40}... | collective-permute-start | bytes 1572872 | tf_op jit(solution)/shard_map/ppermute | solution.py:31
  93.0 1.4 %collective-permute-start.27 = (f32[136,256]{1,0:T(8,128)S(1)}, f32[136,256]{1,0:T(8,128)S(1)}, u32[]{:S(2)}, u32[]{:S(2)}) collective-permute-start(f32[136,256]{1,0:T(8,128)S(1)} %get-tuple-element.60.own), channel_id=1, source_target_pairs={{0,1},{1,0},{2,3},{3,2},{4,5},{5,4},{6,7},{7,6},{8,9},{9,8},{10,11... | collective-permute-start | bytes 417800 | tf_op jit(solution)/shard_map/ppermute | solution.py:31
  94.9 8.4 %collective-permute-start.28 = (f32[136,256]{1,0:T(8,128)S(1)}, f32[136,256]{1,0:T(8,128)S(1)}, u32[]{:S(2)}, u32[]{:S(2)}) collective-permute-start(f32[136,256]{1,0:T(8,128)S(1)} %get-tuple-element.61.total.own), channel_id=1, source_target_pairs={{0,2},{1,7},{2,4},{3,1},{4,6},{5,3},{6,0},{7,5},{8,10},{9,15},{10,... | collective-permute-start | bytes 417800 | tf_op jit(solution)/shard_map/ppermute | solution.py:31
  97.6 5.7 %collective-permute-start.29 = (f32[64,256]{1,0:T(8,128)S(1)}, f32[64,256]{1,0:T(8,128)S(1)}, u32[]{:S(2)}, u32[]{:S(2)}) collective-permute-start(f32[64,256]{1,0:T(8,128)S(1)} %get-tuple-element.62), channel_id=1, source_target_pairs={{0,4},{1,5},{2,6},{3,7},{4,0},{5,1},{6,2},{7,3},{8,12},{9,13},{10,... | collective-permute-start | bytes 196616 | tf_op jit(solution)/shard_map/ppermute | solution.py:31
  98.1 2.5 %copy-start.1 = (f32[10,256,512]{2,1,0:T(8,128)S(1)}, f32[10,256,512]{2,1,0:T(8,128)}, u32[]{:S(2)}) copy-start(f32[10,256,512]{2,1,0:T(8,128)} %copy-done) | copy-start | bytes 15728644
  103.3 3.3 %collective-permute-start.33 = (bf16[512,512]{1,0:T(8,128)(2,1)S(1)}, bf16[512,512]{1,0:T(8,128)(2,1)S(1)}, u32[]{:S(2)}, u32[]{:S(2)}) collective-permute-start(bf16[512,512]{1,0:T(8,128)(2,1)S(1)} %get-tuple-element.68.last), channel_id=1, source_target_pairs={{0,1},{1,0},{2,3},{3,2},{4,5},{5,4},{6,7},{7,6},{8,9},{9,8},{10,11... | collective-permute-start | bytes 1572872 | tf_op jit(solution)/shard_map/ppermute | solution.py:31
  104.8 1.8 %collective-permute-start.31 = (f32[136,256]{1,0:T(8,128)S(1)}, f32[136,256]{1,0:T(8,128)S(1)}, u32[]{:S(2)}, u32[]{:S(2)}) collective-permute-start(f32[136,256]{1,0:T(8,128)S(1)} %get-tuple-element.66.near), channel_id=1, source_target_pairs={{0,1},{1,0},{2,3},{3,2},{4,5},{5,4},{6,7},{7,6},{8,9},{9,8},{10,11... | collective-permute-start | bytes 417800 | tf_op jit(solution)/shard_map/ppermute | solution.py:31
  104.9 1.7 %collective-permute-start.32 = (f32[64,256]{1,0:T(8,128)S(1)}, f32[64,256]{1,0:T(8,128)S(1)}, u32[]{:S(2)}, u32[]{:S(2)}) collective-permute-start(f32[64,256]{1,0:T(8,128)S(1)} %get-tuple-element.67.far), channel_id=1, source_target_pairs={{0,1},{1,0},{2,3},{3,2},{4,5},{5,4},{6,7},{7,6},{8,9},{9,8},{10,11... | collective-permute-start | bytes 196616 | tf_op jit(solution)/shard_map/ppermute | solution.py:31

commit v4 on v3

--- a/solution.py
+++ b/solution.py
@@ -208,65 +208,73 @@
     )(s1, s3, from_minus, from_plus, *through)
 
 
-def first_sum_kernel(place, s0, from_minus, from_plus, late_minus, late_plus, *rest):
-    count = (len(rest) - 5) // 2
-    added = rest[-1]
+def split_count(total):
+    high = jnp.floor(total * (1 / 256))
+    return jnp.concatenate([high, total - 256 * high], axis=0)
+
+
+def first_sum_kernel(place, total, s0, from_minus, from_plus, late_minus, late_plus, u0, u1, u2, u3, added):
+    i = pl.program_id(0)
     for k in range(2):
         added[k] = s0[k, 0].astype(F32) + (late_minus[k, 0].astype(F32) + from_plus[k, 0].astype(F32))
         added[2 + k] = s0[2 + k, 0].astype(F32) + (late_plus[k, 0].astype(F32) + from_minus[k, 0].astype(F32))
     own = lax.select(place[2] == 0, place[0], place[1])
-    for r, u in enumerate(rest[count : count + 4]):
-        u[0] = added[lax.rem(own + r, 4)].astype(u.dtype)
-
-
-def first_sum(place, parts, *through):
-    four = pl.BlockSpec((4, 1, 128, 256), lambda i, p: (0, i, 0, 0))
-    low = pl.BlockSpec((2, 1, 128, 256), lambda i, p: (0, i, 0, 0))
-    high = pl.BlockSpec((2, 1, 128, 256), lambda i, p: (1, i, 0, 0))
-    out = pl.BlockSpec((1, 128, 256), lambda i, p: (i, 0, 0))
-    shape = (HALF_Z, 128, 256)
-    count = len(through)
+    rows = pl.ds(pl.multiple_of(i * 128, 128), 128)
+    for r, u in enumerate((u0, u1, u2, u3)):
+        u[rows, :] = added[lax.rem(own + r, 4)].astype(u.dtype)
+
+    @pl.when(i == 0)
+    def _():
+        ends = split_count(total[...])
+        for u in (u0, u1, u2, u3):
+            u[HALF_Z * 128 :, :] = ends.astype(u.dtype)
+
+
+def first_sum(place, total, parts):
+    four = pl.BlockSpec((4, 1, 128, 256), lambda i: (0, i, 0, 0))
+    low = pl.BlockSpec((2, 1, 128, 256), lambda i: (0, i, 0, 0))
+    high = pl.BlockSpec((2, 1, 128, 256), lambda i: (1, i, 0, 0))
+    vmem = pl.BlockSpec(memory_space=pltpu.VMEM)
+    shape = (HALF_Z * 128 + 16, 256)
     return pl.pallas_call(
         first_sum_kernel,
-        grid_spec=pltpu.PrefetchScalarGridSpec(
-            num_scalar_prefetch=1,
-            grid=(HALF_Z,),
-            in_specs=[four, high, high, low, low] + [ANYWHERE] * count,
-            out_specs=[out] * 4 + [ANYWHERE] * count,
-            scratch_shapes=[pltpu.VMEM((4, 128, 256), F32)],
-        ),
-        out_shape=[jax.ShapeDtypeStruct(shape, F32)]
-        + [jax.ShapeDtypeStruct(shape, BF16)] * 3
-        + [like(a) for a in through],
-        input_output_aliases={6 + k: 4 + k for k in range(count)},
+        grid=(HALF_Z,),
+        in_specs=[SMEM, vmem, four, high, high, low, low],
+        out_specs=[vmem] * 4,
+        out_shape=[jax.ShapeDtypeStruct(shape, F32)] + [jax.ShapeDtypeStruct(shape, BF16)] * 3,
+        scratch_shapes=[pltpu.VMEM((4, 128, 256), F32)],
         compiler_params=params(8),
         cost_estimate=pl.CostEstimate(flops=1 << 20, bytes_accessed=4 << 20, transcendentals=0),
-    )(place, *parts, *through)
-
-
-def second_sum_kernel(place, total, a, b, c, d, dep, *rest):
+    )(place, total, *parts)
+
+
+def second_sum_kernel(a, b, c, d, dep, *rest):
     count = (len(rest) - 4) // 2
-    high = jnp.floor(total[...] * (1 / 256))
-    ends = jnp.concatenate([high, total[...] - 256 * high], axis=0).astype(BF16)
+    ends = HALF_Z * 128
+
+    def added(rows):
+        return (a[rows, :] + b[rows, :].astype(F32)) + (c[rows, :].astype(F32) + d[rows, :].astype(F32))
+
+    counts = added(slice(ends, ends + 16))
+    counts = split_count(256 * counts[0:8] + counts[8:16])
     for k, v in enumerate(rest[count : count + 4]):
-        added = (a[k] + b[k].astype(F32)) + (c[k].astype(F32) + d[k].astype(F32))
-        v[0:128, :] = added.astype(v.dtype)
-        v[128:144, :] = ends
-
-
-def second_sum(place, total, parts, dep, *through):
+        v[0:128, :] = added(slice(k * 128, (k + 1) * 128)).astype(v.dtype)
+        v[128:144, :] = counts.astype(v.dtype)
+
+
+def second_sum(parts, dep, *through):
     count = len(through)
     shape = jax.ShapeDtypeStruct((144, 256), BF16)
     return pl.pallas_call(
         second_sum_kernel,
         grid=(1,),
-        in_specs=[SMEM, whole(total)] + [whole(a) for a in parts] + [ANYWHERE] * (1 + count),
+        in_specs=[whole(a) for a in parts] + [ANYWHERE] * (1 + count),
         out_specs=[whole(shape)] * 4 + [ANYWHERE] * count,
         out_shape=[shape] * 4 + [like(a) for a in through],
-        input_output_aliases={7 + k: 4 + k for k in range(count)},
+        input_output_aliases={5 + k: 4 + k for k in range(count)},
         compiler_params=params(8),
         cost_estimate=pl.CostEstimate(flops=1 << 19, bytes_accessed=1 << 20, transcendentals=0),
-    )(place, total, *parts, dep, *through)
+    )(*parts, dep, *through)
 
 
 def third_sum_kernel(a, b, c, d, *rest):
@@ -503,20 +511,20 @@
     ring1 = hop(chunk, around)
     from_minus, from_plus = hop(plus, s_moves(1)), hop(minus, s_moves(-1))
     total = filled + other_filled
-    total = total + hop(total, lambda z, x, y, c: (z, x, y + 1, c))
-    s1, s3, ring1, total = relay(s1, s3, from_minus, from_plus, ring1, total)
+    total = total + hop(total, s_moves(1))
+    ring1, from_minus, from_plus, total = after(ring1, from_minus, from_plus, total)
+    s1, s3 = relay(s1, s3, from_minus, from_plus)
 
     ring2, ring1_other = hop(ring1, around), swap(ring1)
-    first = (s0, from_minus, from_plus, hop(s1, s_moves(1)), hop(s3, s_moves(-1)))
-    total = total + hop(total, lambda z, x, y, c: (z, x + 1, y, c))
-    total = total + hop(total, lambda z, x, y, c: (z, x, y + 2, c))
-    u0, u1, u2, u3, ring2, ring1_other, total = first_sum(place, first, ring2, ring1_other, total)
+    late_minus, late_plus = hop(s1, s_moves(1)), hop(s3, s_moves(-1))
+    total = total + hop(total, s_moves(2))
+    ring2, ring1_other, late_minus, late_plus, total = after(ring2, ring1_other, late_minus, late_plus, total)
+    u0, u1, u2, u3 = first_sum(place, total, (s0, from_minus, from_plus, late_minus, late_plus))
 
     ring3, ring2_other = hop(ring2, around), swap(ring2)
     second = [u0] + [hop(u, u_moves(r)) for r, u in ((1, u1), (2, u2), (3, u3))]
-    total = total + hop(total, lambda z, x, y, c: (z, x + 2, y, c))
     raw = products(grads, (chunk, ring1, ring1_other, ring2, ring2_other))
-    *sends, ring3 = second_sum(place, total, second, raw, ring3)
+    *sends, ring3 = second_sum(second, raw, ring3)
 
     half = NX * rows // 2
     last = lax.dynamic_slice(ring3, (c * half, 0), (half, width))

time: 109 us -> 107 us (0.982)
  starting transfers between devices: 50.1 us -> 45.4 us
  waiting for transfers between devices: 33.1 us -> 36.1 us
    ppermute x34 -> x32, starting transfers between devices: 50.1 us -> 45.4 us  [hop(): return lax.ppermute(array, ('dp', 'group'), pairs)]
    ppermute x34 -> x32, waiting for transfers between devices: 33.1 us -> 36.1 us  [hop(): return lax.ppermute(array, ('dp', 'group'), pairs)]
  transfers between devices with their start and end apart: 34 -> 32, of which waited for: 13 -> 14; matrix products, arithmetic and copies ran while one was open for 2% -> 2% of each run, Pallas kernels for 11% -> 13%
where the time goes in v4:
time: 107 us; the launch traced here: 106 us
  starting transfers between devices  45.4 us (42%)
  waiting for transfers between devices  36.1 us (34%)
  Pallas kernels  16.3 us (15%)
  local copies, waits for them, and re-layouts  5.94 us (6%)
  between operations  1.77 us (2%)
    ppermute x32, starting transfers between devices, hop(): return lax.ppermute(array, ('dp', 'group'), pairs)  45.4 us
    ppermute x32, waiting for transfers between devices, hop(): return lax.ppermute(array, ('dp', 'group'), pairs)  36.1 us
    unnamed x9, local copies, waits for them, and re-layouts  5.77 us
    pallas_call x1, Pallas kernels, partials(): pl.pallas_call(other_kernel, grid=(HALF_Z,), in_specs=[SMEM, vmem, vmem,...  4.18 us
    pallas_call x1, Pallas kernels, scaled(): pl.pallas_call(functools.partial(scaled_kernel, (*raw_distances, *distanc...  2.72 us
    pallas_call x1, Pallas kernels, own_partials(): pl.pallas_call(own_kernel, grid=(HALF_Z,), in_specs=[SMEM, vmem, vmem, HB...  2.65 us
  transfers between devices with their start and end apart: 32, of which 14 were waited for; matrix products, arithmetic and copies ran while one was open for 2% of the time, Pallas kernels for 13%

profile of v4, /device:TPU:1, one launch (start us, length us, event | category | flops | bytes accessed | tf_op | source)
XLA Modules:
  0.0 106.4 jit_solution(5675979247161893070)
XLA Ops:
  0.6 3.3 %collective-permute-start.5 = (bf16[256,8192]{1,0:T(8,128)(2,1)}, bf16[256,8192]{1,0:T(8,128)(2,1)}, u32[]{:S(2)}, u32[]{:S(2)}) collective-permute-start(bf16[256,8192]{1,0:T(8,128)(2,1)} %source.1), channel_id=1, source_target_pairs={{0,1},{1,0},{2,3},{3,2},{4,5},{5,4},{6,7},{7,6},{8,9},{9,8},{10,11... | collective-permute-start | bytes 12582920 | tf_op jit(solution)/shard_map/ppermute | solution.py:31
  4.6 0.1 collective-permute-start.3
  4.7 0.8 collective-permute-start
  5.5 1.1 %copy.28 = bf16[256,512]{0,1:T(8,128)(2,1)S(1)} copy(bf16[256,512]{1,0:T(8,128)(2,1)} %param.6) | data formatting | bytes 524288 | tf_op args[1]
  6.6 0.7 compare_and_fusion
  7.3 0.1 collective-permute-start.4
  7.5 0.1 copy.29.grads
  7.7 2.8 %collective-permute-done.near = bf16[256,512]{1,0:T(8,128)(2,1)S(1)} collective-permute-done((bf16[256,512]{1,0:T(8,128)(2,1)}, bf16[256,512]{1,0:T(8,128)(2,1)S(1)}, u32[]{:S(2)}, u32[]{:S(2)}) %collective-permute-start) | collective-permute-done | bytes 262176 | tf_op jit(solution)/shard_map/ppermute | solution.py:31
  10.5 2.5 %collective-permute-start.1 = (bf16[256,512]{1,0:T(8,128)(2,1)S(1)}, bf16[256,512]{1,0:T(8,128)(2,1)S(1)}, u32[]{:S(2)}, u32[]{:S(2)}) collective-permute-start(bf16[256,512]{1,0:T(8,128)(2,1)S(1)} %collective-permute-done.near), channel_id=1, source_target_pairs={{0,1},{1,0},{2,3},{3,2},{4,5},{5,4},{6,7},{7,6},{8,9},{9,8},{10,11... | collective-permute-start | bytes 786440 | tf_op jit(solution)/shard_map/ppermute | solution.py:31
  13.0 0.1 pad_add_fusion.place
  13.1 2.2 %copy-done.2 = bf16[256,8192]{1,0:T(8,128)(2,1)S(1)} copy-done((bf16[256,8192]{1,0:T(8,128)(2,1)S(1)}, bf16[256,8192]{1,0:T(8,128)(2,1)}, u32[]{:S(2)}) %copy-start.2) | copy-done | bytes 4194328
  15.3 2.6 %shard_map.68 = (f32[4,4,512,256]{3,2,1,0:T(8,128)S(1)}, bf16[256,512]{1,0:T(8,128)(2,1)S(1)}) custom-call(s32[4]{0:T(128)S(1)} %pad_add_fusion.place, f32[8,256]{1,0:T(8,128)S(1)} %broadcast_in_dim.15.number.filled, bf16[512,256]{1,0:T(8,128)(2,1)S(1)} %fusion.1.gradient, bf16[256,8192]{1,0:T(8,128)(2,1)S(1)} %copy-done.2, ...), custom_call_target="tpu_custom_call", output_to_operand_aliasing={{1}: (4, {})} | custom-call | flops 1073741824 | bytes 4194304 | tf_op jit(solution)/shard_map/pallas_call | solution.py:161
  17.9 0.0 collective-permute-done.4.gradient
  18.0 0.0 collective-permute-done.5.source
  18.0 0.0 copy-start.3
  18.0 4.2 %shard_map.69 = (bf16[4,4,128,256]{3,2,1,0:T(8,128)(2,1)S(1)}, bf16[4,4,128,256]{3,2,1,0:T(8,128)(2,1)S(1)}, bf16[4,4,128,256]{3,2,1,0:T(8,128)(2,1)S(1)}, bf16[...) custom-call(s32[4]{0:T(128)S(1)} %pad_add_fusion.place, f32[8,256]{1,0:T(8,128)S(1)} %collective-permute-done.3.number, ...), custom_call_target="tpu_custom_call" | custom-call | flops 1073741824 | bytes 8388608 | tf_op jit(solution)/shard_map/pallas_call | solution.py:178
  22.2 0.0 collective-permute-done.1.near_other
  22.2 0.0 collective-permute-done.2.far
  22.2 0.6 shard_map.70.refs_0_
  22.8 5.2 %collective-permute-start.6 = (bf16[1040,512]{1,0:T(8,128)(2,1)S(1)}, bf16[1040,512]{1,0:T(8,128)(2,1)S(1)}, u32[]{:S(2)}, u32[]{:S(2)}) collective-permute-start(bf16[1040,512]{1,0:T(8,128)(2,1)S(1)} %shard_map.70.refs_0_), channel_id=1, source_target_pairs={{0,32},{1,225},{2,34},{3,227},{4,36},{5,229},{6,38},{7,231},{8,40}... | collective-permute-start | bytes 3194888 | tf_op jit(solution)/shard_map/ppermute | solution.py:31
  28.0 0.2 collective-permute-start.7
  28.2 2.5 %collective-permute-start.8 = (bf16[4,4,128,256]{3,2,1,0:T(8,128)(2,1)S(1)}, bf16[4,4,128,256]{3,2,1,0:T(8,128)(2,1)S(1)}, u32[]{:S(2)}, u32[]{:S(2)}) collective-permute-start(bf16[4,4,128,256]{3,2,1,0:T(8,128)(2,1)S(1)} %get-tuple-element.44), channel_id=1, source_target_pairs={{0,6},{1,25},{2,0},{3,27},{4,2},{5,29},{6,4},{7,31},{8,14},{9,1},{... | collective-permute-start | bytes 3145736 | tf_op jit(solution)/shard_map/ppermute | solution.py:31
  30.7 0.0 collective-permute-start.9
  30.7 12.3 %collective-permute-done.9 = f32[8,256]{1,0:T(8,128)S(1)} collective-permute-done((f32[8,256]{1,0:T(8,128)S(1)}, f32[8,256]{1,0:T(8,128)S(1)}, u32[]{:S(2)}, u32[]{:S(2)}) %collective-permute-start.9) | collective-permute-done | bytes 8224 | tf_op jit(solution)/shard_map/ppermute | solution.py:31
  43.0 0.8 collective-permute-start.10
  43.8 0.0 collective-permute-start.11
  43.8 0.5 shard_map.72
  44.4 0.1 collective-permute-start.12
  44.4 2.7 %collective-permute-start.13 = (bf16[2,4,128,256]{3,2,1,0:T(8,128)(2,1)S(1)}, bf16[2,4,128,256]{3,2,1,0:T(8,128)(2,1)S(1)}, u32[]{:S(2)}, u32[]{:S(2)}) collective-permute-start(bf16[2,4,128,256]{3,2,1,0:T(8,128)(2,1)S(1)} %get-tuple-element.51), channel_id=1, source_target_pairs={{0,6},{1,25},{2,0},{3,27},{4,2},{5,29},{6,4},{7,31},{8,14},{9,1},{... | collective-permute-start | bytes 1572872 | tf_op jit(solution)/shard_map/ppermute | solution.py:31
  47.1 1.0 collective-permute-start.14
  48.1 6.6 %collective-permute-done.14 = f32[8,256]{1,0:T(8,128)S(1)} collective-permute-done((f32[8,256]{1,0:T(8,128)S(1)}, f32[8,256]{1,0:T(8,128)S(1)}, u32[]{:S(2)}, u32[]{:S(2)}) %collective-permute-start.14) | collective-permute-done | bytes 8224 | tf_op jit(solution)/shard_map/ppermute | solution.py:31
  54.8 2.1 %collective-permute-done.10.refs_0_ = bf16[1040,512]{1,0:T(8,128)(2,1)S(1)} collective-permute-done((bf16[1040,512]{1,0:T(8,128)(2,1)S(1)}, bf16[1040,512]{1,0:T(8,128)(2,1)S(1)}, u32[]{:S(2)}, u32[]{:S(2)}) %collective-permute-start.10) | collective-permute-done | bytes 1064992 | tf_op jit(solution)/shard_map/ppermute | solution.py:31
  56.9 2.0 %collective-permute-start.19 = (bf16[1040,512]{1,0:T(8,128)(2,1)S(1)}, bf16[1040,512]{1,0:T(8,128)(2,1)S(1)}, u32[]{:S(2)}, u32[]{:S(2)}) collective-permute-start(bf16[1040,512]{1,0:T(8,128)(2,1)S(1)} %get-tuple-element.62.refs_3_), channel_id=1, source_target_pairs={{0,32},{1,225},{2,34},{3,227},{4,36},{5,229},{6,38},{7,231},{8,40}... | collective-permute-start | bytes 3194888 | tf_op jit(solution)/shard_map/ppermute | solution.py:31
  58.9 1.4 %shard_map.74 = (f32[528,256]{1,0:T(8,128)S(1)}, bf16[528,256]{1,0:T(8,128)(2,1)S(1)}, bf16[528,256]{1,0:T(8,128)(2,1)S(1)}, bf16[528,256]{1,0:T(8,128)(2,1)S(1)}) custom-call(s32[4]{0:T(128)S(1)} %pad_add_fusion.place, f32[8,256]{1,0:T(8,128)S(1)} %get-tuple-element.53.total, bf16[4,4,128,256]{3,2,1,0:T(8,128)(2,1)S(1)} %get-tuple-element.42.rest_0_.s0, ...), custom_call_target="tpu_custom_call" | custom-call | flops 1048576 | bytes 4194304 | tf_op jit(solution)/shard_map/pallas_call | solution.py:239
  60.3 1.4 %collective-permute-start.15 = (bf16[528,256]{1,0:T(8,128)(2,1)S(1)}, bf16[528,256]{1,0:T(8,128)(2,1)S(1)}, u32[]{:S(2)}, u32[]{:S(2)}) collective-permute-start(bf16[528,256]{1,0:T(8,128)(2,1)S(1)} %get-tuple-element.57), channel_id=1, source_target_pairs={{0,8},{1,3},{2,10},{3,5},{4,12},{5,7},{6,14},{7,1},{8,16},{9,11},{... | collective-permute-start | bytes 811016 | tf_op jit(solution)/shard_map/ppermute | solution.py:31
  61.7 2.6 %collective-permute-start.16 = (bf16[528,256]{1,0:T(8,128)(2,1)S(1)}, bf16[528,256]{1,0:T(8,128)(2,1)S(1)}, u32[]{:S(2)}, u32[]{:S(2)}) collective-permute-start(bf16[528,256]{1,0:T(8,128)(2,1)S(1)} %get-tuple-element.58), channel_id=1, source_target_pairs={{0,16},{1,5},{2,18},{3,7},{4,20},{5,1},{6,22},{7,3},{8,24},{9,13},... | collective-permute-start | bytes 811016 | tf_op jit(solution)/shard_map/ppermute | solution.py:31
  64.3 1.1 %collective-permute-start.17 = (bf16[528,256]{1,0:T(8,128)(2,1)S(1)}, bf16[528,256]{1,0:T(8,128)(2,1)S(1)}, u32[]{:S(2)}, u32[]{:S(2)}) collective-permute-start(bf16[528,256]{1,0:T(8,128)(2,1)S(1)} %get-tuple-element.59), channel_id=1, source_target_pairs={{0,24},{1,7},{2,26},{3,1},{4,28},{5,3},{6,30},{7,5},{8,0},{9,15},{... | collective-permute-start | bytes 811016 | tf_op jit(solution)/shard_map/ppermute | solution.py:31
  65.3 1.6 %shard_map.75.dep.raw = f32[10,256,512]{2,1,0:T(8,128)S(1)} custom-call(bf16[256,512]{1,0:T(8,128)(2,1)S(1)} %get-tuple-element.60.grads, bf16[1040,512]{1,0:T(8,128)(2,1)S(1)} %shard_map.70.refs_0_, bf16[1040,512]{1,0:T(8,128)(2,1)S(1)} %get-tuple-element.45.refs_1_, bf16[1040,512]{1,0:T(8,128)(2,1)S(1)} %get-tuple-element.61.refs_2_, ...), custom_call_target="tpu_custom_call" | custom-call | flops 1342177280 | bytes 10485760 | tf_op jit(solution)/shard_map/pallas_call | solution.py:381
  66.9 0.3 collective-permute-done.15.b
  67.2 3.8 %collective-permute-done.16.c = bf16[528,256]{1,0:T(8,128)(2,1)S(1)} collective-permute-done((bf16[528,256]{1,0:T(8,128)(2,1)S(1)}, bf16[528,256]{1,0:T(8,128)(2,1)S(1)}, u32[]{:S(2)}, u32[]{:S(2)}) %collective-permute-start.16) | collective-permute-done | bytes 270368 | tf_op jit(solution)/shard_map/ppermute | solution.py:31
  71.0 0.1 collective-permute-done.19.rest_0_
  71.1 0.1 shard_map.76
  71.2 2.6 %collective-permute-start.24 = (bf16[1040,512]{1,0:T(8,128)(2,1)S(1)}, bf16[1040,512]{1,0:T(8,128)(2,1)S(1)}, u32[]{:S(2)}, u32[]{:S(2)}) collective-permute-start(bf16[1040,512]{1,0:T(8,128)(2,1)S(1)} %get-tuple-element.67.rest_1_), channel_id=1, source_target_pairs={{0,1},{1,0},{2,3},{3,2},{4,5},{5,4},{6,7},{7,6},{8,9},{9,8},{10,11... | collective-permute-start | bytes 3194888 | tf_op jit(solution)/shard_map/ppermute | solution.py:31
  73.8 6.5 %collective-permute-start.20 = (bf16[144,256]{1,0:T(8,128)(2,1)S(1)}, bf16[144,256]{1,0:T(8,128)(2,1)S(1)}, u32[]{:S(2)}, u32[]{:S(2)}) collective-permute-start(bf16[144,256]{1,0:T(8,128)(2,1)S(1)} %get-tuple-element.63), channel_id=1, source_target_pairs={{0,0},{1,129},{2,2},{3,131},{4,4},{5,133},{6,6},{7,135},{8,8},{9,1... | collective-permute-start | bytes 221192 | tf_op jit(solution)/shard_map/ppermute | solution.py:31
  80.3 0.1 collective-permute-start.21
  80.4 0.1 collective-permute-start.22
  80.5 2.2 %collective-permute-start.23 = (bf16[144,256]{1,0:T(8,128)(2,1)S(1)}, bf16[144,256]{1,0:T(8,128)(2,1)S(1)}, u32[]{:S(2)}, u32[]{:S(2)}) collective-permute-start(bf16[144,256]{1,0:T(8,128)(2,1)S(1)} %get-tuple-element.66), channel_id=1, source_target_pairs={{0,96},{1,161},{2,98},{3,163},{4,100},{5,165},{6,102},{7,167},{8,1... | collective-permute-start | bytes 221192 | tf_op jit(solution)/shard_map/ppermute | solution.py:31
  82.8 0.2 collective-permute-done.20.a
  83.0 0.6 collective-permute-done.21.b
  83.6 1.1 %collective-permute-done.22.c = bf16[144,256]{1,0:T(8,128)(2,1)S(1)} collective-permute-done((bf16[144,256]{1,0:T(8,128)(2,1)S(1)}, bf16[144,256]{1,0:T(8,128)(2,1)S(1)}, u32[]{:S(2)}, u32[]{:S(2)}) %collective-permute-start.22) | collective-permute-done | bytes 73760 | tf_op jit(solution)/shard_map/ppermute | solution.py:31
  84.7 3.3 %collective-permute-done.23.d = bf16[144,256]{1,0:T(8,128)(2,1)S(1)} collective-permute-done((bf16[144,256]{1,0:T(8,128)(2,1)S(1)}, bf16[144,256]{1,0:T(8,128)(2,1)S(1)}, u32[]{:S(2)}, u32[]{:S(2)}) %collective-permute-start.23) | collective-permute-done | bytes 73760 | tf_op jit(solution)/shard_map/ppermute | solution.py:31
  88.0 0.9 collective-permute-start.28
  88.9 1.4 %collective-permute-done.25.other = f32[136,256]{1,0:T(8,128)S(1)} collective-permute-done((f32[136,256]{1,0:T(8,128)S(1)}, f32[136,256]{1,0:T(8,128)S(1)}, u32[]{:S(2)}, u32[]{:S(2)}) %collective-permute-start.25) | collective-permute-done | bytes 139296 | tf_op jit(solution)/shard_map/ppermute | solution.py:31
  90.3 0.6 shard_map.78
  90.8 4.4 %collective-permute-start.26 = (f32[136,256]{1,0:T(8,128)S(1)}, f32[136,256]{1,0:T(8,128)S(1)}, u32[]{:S(2)}, u32[]{:S(2)}) collective-permute-start(f32[136,256]{1,0:T(8,128)S(1)} %get-tuple-element.69.total.own), channel_id=1, source_target_pairs={{0,2},{1,7},{2,4},{3,1},{4,6},{5,3},{6,0},{7,5},{8,10},{9,15},{10,... | collective-permute-start | bytes 417800 | tf_op jit(solution)/shard_map/ppermute | solution.py:31
  95.2 0.3 collective-permute-start.27
  95.5 2.5 %copy-done.1 = f32[10,256,512]{2,1,0:T(8,128)S(1)} copy-done((f32[10,256,512]{2,1,0:T(8,128)S(1)}, f32[10,256,512]{2,1,0:T(8,128)}, u32[]{:S(2)}) %copy-start.1) | copy-done | bytes 5242904
  97.9 2.7 %shard_map.79.refs_3_ = bf16[256,8192]{1,0:T(8,128)(2,1)} custom-call(s32[4]{0:T(128)S(1)} %pad_add_fusion.place, f32[8,256]{1,0:T(8,128)S(1)} %broadcast_in_dim.15.number.filled, f32[136,256]{1,0:T(8,128)S(1)} %get-tuple-element.69.total.own, bf16[256,512]{1,0:T(8,128)(2,1)S(1)} %get-tuple-element.60.grads, f32[10,256,512]{2,1,0:T(8,128)S(1)} %copy-done.1, ...), custom_call_target="tpu_custom_call" | custom-call | flops 1835008 | bytes 11010048 | tf_op jit(solution)/shard_map/pallas_call | solution.py:421
  100.7 0.2 collective-permute-done.27.refs_1_
  100.8 1.6 %collective-permute-start.31 = (bf16[512,512]{1,0:T(8,128)(2,1)S(1)}, bf16[512,512]{1,0:T(8,128)(2,1)S(1)}, u32[]{:S(2)}, u32[]{:S(2)}) collective-permute-start(bf16[512,512]{1,0:T(8,128)(2,1)S(1)} %get-tuple-element.76.last), channel_id=1, source_target_pairs={{0,1},{1,0},{2,3},{3,2},{4,5},{5,4},{6,7},{7,6},{8,9},{9,8},{10,11... | collective-permute-start | bytes 1572872 | tf_op jit(solution)/shard_map/ppermute | solution.py:31
  102.4 0.1 collective-permute-start.29
  102.5 0.4 collective-permute-start.30
  102.9 1.3 %collective-permute-done.30.far_other = f32[64,256]{1,0:T(8,128)S(1)} collective-permute-done((f32[64,256]{1,0:T(8,128)S(1)}, f32[64,256]{1,0:T(8,128)S(1)}, u32[]{:S(2)}, u32[]{:S(2)}) %collective-permute-start.30) | collective-permute-done | bytes 65568 | tf_op jit(solution)/shard_map/ppermute | solution.py:31
  104.3 1.9 %shard_map.81 = (f32[256,512]{1,0:T(8,128)}, bf16[256,8192]{1,0:T(8,128)(2,1)}) custom-call(s32[4]{0:T(128)S(1)} %pad_add_fusion.place, f32[8,256]{1,0:T(8,128)S(1)} %broadcast_in_dim.15.number.filled, f32[136,256]{1,0:T(8,128)S(1)} %get-tuple-element.69.total.own, f32[136,256]{1,0:T(8,128)S(1)} %get-tuple-element.74.near, ...), custom_call_target="tpu_custom_call", output_to_operand_aliasing={{1}: (10, {})} | custom-call | flops 268435456 | bytes 3145728 | tf_op jit(solution)/shard_map/pallas_call | solution.py:468
  (33 shorter events, 0.2 us)
Async XLA Ops:
  0.6 17.3 %collective-permute-start.5 = (bf16[256,8192]{1,0:T(8,128)(2,1)}, bf16[256,8192]{1,0:T(8,128)(2,1)}, u32[]{:S(2)}, u32[]{:S(2)}) collective-permute-start(bf16[256,8192]{1,0:T(8,128)(2,1)} %source.1), channel_id=1, source_target_pairs={{0,1},{1,0},{2,3},{3,2},{4,5},{5,4},{6,7},{7,6},{8,9},{9,8},{10,11... | collective-permute-start | bytes 12582920 | tf_op jit(solution)/shard_map/ppermute | solution.py:31
  4.6 13.3 %collective-permute-start.3 = (f32[8,256]{1,0:T(8,128)S(1)}, f32[8,256]{1,0:T(8,128)S(1)}, u32[]{:S(2)}, u32[]{:S(2)}) collective-permute-start(f32[8,256]{1,0:T(8,128)S(1)} %broadcast_in_dim.15.number.filled), channel_id=1, source_target_pairs={{0,1},{1,0},{2,3},{3,2},{4,5},{5,4},{6,7},{7,6},{8,9},{9,8},{10,11... | collective-permute-start | bytes 24584 | tf_op jit(solution)/shard_map/ppermute | solution.py:31
  4.7 5.8 %collective-permute-start = (bf16[256,512]{1,0:T(8,128)(2,1)}, bf16[256,512]{1,0:T(8,128)(2,1)S(1)}, u32[]{:S(2)}, u32[]{:S(2)}) collective-permute-start(bf16[256,512]{1,0:T(8,128)(2,1)} %own.1), channel_id=1, source_target_pairs={{0,8},{1,25},{2,10},{3,27},{4,12},{5,29},{6,14},{7,31},{8,16},{9,1... | collective-permute-start | bytes 786440 | tf_op jit(solution)/shard_map/ppermute | solution.py:31
  7.3 10.6 %collective-permute-start.4 = (bf16[512,256]{1,0:T(8,128)(2,1)S(1)}, bf16[512,256]{1,0:T(8,128)(2,1)S(1)}, u32[]{:S(2)}, u32[]{:S(2)}) collective-permute-start(bf16[512,256]{1,0:T(8,128)(2,1)S(1)} %fusion.1.gradient), channel_id=1, source_target_pairs={{0,1},{1,0},{2,3},{3,2},{4,5},{5,4},{6,7},{7,6},{8,9},{9,8},{10,11... | collective-permute-start | bytes 786440 | tf_op jit(solution)/shard_map/ppermute | solution.py:31
  10.5 11.6 %collective-permute-start.1 = (bf16[256,512]{1,0:T(8,128)(2,1)S(1)}, bf16[256,512]{1,0:T(8,128)(2,1)S(1)}, u32[]{:S(2)}, u32[]{:S(2)}) collective-permute-start(bf16[256,512]{1,0:T(8,128)(2,1)S(1)} %collective-permute-done.near), channel_id=1, source_target_pairs={{0,1},{1,0},{2,3},{3,2},{4,5},{5,4},{6,7},{7,6},{8,9},{9,8},{10,11... | collective-permute-start | bytes 786440 | tf_op jit(solution)/shard_map/ppermute | solution.py:31
  13.0 9.2 %collective-permute-start.2 = (bf16[256,512]{1,0:T(8,128)(2,1)S(1)}, bf16[256,512]{1,0:T(8,128)(2,1)S(1)}, u32[]{:S(2)}, u32[]{:S(2)}) collective-permute-start(bf16[256,512]{1,0:T(8,128)(2,1)S(1)} %collective-permute-done.near), channel_id=1, source_target_pairs={{0,8},{1,25},{2,10},{3,27},{4,12},{5,29},{6,14},{7,31},{8,16},{9,1... | collective-permute-start | bytes 786440 | tf_op jit(solution)/shard_map/ppermute | solution.py:31
  13.1 2.2 %copy-start.2 = (bf16[256,8192]{1,0:T(8,128)(2,1)S(1)}, bf16[256,8192]{1,0:T(8,128)(2,1)}, u32[]{:S(2)}) copy-start(bf16[256,8192]{1,0:T(8,128)(2,1)} %source.1) | copy-start | bytes 12582916
  18.0 4.2 %copy-start.3 = (bf16[256,512]{1,0:T(8,128)(2,1)S(1)}, bf16[256,512]{1,0:T(8,128)(2,1)}, u32[]{:S(2)}) copy-start(bf16[256,512]{1,0:T(8,128)(2,1)} %own.1) | copy-start | bytes 786436
  22.8 20.1 %collective-permute-start.6 = (bf16[1040,512]{1,0:T(8,128)(2,1)S(1)}, bf16[1040,512]{1,0:T(8,128)(2,1)S(1)}, u32[]{:S(2)}, u32[]{:S(2)}) collective-permute-start(bf16[1040,512]{1,0:T(8,128)(2,1)S(1)} %shard_map.70.refs_0_), channel_id=1, source_target_pairs={{0,32},{1,225},{2,34},{3,227},{4,36},{5,229},{6,38},{7,231},{8,40}... | collective-permute-start | bytes 3194888 | tf_op jit(solution)/shard_map/ppermute | solution.py:31
  28.0 15.0 %collective-permute-start.7 = (bf16[4,4,128,256]{3,2,1,0:T(8,128)(2,1)S(1)}, bf16[4,4,128,256]{3,2,1,0:T(8,128)(2,1)S(1)}, u32[]{:S(2)}, u32[]{:S(2)}) collective-permute-start(bf16[4,4,128,256]{3,2,1,0:T(8,128)(2,1)S(1)} %get-tuple-element.43), channel_id=1, source_target_pairs={{0,2},{1,9},{2,4},{3,11},{4,6},{5,13},{6,0},{7,15},{8,10},{9,17},{... | collective-permute-start | bytes 3145736 | tf_op jit(solution)/shard_map/ppermute | solution.py:31
  28.2 14.8 %collective-permute-start.8 = (bf16[4,4,128,256]{3,2,1,0:T(8,128)(2,1)S(1)}, bf16[4,4,128,256]{3,2,1,0:T(8,128)(2,1)S(1)}, u32[]{:S(2)}, u32[]{:S(2)}) collective-permute-start(bf16[4,4,128,256]{3,2,1,0:T(8,128)(2,1)S(1)} %get-tuple-element.44), channel_id=1, source_target_pairs={{0,6},{1,25},{2,0},{3,27},{4,2},{5,29},{6,4},{7,31},{8,14},{9,1},{... | collective-permute-start | bytes 3145736 | tf_op jit(solution)/shard_map/ppermute | solution.py:31
  30.7 12.3 %collective-permute-start.9 = (f32[8,256]{1,0:T(8,128)S(1)}, f32[8,256]{1,0:T(8,128)S(1)}, u32[]{:S(2)}, u32[]{:S(2)}) collective-permute-start(f32[8,256]{1,0:T(8,128)S(1)} %broadcast_add_fusion), channel_id=1, source_target_pairs={{0,2},{1,9},{2,4},{3,11},{4,6},{5,13},{6,0},{7,15},{8,10},{9,17},{... | collective-permute-start | bytes 24584 | tf_op jit(solution)/shard_map/ppermute | solution.py:31
  43.0 13.9 %collective-permute-start.10 = (bf16[1040,512]{1,0:T(8,128)(2,1)S(1)}, bf16[1040,512]{1,0:T(8,128)(2,1)S(1)}, u32[]{:S(2)}, u32[]{:S(2)}) collective-permute-start(bf16[1040,512]{1,0:T(8,128)(2,1)S(1)} %get-tuple-element.45.refs_1_), channel_id=1, source_target_pairs={{0,32},{1,225},{2,34},{3,227},{4,36},{5,229},{6,38},{7,231},{8,40}... | collective-permute-start | bytes 3194888 | tf_op jit(solution)/shard_map/ppermute | solution.py:31
  43.8 13.1 %collective-permute-start.11 = (bf16[1040,512]{1,0:T(8,128)(2,1)S(1)}, bf16[1040,512]{1,0:T(8,128)(2,1)S(1)}, u32[]{:S(2)}, u32[]{:S(2)}) collective-permute-start(bf16[1040,512]{1,0:T(8,128)(2,1)S(1)} %get-tuple-element.45.refs_1_), channel_id=1, source_target_pairs={{0,1},{1,0},{2,3},{3,2},{4,5},{5,4},{6,7},{7,6},{8,9},{9,8},{10,11... | collective-permute-start | bytes 3194888 | tf_op jit(solution)/shard_map/ppermute | solution.py:31
  44.4 10.4 %collective-permute-start.12 = (bf16[2,4,128,256]{3,2,1,0:T(8,128)(2,1)S(1)}, bf16[2,4,128,256]{3,2,1,0:T(8,128)(2,1)S(1)}, u32[]{:S(2)}, u32[]{:S(2)}) collective-permute-start(bf16[2,4,128,256]{3,2,1,0:T(8,128)(2,1)S(1)} %get-tuple-element.50), channel_id=1, source_target_pairs={{0,2},{1,9},{2,4},{3,11},{4,6},{5,13},{6,0},{7,15},{8,10},{9,17},{... | collective-permute-start | bytes 1572872 | tf_op jit(solution)/shard_map/ppermute | solution.py:31
  44.4 10.3 %collective-permute-start.13 = (bf16[2,4,128,256]{3,2,1,0:T(8,128)(2,1)S(1)}, bf16[2,4,128,256]{3,2,1,0:T(8,128)(2,1)S(1)}, u32[]{:S(2)}, u32[]{:S(2)}) collective-permute-start(bf16[2,4,128,256]{3,2,1,0:T(8,128)(2,1)S(1)} %get-tuple-element.51), channel_id=1, source_target_pairs={{0,6},{1,25},{2,0},{3,27},{4,2},{5,29},{6,4},{7,31},{8,14},{9,1},{... | collective-permute-start | bytes 1572872 | tf_op jit(solution)/shard_map/ppermute | solution.py:31
  47.1 7.6 %collective-permute-start.14 = (f32[8,256]{1,0:T(8,128)S(1)}, f32[8,256]{1,0:T(8,128)S(1)}, u32[]{:S(2)}, u32[]{:S(2)}) collective-permute-start(f32[8,256]{1,0:T(8,128)S(1)} %get-tuple-element.52), channel_id=1, source_target_pairs={{0,4},{1,17},{2,6},{3,19},{4,0},{5,21},{6,2},{7,23},{8,12},{9,25},... | collective-permute-start | bytes 24584 | tf_op jit(solution)/shard_map/ppermute | solution.py:31
  56.9 8.5 %collective-permute-start.18 = (bf16[1040,512]{1,0:T(8,128)(2,1)S(1)}, bf16[1040,512]{1,0:T(8,128)(2,1)S(1)}, u32[]{:S(2)}, u32[]{:S(2)}) collective-permute-start(bf16[1040,512]{1,0:T(8,128)(2,1)S(1)} %get-tuple-element.62.refs_3_), channel_id=1, source_target_pairs={{0,1},{1,0},{2,3},{3,2},{4,5},{5,4},{6,7},{7,6},{8,9},{9,8},{10,11... | collective-permute-start | bytes 3194888 | tf_op jit(solution)/shard_map/ppermute | solution.py:31
  56.9 14.2 %collective-permute-start.19 = (bf16[1040,512]{1,0:T(8,128)(2,1)S(1)}, bf16[1040,512]{1,0:T(8,128)(2,1)S(1)}, u32[]{:S(2)}, u32[]{:S(2)}) collective-permute-start(bf16[1040,512]{1,0:T(8,128)(2,1)S(1)} %get-tuple-element.62.refs_3_), channel_id=1, source_target_pairs={{0,32},{1,225},{2,34},{3,227},{4,36},{5,229},{6,38},{7,231},{8,40}... | collective-permute-start | bytes 3194888 | tf_op jit(solution)/shard_map/ppermute | solution.py:31
  60.3 7.0 %collective-permute-start.15 = (bf16[528,256]{1,0:T(8,128)(2,1)S(1)}, bf16[528,256]{1,0:T(8,128)(2,1)S(1)}, u32[]{:S(2)}, u32[]{:S(2)}) collective-permute-start(bf16[528,256]{1,0:T(8,128)(2,1)S(1)} %get-tuple-element.57), channel_id=1, source_target_pairs={{0,8},{1,3},{2,10},{3,5},{4,12},{5,7},{6,14},{7,1},{8,16},{9,11},{... | collective-permute-start | bytes 811016 | tf_op jit(solution)/shard_map/ppermute | solution.py:31
  61.7 9.4 %collective-permute-start.16 = (bf16[528,256]{1,0:T(8,128)(2,1)S(1)}, bf16[528,256]{1,0:T(8,128)(2,1)S(1)}, u32[]{:S(2)}, u32[]{:S(2)}) collective-permute-start(bf16[528,256]{1,0:T(8,128)(2,1)S(1)} %get-tuple-element.58), channel_id=1, source_target_pairs={{0,16},{1,5},{2,18},{3,7},{4,20},{5,1},{6,22},{7,3},{8,24},{9,13},... | collective-permute-start | bytes 811016 | tf_op jit(solution)/shard_map/ppermute | solution.py:31
  64.3 6.7 %collective-permute-start.17 = (bf16[528,256]{1,0:T(8,128)(2,1)S(1)}, bf16[528,256]{1,0:T(8,128)(2,1)S(1)}, u32[]{:S(2)}, u32[]{:S(2)}) collective-permute-start(bf16[528,256]{1,0:T(8,128)(2,1)S(1)} %get-tuple-element.59), channel_id=1, source_target_pairs={{0,24},{1,7},{2,26},{3,1},{4,28},{5,3},{6,30},{7,5},{8,0},{9,15},{... | collective-permute-start | bytes 811016 | tf_op jit(solution)/shard_map/ppermute | solution.py:31
  66.9 4.3 %copy-start = (f32[10,256,512]{2,1,0:T(8,128)}, f32[10,256,512]{2,1,0:T(8,128)S(1)}, u32[]{:S(2)}) copy-start(f32[10,256,512]{2,1,0:T(8,128)S(1)} %shard_map.75.dep.raw) | copy-start | bytes 15728644
  71.2 16.7 %collective-permute-start.24 = (bf16[1040,512]{1,0:T(8,128)(2,1)S(1)}, bf16[1040,512]{1,0:T(8,128)(2,1)S(1)}, u32[]{:S(2)}, u32[]{:S(2)}) collective-permute-start(bf16[1040,512]{1,0:T(8,128)(2,1)S(1)} %get-tuple-element.67.rest_1_), channel_id=1, source_target_pairs={{0,1},{1,0},{2,3},{3,2},{4,5},{5,4},{6,7},{7,6},{8,9},{9,8},{10,11... | collective-permute-start | bytes 3194888 | tf_op jit(solution)/shard_map/ppermute | solution.py:31
  73.8 9.1 %collective-permute-start.20 = (bf16[144,256]{1,0:T(8,128)(2,1)S(1)}, bf16[144,256]{1,0:T(8,128)(2,1)S(1)}, u32[]{:S(2)}, u32[]{:S(2)}) collective-permute-start(bf16[144,256]{1,0:T(8,128)(2,1)S(1)} %get-tuple-element.63), channel_id=1, source_target_pairs={{0,0},{1,129},{2,2},{3,131},{4,4},{5,133},{6,6},{7,135},{8,8},{9,1... | collective-permute-start | bytes 221192 | tf_op jit(solution)/shard_map/ppermute | solution.py:31
  80.3 3.3 %collective-permute-start.21 = (bf16[144,256]{1,0:T(8,128)(2,1)S(1)}, bf16[144,256]{1,0:T(8,128)(2,1)S(1)}, u32[]{:S(2)}, u32[]{:S(2)}) collective-permute-start(bf16[144,256]{1,0:T(8,128)(2,1)S(1)} %get-tuple-element.64), channel_id=1, source_target_pairs={{0,32},{1,225},{2,34},{3,227},{4,36},{5,229},{6,38},{7,231},{8,40}... | collective-permute-start | bytes 221192 | tf_op jit(solution)/shard_map/ppermute | solution.py:31
  80.4 4.3 %collective-permute-start.22 = (bf16[144,256]{1,0:T(8,128)(2,1)S(1)}, bf16[144,256]{1,0:T(8,128)(2,1)S(1)}, u32[]{:S(2)}, u32[]{:S(2)}) collective-permute-start(bf16[144,256]{1,0:T(8,128)(2,1)S(1)} %get-tuple-element.65), channel_id=1, source_target_pairs={{0,64},{1,193},{2,66},{3,195},{4,68},{5,197},{6,70},{7,199},{8,72}... | collective-permute-start | bytes 221192 | tf_op jit(solution)/shard_map/ppermute | solution.py:31
  80.5 7.5 %collective-permute-start.23 = (bf16[144,256]{1,0:T(8,128)(2,1)S(1)}, bf16[144,256]{1,0:T(8,128)(2,1)S(1)}, u32[]{:S(2)}, u32[]{:S(2)}) collective-permute-start(bf16[144,256]{1,0:T(8,128)(2,1)S(1)} %get-tuple-element.66), channel_id=1, source_target_pairs={{0,96},{1,161},{2,98},{3,163},{4,100},{5,165},{6,102},{7,167},{8,1... | collective-permute-start | bytes 221192 | tf_op jit(solution)/shard_map/ppermute | solution.py:31
  88.0 12.8 %collective-permute-start.28 = (bf16[512,512]{1,0:T(8,128)(2,1)S(1)}, bf16[512,512]{1,0:T(8,128)(2,1)S(1)}, u32[]{:S(2)}, u32[]{:S(2)}) collective-permute-start(bf16[512,512]{1,0:T(8,128)(2,1)S(1)} %get-tuple-element.71), channel_id=1, source_target_pairs={{0,32},{1,225},{2,34},{3,227},{4,36},{5,229},{6,38},{7,231},{8,40}... | collective-permute-start | bytes 1572872 | tf_op jit(solution)/shard_map/ppermute | solution.py:31
  88.9 1.4 %collective-permute-start.25 = (f32[136,256]{1,0:T(8,128)S(1)}, f32[136,256]{1,0:T(8,128)S(1)}, u32[]{:S(2)}, u32[]{:S(2)}) collective-permute-start(f32[136,256]{1,0:T(8,128)S(1)} %get-tuple-element.68.own), channel_id=1, source_target_pairs={{0,1},{1,0},{2,3},{3,2},{4,5},{5,4},{6,7},{7,6},{8,9},{9,8},{10,11... | collective-permute-start | bytes 417800 | tf_op jit(solution)/shard_map/ppermute | solution.py:31
  90.8 10.0 %collective-permute-start.26 = (f32[136,256]{1,0:T(8,128)S(1)}, f32[136,256]{1,0:T(8,128)S(1)}, u32[]{:S(2)}, u32[]{:S(2)}) collective-permute-start(f32[136,256]{1,0:T(8,128)S(1)} %get-tuple-element.69.total.own), channel_id=1, source_target_pairs={{0,2},{1,7},{2,4},{3,1},{4,6},{5,3},{6,0},{7,5},{8,10},{9,15},{10,... | collective-permute-start | bytes 417800 | tf_op jit(solution)/shard_map/ppermute | solution.py:31
  95.2 5.6 %collective-permute-start.27 = (f32[64,256]{1,0:T(8,128)S(1)}, f32[64,256]{1,0:T(8,128)S(1)}, u32[]{:S(2)}, u32[]{:S(2)}) collective-permute-start(f32[64,256]{1,0:T(8,128)S(1)} %get-tuple-element.70), channel_id=1, source_target_pairs={{0,4},{1,5},{2,6},{3,7},{4,0},{5,1},{6,2},{7,3},{8,12},{9,13},{10,... | collective-permute-start | bytes 196616 | tf_op jit(solution)/shard_map/ppermute | solution.py:31
  95.5 2.5 %copy-start.1 = (f32[10,256,512]{2,1,0:T(8,128)S(1)}, f32[10,256,512]{2,1,0:T(8,128)}, u32[]{:S(2)}) copy-start(f32[10,256,512]{2,1,0:T(8,128)} %copy-done) | copy-start | bytes 15728644
  100.8 3.4 %collective-permute-start.31 = (bf16[512,512]{1,0:T(8,128)(2,1)S(1)}, bf16[512,512]{1,0:T(8,128)(2,1)S(1)}, u32[]{:S(2)}, u32[]{:S(2)}) collective-permute-start(bf16[512,512]{1,0:T(8,128)(2,1)S(1)} %get-tuple-element.76.last), channel_id=1, source_target_pairs={{0,1},{1,0},{2,3},{3,2},{4,5},{5,4},{6,7},{7,6},{8,9},{9,8},{10,11... | collective-permute-start | bytes 1572872 | tf_op jit(solution)/shard_map/ppermute | solution.py:31
  102.4 1.8 %collective-permute-start.29 = (f32[136,256]{1,0:T(8,128)S(1)}, f32[136,256]{1,0:T(8,128)S(1)}, u32[]{:S(2)}, u32[]{:S(2)}) collective-permute-start(f32[136,256]{1,0:T(8,128)S(1)} %get-tuple-element.74.near), channel_id=1, source_target_pairs={{0,1},{1,0},{2,3},{3,2},{4,5},{5,4},{6,7},{7,6},{8,9},{9,8},{10,11... | collective-permute-start | bytes 417800 | tf_op jit(solution)/shard_map/ppermute | solution.py:31
  102.5 1.7 %collective-permute-start.30 = (f32[64,256]{1,0:T(8,128)S(1)}, f32[64,256]{1,0:T(8,128)S(1)}, u32[]{:S(2)}, u32[]{:S(2)}) collective-permute-start(f32[64,256]{1,0:T(8,128)S(1)} %get-tuple-element.75.far), channel_id=1, source_target_pairs={{0,1},{1,0},{2,3},{3,2},{4,5},{5,4},{6,7},{7,6},{8,9},{9,8},{10,11... | collective-permute-start | bytes 196616 | tf_op jit(solution)/shard_map/ppermute | solution.py:31

commit v5 on v4

--- a/solution.py
+++ b/solution.py
@@ -371,7 +371,7 @@
     chunks, out = refs[:-1], refs[-1]
     for k, chunk in enumerate(chunks):
         for n in range(2):
-            out[2 * k + n] = nt_dot(grads[...], chunk[n * SPAN : (n + 1) * SPAN, :])
+            out[2 * k + n] = nt_dot(grads[...], chunk[n * SPAN : (n + 1) * SPAN, :]).astype(BF16)
 
 
 def products(grads, chunks):
@@ -382,10 +382,10 @@
         products_kernel,
         in_specs=[vmem] * (1 + len(chunks)),
         out_specs=vmem,
-        out_shape=jax.ShapeDtypeStruct((pieces, tokens, SPAN), F32),
+        out_shape=jax.ShapeDtypeStruct((pieces, tokens, SPAN), BF16),
         compiler_params=params(16),
         cost_estimate=pl.CostEstimate(
-            flops=2 * tokens * width * SPAN * pieces, bytes_accessed=pieces << 20, transcendentals=0
+            flops=2 * tokens * width * SPAN * pieces, bytes_accessed=pieces * 3 << 18, transcendentals=0
         ),
     )(grads, *chunks)
 
@@ -403,7 +403,7 @@
     stores = []
     for n in range(made.shape[0]):
         if n < count:
-            piece = raw[n]
+            piece = raw[n].astype(F32)
         else:
             k, at = divmod(n - count, 2)
             piece = nt_dot(grads[...], chunks[k][at * SPAN : (at + 1) * SPAN, :])

time: 107 us -> 106 us (level)
  local copies, waits for them, and re-layouts: 5.94 us -> 4.49 us
  Pallas kernels: 16.3 us -> 17.4 us
    unnamed x9 -> x5, local copies, waits for them, and re-layouts: 5.77 us -> 3.28 us
  transfers between devices with their start and end apart: 32 -> 32, of which waited for: 14 -> 12; matrix products, arithmetic and copies ran while one was open for 2% -> 3% of each run, Pallas kernels for 13% -> 14%
where the time goes in v5:
time: 106 us
  starting transfers between devices  45.4 us (43%)
  waiting for transfers between devices  35.8 us (34%)
  Pallas kernels  17.4 us (16%)
  local copies, waits for them, and re-layouts  4.49 us (4%)
  between operations  1.77 us (2%)
    ppermute x32, starting transfers between devices, hop(): return lax.ppermute(array, ('dp', 'group'), pairs)  45.4 us
    ppermute x32, waiting for transfers between devices, hop(): return lax.ppermute(array, ('dp', 'group'), pairs)  35.8 us
    pallas_call x1, Pallas kernels, partials(): pl.pallas_call(other_kernel, grid=(HALF_Z,), in_specs=[SMEM, vmem, vmem,...  4.18 us
    pallas_call x1, Pallas kernels, scaled(): pl.pallas_call(functools.partial(scaled_kernel, (*raw_distances, *distanc...  3.78 us
    unnamed x5, local copies, waits for them, and re-layouts  3.28 us
    pallas_call x1, Pallas kernels, own_partials(): pl.pallas_call(own_kernel, grid=(HALF_Z,), in_specs=[SMEM, vmem, vmem, HB...  2.65 us
  transfers between devices with their start and end apart: 32, of which 12 were waited for; matrix products, arithmetic and copies ran while one was open for 3% of the time, Pallas kernels for 14%

profile of v5, /device:TPU:1, one launch (start us, length us, event | category | flops | bytes accessed | tf_op | source)
XLA Modules:
  0.0 105.6 jit_solution(17851445747258565317)
XLA Ops:
  0.6 3.3 %collective-permute-start.5 = (bf16[256,8192]{1,0:T(8,128)(2,1)}, bf16[256,8192]{1,0:T(8,128)(2,1)}, u32[]{:S(2)}, u32[]{:S(2)}) collective-permute-start(bf16[256,8192]{1,0:T(8,128)(2,1)} %source.1), channel_id=1, source_target_pairs={{0,1},{1,0},{2,3},{3,2},{4,5},{5,4},{6,7},{7,6},{8,9},{9,8},{10,11... | collective-permute-start | bytes 12582920 | tf_op jit(solution)/shard_map/ppermute | solution.py:31
  4.6 0.1 collective-permute-start.3
  4.7 0.8 collective-permute-start
  5.5 1.1 %copy.28 = bf16[256,512]{0,1:T(8,128)(2,1)S(1)} copy(bf16[256,512]{1,0:T(8,128)(2,1)} %param.6) | data formatting | bytes 524288 | tf_op args[1]
  6.6 0.7 compare_and_fusion
  7.3 0.1 collective-permute-start.4
  7.5 0.1 copy.29.grads
  7.7 2.8 %collective-permute-done.near = bf16[256,512]{1,0:T(8,128)(2,1)S(1)} collective-permute-done((bf16[256,512]{1,0:T(8,128)(2,1)}, bf16[256,512]{1,0:T(8,128)(2,1)S(1)}, u32[]{:S(2)}, u32[]{:S(2)}) %collective-permute-start) | collective-permute-done | bytes 262176 | tf_op jit(solution)/shard_map/ppermute | solution.py:31
  10.5 2.5 %collective-permute-start.1 = (bf16[256,512]{1,0:T(8,128)(2,1)S(1)}, bf16[256,512]{1,0:T(8,128)(2,1)S(1)}, u32[]{:S(2)}, u32[]{:S(2)}) collective-permute-start(bf16[256,512]{1,0:T(8,128)(2,1)S(1)} %collective-permute-done.near), channel_id=1, source_target_pairs={{0,1},{1,0},{2,3},{3,2},{4,5},{5,4},{6,7},{7,6},{8,9},{9,8},{10,11... | collective-permute-start | bytes 786440 | tf_op jit(solution)/shard_map/ppermute | solution.py:31
  13.0 0.1 pad_add_fusion.place
  13.1 2.2 %copy-done = bf16[256,8192]{1,0:T(8,128)(2,1)S(1)} copy-done((bf16[256,8192]{1,0:T(8,128)(2,1)S(1)}, bf16[256,8192]{1,0:T(8,128)(2,1)}, u32[]{:S(2)}) %copy-start) | copy-done | bytes 4194328
  15.3 2.6 %shard_map.68 = (f32[4,4,512,256]{3,2,1,0:T(8,128)S(1)}, bf16[256,512]{1,0:T(8,128)(2,1)S(1)}) custom-call(s32[4]{0:T(128)S(1)} %pad_add_fusion.place, f32[8,256]{1,0:T(8,128)S(1)} %broadcast_in_dim.15.number.filled, bf16[512,256]{1,0:T(8,128)(2,1)S(1)} %fusion.1.gradient, bf16[256,8192]{1,0:T(8,128)(2,1)S(1)} %copy-done, ...), custom_call_target="tpu_custom_call", output_to_operand_aliasing={{1}: (4, {})} | custom-call | flops 1073741824 | bytes 4194304 | tf_op jit(solution)/shard_map/pallas_call | solution.py:161
  17.9 0.0 collective-permute-done.4.gradient
  18.0 0.0 collective-permute-done.5.source
  18.0 0.0 copy-start.1
  18.0 4.2 %shard_map.69 = (bf16[4,4,128,256]{3,2,1,0:T(8,128)(2,1)S(1)}, bf16[4,4,128,256]{3,2,1,0:T(8,128)(2,1)S(1)}, bf16[4,4,128,256]{3,2,1,0:T(8,128)(2,1)S(1)}, bf16[...) custom-call(s32[4]{0:T(128)S(1)} %pad_add_fusion.place, f32[8,256]{1,0:T(8,128)S(1)} %collective-permute-done.3.number, ...), custom_call_target="tpu_custom_call" | custom-call | flops 1073741824 | bytes 8388608 | tf_op jit(solution)/shard_map/pallas_call | solution.py:178
  22.2 0.0 collective-permute-done.1.near_other
  22.2 0.0 collective-permute-done.2.far
  22.2 0.6 shard_map.70.refs_0_
  22.8 5.2 %collective-permute-start.6 = (bf16[1040,512]{1,0:T(8,128)(2,1)S(1)}, bf16[1040,512]{1,0:T(8,128)(2,1)S(1)}, u32[]{:S(2)}, u32[]{:S(2)}) collective-permute-start(bf16[1040,512]{1,0:T(8,128)(2,1)S(1)} %shard_map.70.refs_0_), channel_id=1, source_target_pairs={{0,32},{1,225},{2,34},{3,227},{4,36},{5,229},{6,38},{7,231},{8,40}... | collective-permute-start | bytes 3194888 | tf_op jit(solution)/shard_map/ppermute | solution.py:31
  28.0 0.2 collective-permute-start.7
  28.2 2.5 %collective-permute-start.8 = (bf16[4,4,128,256]{3,2,1,0:T(8,128)(2,1)S(1)}, bf16[4,4,128,256]{3,2,1,0:T(8,128)(2,1)S(1)}, u32[]{:S(2)}, u32[]{:S(2)}) collective-permute-start(bf16[4,4,128,256]{3,2,1,0:T(8,128)(2,1)S(1)} %get-tuple-element.44), channel_id=1, source_target_pairs={{0,6},{1,25},{2,0},{3,27},{4,2},{5,29},{6,4},{7,31},{8,14},{9,1},{... | collective-permute-start | bytes 3145736 | tf_op jit(solution)/shard_map/ppermute | solution.py:31
  30.7 12.3 %collective-permute-done.9 = f32[8,256]{1,0:T(8,128)S(1)} collective-permute-done((f32[8,256]{1,0:T(8,128)S(1)}, f32[8,256]{1,0:T(8,128)S(1)}, u32[]{:S(2)}, u32[]{:S(2)}) %collective-permute-start.9) | collective-permute-done | bytes 8224 | tf_op jit(solution)/shard_map/ppermute | solution.py:31
  43.0 0.8 collective-permute-start.10
  43.8 0.5 shard_map.72
  44.4 0.1 collective-permute-start.12
  44.4 2.7 %collective-permute-start.13 = (bf16[2,4,128,256]{3,2,1,0:T(8,128)(2,1)S(1)}, bf16[2,4,128,256]{3,2,1,0:T(8,128)(2,1)S(1)}, u32[]{:S(2)}, u32[]{:S(2)}) collective-permute-start(bf16[2,4,128,256]{3,2,1,0:T(8,128)(2,1)S(1)} %get-tuple-element.51), channel_id=1, source_target_pairs={{0,6},{1,25},{2,0},{3,27},{4,2},{5,29},{6,4},{7,31},{8,14},{9,1},{... | collective-permute-start | bytes 1572872 | tf_op jit(solution)/shard_map/ppermute | solution.py:31
  47.1 1.0 collective-permute-start.14
  48.1 6.6 %collective-permute-done.14 = f32[8,256]{1,0:T(8,128)S(1)} collective-permute-done((f32[8,256]{1,0:T(8,128)S(1)}, f32[8,256]{1,0:T(8,128)S(1)}, u32[]{:S(2)}, u32[]{:S(2)}) %collective-permute-start.14) | collective-permute-done | bytes 8224 | tf_op jit(solution)/shard_map/ppermute | solution.py:31
  54.8 0.0 collective-permute-done.12.refs_2_
  54.8 0.0 collective-permute-done.13.refs_3_
  54.8 2.1 %collective-permute-done.10.refs_0_ = bf16[1040,512]{1,0:T(8,128)(2,1)S(1)} collective-permute-done((bf16[1040,512]{1,0:T(8,128)(2,1)S(1)}, bf16[1040,512]{1,0:T(8,128)(2,1)S(1)}, u32[]{:S(2)}, u32[]{:S(2)}) %collective-permute-start.10) | collective-permute-done | bytes 1064992 | tf_op jit(solution)/shard_map/ppermute | solution.py:31
  56.9 0.0 collective-permute-start.18
  56.9 2.0 %collective-permute-start.19 = (bf16[1040,512]{1,0:T(8,128)(2,1)S(1)}, bf16[1040,512]{1,0:T(8,128)(2,1)}, u32[]{:S(2)}, u32[]{:S(2)}) collective-permute-start(bf16[1040,512]{1,0:T(8,128)(2,1)S(1)} %get-tuple-element.62.refs_3_), channel_id=1, source_target_pairs={{0,32},{1,225},{2,34},{3,227},{4,36},{5,229},{6,38},{7,231},{8,40}... | collective-permute-start | bytes 3194888 | tf_op jit(solution)/shard_map/ppermute | solution.py:31
  58.9 1.4 %shard_map.74 = (f32[528,256]{1,0:T(8,128)S(1)}, bf16[528,256]{1,0:T(8,128)(2,1)S(1)}, bf16[528,256]{1,0:T(8,128)(2,1)S(1)}, bf16[528,256]{1,0:T(8,128)(2,1)S(1)}) custom-call(s32[4]{0:T(128)S(1)} %pad_add_fusion.place, f32[8,256]{1,0:T(8,128)S(1)} %get-tuple-element.53.total, bf16[4,4,128,256]{3,2,1,0:T(8,128)(2,1)S(1)} %get-tuple-element.42.rest_0_.s0, ...), custom_call_target="tpu_custom_call" | custom-call | flops 1048576 | bytes 4194304 | tf_op jit(solution)/shard_map/pallas_call | solution.py:239
  60.3 1.4 %collective-permute-start.15 = (bf16[528,256]{1,0:T(8,128)(2,1)S(1)}, bf16[528,256]{1,0:T(8,128)(2,1)S(1)}, u32[]{:S(2)}, u32[]{:S(2)}) collective-permute-start(bf16[528,256]{1,0:T(8,128)(2,1)S(1)} %get-tuple-element.57), channel_id=1, source_target_pairs={{0,8},{1,3},{2,10},{3,5},{4,12},{5,7},{6,14},{7,1},{8,16},{9,11},{... | collective-permute-start | bytes 811016 | tf_op jit(solution)/shard_map/ppermute | solution.py:31
  61.7 2.6 %collective-permute-start.16 = (bf16[528,256]{1,0:T(8,128)(2,1)S(1)}, bf16[528,256]{1,0:T(8,128)(2,1)S(1)}, u32[]{:S(2)}, u32[]{:S(2)}) collective-permute-start(bf16[528,256]{1,0:T(8,128)(2,1)S(1)} %get-tuple-element.58), channel_id=1, source_target_pairs={{0,16},{1,5},{2,18},{3,7},{4,20},{5,1},{6,22},{7,3},{8,24},{9,13},... | collective-permute-start | bytes 811016 | tf_op jit(solution)/shard_map/ppermute | solution.py:31
  64.3 1.1 %collective-permute-start.17 = (bf16[528,256]{1,0:T(8,128)(2,1)S(1)}, bf16[528,256]{1,0:T(8,128)(2,1)S(1)}, u32[]{:S(2)}, u32[]{:S(2)}) collective-permute-start(bf16[528,256]{1,0:T(8,128)(2,1)S(1)} %get-tuple-element.59), channel_id=1, source_target_pairs={{0,24},{1,7},{2,26},{3,1},{4,28},{5,3},{6,30},{7,5},{8,0},{9,15},{... | collective-permute-start | bytes 811016 | tf_op jit(solution)/shard_map/ppermute | solution.py:31
  65.3 1.6 %shard_map.75.dep.raw = bf16[10,256,512]{2,1,0:T(8,128)(2,1)S(1)} custom-call(bf16[256,512]{1,0:T(8,128)(2,1)S(1)} %get-tuple-element.60.grads, bf16[1040,512]{1,0:T(8,128)(2,1)S(1)} %shard_map.70.refs_0_, bf16[1040,512]{1,0:T(8,128)(2,1)S(1)} %get-tuple-element.45.refs_1_, bf16[1040,512]{1,0:T(8,128)(2,1)S(1)} %get-tuple-element.61.refs_2_, ...), custom_call_target="tpu_custom_call" | custom-call | flops 1342177280 | bytes 7864320 | tf_op jit(solution)/shard_map/pallas_call | solution.py:381
  66.9 0.4 collective-permute-done.15.b
  67.3 3.7 %collective-permute-done.16.c = bf16[528,256]{1,0:T(8,128)(2,1)S(1)} collective-permute-done((bf16[528,256]{1,0:T(8,128)(2,1)S(1)}, bf16[528,256]{1,0:T(8,128)(2,1)S(1)}, u32[]{:S(2)}, u32[]{:S(2)}) %collective-permute-start.16) | collective-permute-done | bytes 270368 | tf_op jit(solution)/shard_map/ppermute | solution.py:31
  71.0 0.2 collective-permute-done.19.rest_0_
  71.2 0.1 shard_map.76
  71.3 2.6 %collective-permute-start.24 = (bf16[1040,512]{1,0:T(8,128)(2,1)}, bf16[1040,512]{1,0:T(8,128)(2,1)}, u32[]{:S(2)}, u32[]{:S(2)}) collective-permute-start(bf16[1040,512]{1,0:T(8,128)(2,1)} %get-tuple-element.67.rest_1_), channel_id=1, source_target_pairs={{0,1},{1,0},{2,3},{3,2},{4,5},{5,4},{6,7},{7,6},{8,9},{9,8},{10,11... | collective-permute-start | bytes 3194888 | tf_op jit(solution)/shard_map/ppermute | solution.py:31
  73.9 6.5 %collective-permute-start.20 = (bf16[144,256]{1,0:T(8,128)(2,1)S(1)}, bf16[144,256]{1,0:T(8,128)(2,1)S(1)}, u32[]{:S(2)}, u32[]{:S(2)}) collective-permute-start(bf16[144,256]{1,0:T(8,128)(2,1)S(1)} %get-tuple-element.63), channel_id=1, source_target_pairs={{0,0},{1,129},{2,2},{3,131},{4,4},{5,133},{6,6},{7,135},{8,8},{9,1... | collective-permute-start | bytes 221192 | tf_op jit(solution)/shard_map/ppermute | solution.py:31
  80.4 0.1 collective-permute-start.21
  80.5 0.1 collective-permute-start.22
  80.6 2.2 %collective-permute-start.23 = (bf16[144,256]{1,0:T(8,128)(2,1)S(1)}, bf16[144,256]{1,0:T(8,128)(2,1)S(1)}, u32[]{:S(2)}, u32[]{:S(2)}) collective-permute-start(bf16[144,256]{1,0:T(8,128)(2,1)S(1)} %get-tuple-element.66), channel_id=1, source_target_pairs={{0,96},{1,161},{2,98},{3,163},{4,100},{5,165},{6,102},{7,167},{8,1... | collective-permute-start | bytes 221192 | tf_op jit(solution)/shard_map/ppermute | solution.py:31
  82.8 1.1 %constant_dynamic-slice_fusion.rest_0_ = bf16[512,512]{1,0:T(8,128)(2,1)S(1)} fusion(bf16[1040,512]{1,0:T(8,128)(2,1)} %get-tuple-element.67.rest_1_, s32[]{:T(128)S(6)} %select_n.30), kind=kLoop, calls=%fused_computation.4 | loop fusion | bytes 1048580 | tf_op jit(solution)/shard_map/dynamic_slice | solution.py:530
  83.9 0.9 collective-permute-done.22.c
  84.8 2.5 %collective-permute-done.23.d = bf16[144,256]{1,0:T(8,128)(2,1)S(1)} collective-permute-done((bf16[144,256]{1,0:T(8,128)(2,1)S(1)}, bf16[144,256]{1,0:T(8,128)(2,1)S(1)}, u32[]{:S(2)}, u32[]{:S(2)}) %collective-permute-start.23) | collective-permute-done | bytes 73760 | tf_op jit(solution)/shard_map/ppermute | solution.py:31
  87.3 1.6 %collective-permute-start.28 = (bf16[512,512]{1,0:T(8,128)(2,1)S(1)}, bf16[512,512]{1,0:T(8,128)(2,1)S(1)}, u32[]{:S(2)}, u32[]{:S(2)}) collective-permute-start(bf16[512,512]{1,0:T(8,128)(2,1)S(1)} %get-tuple-element.71), channel_id=1, source_target_pairs={{0,32},{1,225},{2,34},{3,227},{4,36},{5,229},{6,38},{7,231},{8,40}... | collective-permute-start | bytes 1572872 | tf_op jit(solution)/shard_map/ppermute | solution.py:31
  88.9 0.0 collective-permute-start.25
  88.9 1.4 %collective-permute-done.25.other = f32[136,256]{1,0:T(8,128)S(1)} collective-permute-done((f32[136,256]{1,0:T(8,128)S(1)}, f32[136,256]{1,0:T(8,128)S(1)}, u32[]{:S(2)}, u32[]{:S(2)}) %collective-permute-start.25) | collective-permute-done | bytes 139296 | tf_op jit(solution)/shard_map/ppermute | solution.py:31
  90.3 0.6 shard_map.78
  90.9 4.4 %collective-permute-start.26 = (f32[136,256]{1,0:T(8,128)S(1)}, f32[136,256]{1,0:T(8,128)S(1)}, u32[]{:S(2)}, u32[]{:S(2)}) collective-permute-start(f32[136,256]{1,0:T(8,128)S(1)} %get-tuple-element.69.total.own), channel_id=1, source_target_pairs={{0,2},{1,7},{2,4},{3,1},{4,6},{5,3},{6,0},{7,5},{8,10},{9,15},{10,... | collective-permute-start | bytes 417800 | tf_op jit(solution)/shard_map/ppermute | solution.py:31
  95.3 0.3 collective-permute-start.27
  95.6 3.8 %shard_map.79.refs_3_ = bf16[256,8192]{1,0:T(8,128)(2,1)} custom-call(s32[4]{0:T(128)S(1)} %pad_add_fusion.place, f32[8,256]{1,0:T(8,128)S(1)} %broadcast_in_dim.15.number.filled, f32[136,256]{1,0:T(8,128)S(1)} %get-tuple-element.69.total.own, bf16[256,512]{1,0:T(8,128)(2,1)S(1)} %get-tuple-element.60.grads, bf16[10,256,512]{2,1,0:T(8,128)(2,1)S(1)} %shard_map.75.dep.raw, ...), custom_call_target="tpu_custom_call" | custom-call | flops 1835008 | bytes 11010048 | tf_op jit(solution)/shard_map/pallas_call | solution.py:421
  99.3 1.6 %collective-permute-done.27.refs_1_ = f32[64,256]{1,0:T(8,128)S(1)} collective-permute-done((f32[64,256]{1,0:T(8,128)S(1)}, f32[64,256]{1,0:T(8,128)S(1)}, u32[]{:S(2)}, u32[]{:S(2)}) %collective-permute-start.27) | collective-permute-done | bytes 65568 | tf_op jit(solution)/shard_map/ppermute | solution.py:31
  100.9 0.8 collective-permute-start.31
  101.7 0.1 collective-permute-start.29
  101.8 0.4 collective-permute-start.30
  102.2 1.3 %collective-permute-done.30.far_other = f32[64,256]{1,0:T(8,128)S(1)} collective-permute-done((f32[64,256]{1,0:T(8,128)S(1)}, f32[64,256]{1,0:T(8,128)S(1)}, u32[]{:S(2)}, u32[]{:S(2)}) %collective-permute-start.30) | collective-permute-done | bytes 65568 | tf_op jit(solution)/shard_map/ppermute | solution.py:31
  103.5 1.9 %shard_map.81 = (f32[256,512]{1,0:T(8,128)}, bf16[256,8192]{1,0:T(8,128)(2,1)}) custom-call(s32[4]{0:T(128)S(1)} %pad_add_fusion.place, f32[8,256]{1,0:T(8,128)S(1)} %broadcast_in_dim.15.number.filled, f32[136,256]{1,0:T(8,128)S(1)} %get-tuple-element.69.total.own, f32[136,256]{1,0:T(8,128)S(1)} %get-tuple-element.74.near, ...), custom_call_target="tpu_custom_call", output_to_operand_aliasing={{1}: (10, {})} | custom-call | flops 268435456 | bytes 3145728 | tf_op jit(solution)/shard_map/pallas_call | solution.py:468
  (29 shorter events, 0.2 us)
Async XLA Ops:
  0.6 17.3 %collective-permute-start.5 = (bf16[256,8192]{1,0:T(8,128)(2,1)}, bf16[256,8192]{1,0:T(8,128)(2,1)}, u32[]{:S(2)}, u32[]{:S(2)}) collective-permute-start(bf16[256,8192]{1,0:T(8,128)(2,1)} %source.1), channel_id=1, source_target_pairs={{0,1},{1,0},{2,3},{3,2},{4,5},{5,4},{6,7},{7,6},{8,9},{9,8},{10,11... | collective-permute-start | bytes 12582920 | tf_op jit(solution)/shard_map/ppermute | solution.py:31
  4.6 13.3 %collective-permute-start.3 = (f32[8,256]{1,0:T(8,128)S(1)}, f32[8,256]{1,0:T(8,128)S(1)}, u32[]{:S(2)}, u32[]{:S(2)}) collective-permute-start(f32[8,256]{1,0:T(8,128)S(1)} %broadcast_in_dim.15.number.filled), channel_id=1, source_target_pairs={{0,1},{1,0},{2,3},{3,2},{4,5},{5,4},{6,7},{7,6},{8,9},{9,8},{10,11... | collective-permute-start | bytes 24584 | tf_op jit(solution)/shard_map/ppermute | solution.py:31
  4.7 5.8 %collective-permute-start = (bf16[256,512]{1,0:T(8,128)(2,1)}, bf16[256,512]{1,0:T(8,128)(2,1)S(1)}, u32[]{:S(2)}, u32[]{:S(2)}) collective-permute-start(bf16[256,512]{1,0:T(8,128)(2,1)} %own.1), channel_id=1, source_target_pairs={{0,8},{1,25},{2,10},{3,27},{4,12},{5,29},{6,14},{7,31},{8,16},{9,1... | collective-permute-start | bytes 786440 | tf_op jit(solution)/shard_map/ppermute | solution.py:31
  7.3 10.6 %collective-permute-start.4 = (bf16[512,256]{1,0:T(8,128)(2,1)S(1)}, bf16[512,256]{1,0:T(8,128)(2,1)S(1)}, u32[]{:S(2)}, u32[]{:S(2)}) collective-permute-start(bf16[512,256]{1,0:T(8,128)(2,1)S(1)} %fusion.1.gradient), channel_id=1, source_target_pairs={{0,1},{1,0},{2,3},{3,2},{4,5},{5,4},{6,7},{7,6},{8,9},{9,8},{10,11... | collective-permute-start | bytes 786440 | tf_op jit(solution)/shard_map/ppermute | solution.py:31
  10.5 11.6 %collective-permute-start.1 = (bf16[256,512]{1,0:T(8,128)(2,1)S(1)}, bf16[256,512]{1,0:T(8,128)(2,1)S(1)}, u32[]{:S(2)}, u32[]{:S(2)}) collective-permute-start(bf16[256,512]{1,0:T(8,128)(2,1)S(1)} %collective-permute-done.near), channel_id=1, source_target_pairs={{0,1},{1,0},{2,3},{3,2},{4,5},{5,4},{6,7},{7,6},{8,9},{9,8},{10,11... | collective-permute-start | bytes 786440 | tf_op jit(solution)/shard_map/ppermute | solution.py:31
  13.0 9.2 %collective-permute-start.2 = (bf16[256,512]{1,0:T(8,128)(2,1)S(1)}, bf16[256,512]{1,0:T(8,128)(2,1)S(1)}, u32[]{:S(2)}, u32[]{:S(2)}) collective-permute-start(bf16[256,512]{1,0:T(8,128)(2,1)S(1)} %collective-permute-done.near), channel_id=1, source_target_pairs={{0,8},{1,25},{2,10},{3,27},{4,12},{5,29},{6,14},{7,31},{8,16},{9,1... | collective-permute-start | bytes 786440 | tf_op jit(solution)/shard_map/ppermute | solution.py:31
  13.1 2.2 %copy-start = (bf16[256,8192]{1,0:T(8,128)(2,1)S(1)}, bf16[256,8192]{1,0:T(8,128)(2,1)}, u32[]{:S(2)}) copy-start(bf16[256,8192]{1,0:T(8,128)(2,1)} %source.1) | copy-start | bytes 12582916
  18.0 4.2 %copy-start.1 = (bf16[256,512]{1,0:T(8,128)(2,1)S(1)}, bf16[256,512]{1,0:T(8,128)(2,1)}, u32[]{:S(2)}) copy-start(bf16[256,512]{1,0:T(8,128)(2,1)} %own.1) | copy-start | bytes 786436
  22.8 20.1 %collective-permute-start.6 = (bf16[1040,512]{1,0:T(8,128)(2,1)S(1)}, bf16[1040,512]{1,0:T(8,128)(2,1)S(1)}, u32[]{:S(2)}, u32[]{:S(2)}) collective-permute-start(bf16[1040,512]{1,0:T(8,128)(2,1)S(1)} %shard_map.70.refs_0_), channel_id=1, source_target_pairs={{0,32},{1,225},{2,34},{3,227},{4,36},{5,229},{6,38},{7,231},{8,40}... | collective-permute-start | bytes 3194888 | tf_op jit(solution)/shard_map/ppermute | solution.py:31
  28.0 15.0 %collective-permute-start.7 = (bf16[4,4,128,256]{3,2,1,0:T(8,128)(2,1)S(1)}, bf16[4,4,128,256]{3,2,1,0:T(8,128)(2,1)S(1)}, u32[]{:S(2)}, u32[]{:S(2)}) collective-permute-start(bf16[4,4,128,256]{3,2,1,0:T(8,128)(2,1)S(1)} %get-tuple-element.43), channel_id=1, source_target_pairs={{0,2},{1,9},{2,4},{3,11},{4,6},{5,13},{6,0},{7,15},{8,10},{9,17},{... | collective-permute-start | bytes 3145736 | tf_op jit(solution)/shard_map/ppermute | solution.py:31
  28.2 14.8 %collective-permute-start.8 = (bf16[4,4,128,256]{3,2,1,0:T(8,128)(2,1)S(1)}, bf16[4,4,128,256]{3,2,1,0:T(8,128)(2,1)S(1)}, u32[]{:S(2)}, u32[]{:S(2)}) collective-permute-start(bf16[4,4,128,256]{3,2,1,0:T(8,128)(2,1)S(1)} %get-tuple-element.44), channel_id=1, source_target_pairs={{0,6},{1,25},{2,0},{3,27},{4,2},{5,29},{6,4},{7,31},{8,14},{9,1},{... | collective-permute-start | bytes 3145736 | tf_op jit(solution)/shard_map/ppermute | solution.py:31
  30.7 12.3 %collective-permute-start.9 = (f32[8,256]{1,0:T(8,128)S(1)}, f32[8,256]{1,0:T(8,128)S(1)}, u32[]{:S(2)}, u32[]{:S(2)}) collective-permute-start(f32[8,256]{1,0:T(8,128)S(1)} %broadcast_add_fusion), channel_id=1, source_target_pairs={{0,2},{1,9},{2,4},{3,11},{4,6},{5,13},{6,0},{7,15},{8,10},{9,17},{... | collective-permute-start | bytes 24584 | tf_op jit(solution)/shard_map/ppermute | solution.py:31
  43.0 13.9 %collective-permute-start.10 = (bf16[1040,512]{1,0:T(8,128)(2,1)S(1)}, bf16[1040,512]{1,0:T(8,128)(2,1)S(1)}, u32[]{:S(2)}, u32[]{:S(2)}) collective-permute-start(bf16[1040,512]{1,0:T(8,128)(2,1)S(1)} %get-tuple-element.45.refs_1_), channel_id=1, source_target_pairs={{0,32},{1,225},{2,34},{3,227},{4,36},{5,229},{6,38},{7,231},{8,40}... | collective-permute-start | bytes 3194888 | tf_op jit(solution)/shard_map/ppermute | solution.py:31
  43.8 13.1 %collective-permute-start.11 = (bf16[1040,512]{1,0:T(8,128)(2,1)S(1)}, bf16[1040,512]{1,0:T(8,128)(2,1)S(1)}, u32[]{:S(2)}, u32[]{:S(2)}) collective-permute-start(bf16[1040,512]{1,0:T(8,128)(2,1)S(1)} %get-tuple-element.45.refs_1_), channel_id=1, source_target_pairs={{0,1},{1,0},{2,3},{3,2},{4,5},{5,4},{6,7},{7,6},{8,9},{9,8},{10,11... | collective-permute-start | bytes 3194888 | tf_op jit(solution)/shard_map/ppermute | solution.py:31
  44.4 10.4 %collective-permute-start.12 = (bf16[2,4,128,256]{3,2,1,0:T(8,128)(2,1)S(1)}, bf16[2,4,128,256]{3,2,1,0:T(8,128)(2,1)S(1)}, u32[]{:S(2)}, u32[]{:S(2)}) collective-permute-start(bf16[2,4,128,256]{3,2,1,0:T(8,128)(2,1)S(1)} %get-tuple-element.50), channel_id=1, source_target_pairs={{0,2},{1,9},{2,4},{3,11},{4,6},{5,13},{6,0},{7,15},{8,10},{9,17},{... | collective-permute-start | bytes 1572872 | tf_op jit(solution)/shard_map/ppermute | solution.py:31
  44.4 10.3 %collective-permute-start.13 = (bf16[2,4,128,256]{3,2,1,0:T(8,128)(2,1)S(1)}, bf16[2,4,128,256]{3,2,1,0:T(8,128)(2,1)S(1)}, u32[]{:S(2)}, u32[]{:S(2)}) collective-permute-start(bf16[2,4,128,256]{3,2,1,0:T(8,128)(2,1)S(1)} %get-tuple-element.51), channel_id=1, source_target_pairs={{0,6},{1,25},{2,0},{3,27},{4,2},{5,29},{6,4},{7,31},{8,14},{9,1},{... | collective-permute-start | bytes 1572872 | tf_op jit(solution)/shard_map/ppermute | solution.py:31
  47.1 7.6 %collective-permute-start.14 = (f32[8,256]{1,0:T(8,128)S(1)}, f32[8,256]{1,0:T(8,128)S(1)}, u32[]{:S(2)}, u32[]{:S(2)}) collective-permute-start(f32[8,256]{1,0:T(8,128)S(1)} %get-tuple-element.52), channel_id=1, source_target_pairs={{0,4},{1,17},{2,6},{3,19},{4,0},{5,21},{6,2},{7,23},{8,12},{9,25},... | collective-permute-start | bytes 24584 | tf_op jit(solution)/shard_map/ppermute | solution.py:31
  56.9 8.5 %collective-permute-start.18 = (bf16[1040,512]{1,0:T(8,128)(2,1)S(1)}, bf16[1040,512]{1,0:T(8,128)(2,1)S(1)}, u32[]{:S(2)}, u32[]{:S(2)}) collective-permute-start(bf16[1040,512]{1,0:T(8,128)(2,1)S(1)} %get-tuple-element.62.refs_3_), channel_id=1, source_target_pairs={{0,1},{1,0},{2,3},{3,2},{4,5},{5,4},{6,7},{7,6},{8,9},{9,8},{10,11... | collective-permute-start | bytes 3194888 | tf_op jit(solution)/shard_map/ppermute | solution.py:31
  56.9 14.3 %collective-permute-start.19 = (bf16[1040,512]{1,0:T(8,128)(2,1)S(1)}, bf16[1040,512]{1,0:T(8,128)(2,1)}, u32[]{:S(2)}, u32[]{:S(2)}) collective-permute-start(bf16[1040,512]{1,0:T(8,128)(2,1)S(1)} %get-tuple-element.62.refs_3_), channel_id=1, source_target_pairs={{0,32},{1,225},{2,34},{3,227},{4,36},{5,229},{6,38},{7,231},{8,40}... | collective-permute-start | bytes 3194888 | tf_op jit(solution)/shard_map/ppermute | solution.py:31
  60.3 7.1 %collective-permute-start.15 = (bf16[528,256]{1,0:T(8,128)(2,1)S(1)}, bf16[528,256]{1,0:T(8,128)(2,1)S(1)}, u32[]{:S(2)}, u32[]{:S(2)}) collective-permute-start(bf16[528,256]{1,0:T(8,128)(2,1)S(1)} %get-tuple-element.57), channel_id=1, source_target_pairs={{0,8},{1,3},{2,10},{3,5},{4,12},{5,7},{6,14},{7,1},{8,16},{9,11},{... | collective-permute-start | bytes 811016 | tf_op jit(solution)/shard_map/ppermute | solution.py:31
  61.7 9.4 %collective-permute-start.16 = (bf16[528,256]{1,0:T(8,128)(2,1)S(1)}, bf16[528,256]{1,0:T(8,128)(2,1)S(1)}, u32[]{:S(2)}, u32[]{:S(2)}) collective-permute-start(bf16[528,256]{1,0:T(8,128)(2,1)S(1)} %get-tuple-element.58), channel_id=1, source_target_pairs={{0,16},{1,5},{2,18},{3,7},{4,20},{5,1},{6,22},{7,3},{8,24},{9,13},... | collective-permute-start | bytes 811016 | tf_op jit(solution)/shard_map/ppermute | solution.py:31
  64.3 6.7 %collective-permute-start.17 = (bf16[528,256]{1,0:T(8,128)(2,1)S(1)}, bf16[528,256]{1,0:T(8,128)(2,1)S(1)}, u32[]{:S(2)}, u32[]{:S(2)}) collective-permute-start(bf16[528,256]{1,0:T(8,128)(2,1)S(1)} %get-tuple-element.59), channel_id=1, source_target_pairs={{0,24},{1,7},{2,26},{3,1},{4,28},{5,3},{6,30},{7,5},{8,0},{9,15},{... | collective-permute-start | bytes 811016 | tf_op jit(solution)/shard_map/ppermute | solution.py:31
  71.3 15.9 %collective-permute-start.24 = (bf16[1040,512]{1,0:T(8,128)(2,1)}, bf16[1040,512]{1,0:T(8,128)(2,1)}, u32[]{:S(2)}, u32[]{:S(2)}) collective-permute-start(bf16[1040,512]{1,0:T(8,128)(2,1)} %get-tuple-element.67.rest_1_), channel_id=1, source_target_pairs={{0,1},{1,0},{2,3},{3,2},{4,5},{5,4},{6,7},{7,6},{8,9},{9,8},{10,11... | collective-permute-start | bytes 3194888 | tf_op jit(solution)/shard_map/ppermute | solution.py:31
  73.9 10.0 %collective-permute-start.20 = (bf16[144,256]{1,0:T(8,128)(2,1)S(1)}, bf16[144,256]{1,0:T(8,128)(2,1)S(1)}, u32[]{:S(2)}, u32[]{:S(2)}) collective-permute-start(bf16[144,256]{1,0:T(8,128)(2,1)S(1)} %get-tuple-element.63), channel_id=1, source_target_pairs={{0,0},{1,129},{2,2},{3,131},{4,4},{5,133},{6,6},{7,135},{8,8},{9,1... | collective-permute-start | bytes 221192 | tf_op jit(solution)/shard_map/ppermute | solution.py:31
  80.4 3.5 %collective-permute-start.21 = (bf16[144,256]{1,0:T(8,128)(2,1)S(1)}, bf16[144,256]{1,0:T(8,128)(2,1)S(1)}, u32[]{:S(2)}, u32[]{:S(2)}) collective-permute-start(bf16[144,256]{1,0:T(8,128)(2,1)S(1)} %get-tuple-element.64), channel_id=1, source_target_pairs={{0,32},{1,225},{2,34},{3,227},{4,36},{5,229},{6,38},{7,231},{8,40}... | collective-permute-start | bytes 221192 | tf_op jit(solution)/shard_map/ppermute | solution.py:31
  80.5 4.3 %collective-permute-start.22 = (bf16[144,256]{1,0:T(8,128)(2,1)S(1)}, bf16[144,256]{1,0:T(8,128)(2,1)S(1)}, u32[]{:S(2)}, u32[]{:S(2)}) collective-permute-start(bf16[144,256]{1,0:T(8,128)(2,1)S(1)} %get-tuple-element.65), channel_id=1, source_target_pairs={{0,64},{1,193},{2,66},{3,195},{4,68},{5,197},{6,70},{7,199},{8,72}... | collective-permute-start | bytes 221192 | tf_op jit(solution)/shard_map/ppermute | solution.py:31
  80.6 6.7 %collective-permute-start.23 = (bf16[144,256]{1,0:T(8,128)(2,1)S(1)}, bf16[144,256]{1,0:T(8,128)(2,1)S(1)}, u32[]{:S(2)}, u32[]{:S(2)}) collective-permute-start(bf16[144,256]{1,0:T(8,128)(2,1)S(1)} %get-tuple-element.66), channel_id=1, source_target_pairs={{0,96},{1,161},{2,98},{3,163},{4,100},{5,165},{6,102},{7,167},{8,1... | collective-permute-start | bytes 221192 | tf_op jit(solution)/shard_map/ppermute | solution.py:31
  87.3 13.6 %collective-permute-start.28 = (bf16[512,512]{1,0:T(8,128)(2,1)S(1)}, bf16[512,512]{1,0:T(8,128)(2,1)S(1)}, u32[]{:S(2)}, u32[]{:S(2)}) collective-permute-start(bf16[512,512]{1,0:T(8,128)(2,1)S(1)} %get-tuple-element.71), channel_id=1, source_target_pairs={{0,32},{1,225},{2,34},{3,227},{4,36},{5,229},{6,38},{7,231},{8,40}... | collective-permute-start | bytes 1572872 | tf_op jit(solution)/shard_map/ppermute | solution.py:31
  88.9 1.4 %collective-permute-start.25 = (f32[136,256]{1,0:T(8,128)S(1)}, f32[136,256]{1,0:T(8,128)S(1)}, u32[]{:S(2)}, u32[]{:S(2)}) collective-permute-start(f32[136,256]{1,0:T(8,128)S(1)} %get-tuple-element.68.own), channel_id=1, source_target_pairs={{0,1},{1,0},{2,3},{3,2},{4,5},{5,4},{6,7},{7,6},{8,9},{9,8},{10,11... | collective-permute-start | bytes 417800 | tf_op jit(solution)/shard_map/ppermute | solution.py:31
  90.9 10.1 %collective-permute-start.26 = (f32[136,256]{1,0:T(8,128)S(1)}, f32[136,256]{1,0:T(8,128)S(1)}, u32[]{:S(2)}, u32[]{:S(2)}) collective-permute-start(f32[136,256]{1,0:T(8,128)S(1)} %get-tuple-element.69.total.own), channel_id=1, source_target_pairs={{0,2},{1,7},{2,4},{3,1},{4,6},{5,3},{6,0},{7,5},{8,10},{9,15},{10,... | collective-permute-start | bytes 417800 | tf_op jit(solution)/shard_map/ppermute | solution.py:31
  95.3 5.6 %collective-permute-start.27 = (f32[64,256]{1,0:T(8,128)S(1)}, f32[64,256]{1,0:T(8,128)S(1)}, u32[]{:S(2)}, u32[]{:S(2)}) collective-permute-start(f32[64,256]{1,0:T(8,128)S(1)} %get-tuple-element.70), channel_id=1, source_target_pairs={{0,4},{1,5},{2,6},{3,7},{4,0},{5,1},{6,2},{7,3},{8,12},{9,13},{10,... | collective-permute-start | bytes 196616 | tf_op jit(solution)/shard_map/ppermute | solution.py:31
  100.9 2.6 %collective-permute-start.31 = (bf16[512,512]{1,0:T(8,128)(2,1)S(1)}, bf16[512,512]{1,0:T(8,128)(2,1)S(1)}, u32[]{:S(2)}, u32[]{:S(2)}) collective-permute-start(bf16[512,512]{1,0:T(8,128)(2,1)S(1)} %get-tuple-element.76.last), channel_id=1, source_target_pairs={{0,1},{1,0},{2,3},{3,2},{4,5},{5,4},{6,7},{7,6},{8,9},{9,8},{10,11... | collective-permute-start | bytes 1572872 | tf_op jit(solution)/shard_map/ppermute | solution.py:31
  101.7 1.8 %collective-permute-start.29 = (f32[136,256]{1,0:T(8,128)S(1)}, f32[136,256]{1,0:T(8,128)S(1)}, u32[]{:S(2)}, u32[]{:S(2)}) collective-permute-start(f32[136,256]{1,0:T(8,128)S(1)} %get-tuple-element.74.near), channel_id=1, source_target_pairs={{0,1},{1,0},{2,3},{3,2},{4,5},{5,4},{6,7},{7,6},{8,9},{9,8},{10,11... | collective-permute-start | bytes 417800 | tf_op jit(solution)/shard_map/ppermute | solution.py:31
  101.8 1.7 %collective-permute-start.30 = (f32[64,256]{1,0:T(8,128)S(1)}, f32[64,256]{1,0:T(8,128)S(1)}, u32[]{:S(2)}, u32[]{:S(2)}) collective-permute-start(f32[64,256]{1,0:T(8,128)S(1)} %get-tuple-element.75.far), channel_id=1, source_target_pairs={{0,1},{1,0},{2,3},{3,2},{4,5},{5,4},{6,7},{7,6},{8,9},{9,8},{10,11... | collective-permute-start | bytes 196616 | tf_op jit(solution)/shard_map/ppermute | solution.py:31
